TPU v7x, 256 devices: a whole 4x4x8 slice. The times are simulated.
256 devices in a mesh: sp: 16 (over z, y_lo), fsdp: 16 (over y_hi, x, core).
Axes of the slice: x: 4, y: 4 (y_hi: 2, y_lo: 2; y = y_hi * 2 + y_lo), z: 8, core: 2. Of those that a mesh axis runs over, the one named last changes fastest.
Arguments:
- query_states: bfloat16 [16, 2048, 4096], P('fsdp', 'sp'), may hold values from -6 to 6
- key_states: bfloat16 [16, 2048, 512], P('fsdp', 'sp'), may hold values from -6 to 6
- forward_value_states: bfloat16 [16, 2048, 512], P('fsdp', 'sp'), may hold values from -6 to 6
- grad_output: bfloat16 [16, 2048, 4096], P('fsdp', 'sp'), may hold values from -6 to 6
- layer_input: bfloat16 [16, 2048, 5120], P('fsdp', 'sp'), may hold values from -6 to 6
- segment_ids: int32 [16, 2048], P('fsdp'), may hold values from 0 to 3, never falling along the last dimension, each value on 1 to 1024 neighbouring positions
Outputs:
- grad_query: bfloat16 [16, 2048, 4096], P('fsdp', 'sp')
- grad_key: bfloat16 [16, 2048, 512], P('fsdp', 'sp')
- grad_value_weight: float32 [5120, 512], P(('sp', 'fsdp'))
Inputs may be any that keep to these rules, and one draw needn't show every extreme that they name: `segment_ids`: in each sequence the rollout numbers never fall; every rollout has 1 to 1024 positions and one has exactly 1024.
All inputs are finite; a program needn't handle non-finite values.
Results may differ from a plain program's by a relative error of at most 0.012.
Values may be sent and summed in bfloat16 or wider, within the bound.
No kernel may reach another device: no remote copies, remote signals or barrier semaphores. Data moves between devices by JAX's collectives and lax.ppermute only.
A program may use at most 128 MiB of HBM per device.

v0:
```python
import math

import jax
import jax.numpy as jnp
from jax import lax
from jax.sharding import PartitionSpec as P

KEY_VALUE_HEADS = 4
HEAD_SIZE = 128


def attention_blocks(query_heads, grad_heads, key_head, value_head, segment_row):
    token_length = query_heads.shape[0]
    local_heads = query_heads.shape[1] // HEAD_SIZE
    block = min(512, token_length)
    softmax_scale = 1.0 / math.sqrt(HEAD_SIZE)
    query_split = query_heads.reshape(token_length, local_heads, HEAD_SIZE)
    grad_split = grad_heads.reshape(token_length, local_heads, HEAD_SIZE)
    columns = jnp.arange(token_length, dtype=jnp.int32)

    def block_step(carry, start):
        key_total, value_total = carry
        query_block = lax.dynamic_slice_in_dim(query_split, start, block, 0)
        grad_block = lax.dynamic_slice_in_dim(grad_split, start, block, 0)
        segment_block = lax.dynamic_slice_in_dim(segment_row, start, block, 0)
        rows_here = start + jnp.arange(block, dtype=jnp.int32)
        allowed = (segment_block[:, None] == segment_row[None, :]) & (
            columns[None, :] <= rows_here[:, None]
        )
        scores = (
            jnp.einsum("qhd,kd->hqk", query_block, key_head, preferred_element_type=jnp.float32)
            * softmax_scale
        )
        scores = jnp.where(allowed[None], scores, -jnp.inf)
        largest = jnp.max(scores, axis=2, keepdims=True)
        weights = jnp.exp(scores - largest)
        weights = weights / jnp.sum(weights, axis=2, keepdims=True)
        weights_low = weights.astype(jnp.bfloat16)
        attended = jnp.einsum(
            "hqk,kd->qhd", weights_low, value_head, preferred_element_type=jnp.float32
        )
        row_terms = jnp.sum(grad_block.astype(jnp.float32) * attended, axis=2)
        grad_weights = jnp.einsum(
            "qhd,kd->hqk", grad_block, value_head, preferred_element_type=jnp.float32
        )
        grad_scores = (weights * (grad_weights - jnp.transpose(row_terms)[:, :, None])).astype(
            jnp.bfloat16
        )
        grad_query = (
            jnp.einsum("hqk,kd->qhd", grad_scores, key_head, preferred_element_type=jnp.float32)
            * softmax_scale
        ).astype(jnp.bfloat16)
        key_total = (
            key_total
            + jnp.einsum(
                "hqk,qhd->kd", grad_scores, query_block, preferred_element_type=jnp.float32
            )
            * softmax_scale
        )
        value_total = value_total + jnp.einsum(
            "hqk,qhd->kd", weights_low, grad_block, preferred_element_type=jnp.float32
        )
        return ((key_total, value_total), grad_query)

    empty = jnp.zeros((token_length, HEAD_SIZE), jnp.float32)
    starts = jnp.arange(token_length // block, dtype=jnp.int32) * block
    totals, grad_blocks = lax.scan(block_step, (empty, empty), starts)
    return (grad_blocks.reshape(token_length, local_heads * HEAD_SIZE), totals[0], totals[1])


def body(query_states, key_states, forward_value_states, grad_output, layer_input, segment_ids):
    query_local = query_states[0]
    key_shard = key_states[0]
    value_shard = forward_value_states[0]
    grad_local = grad_output[0]
    input_local = layer_input[0]
    segment_row = segment_ids[0]
    local_tokens = query_local.shape[0]
    sequence_parallel_width = lax.axis_size("sp")
    fsdp_size = lax.axis_size("fsdp")
    query_heads, grad_heads = (
        lax.all_to_all(query_local, "sp", split_axis=1, concat_axis=0, tiled=True),
        lax.all_to_all(grad_local, "sp", split_axis=1, concat_axis=0, tiled=True),
    )
    head_copies = sequence_parallel_width // KEY_VALUE_HEADS
    key_replicas = jnp.repeat(
        key_shard.reshape(local_tokens, KEY_VALUE_HEADS, HEAD_SIZE), head_copies, axis=1
    ).reshape(local_tokens, sequence_parallel_width * HEAD_SIZE)
    value_replicas = jnp.repeat(
        value_shard.reshape(local_tokens, KEY_VALUE_HEADS, HEAD_SIZE), head_copies, axis=1
    ).reshape(local_tokens, sequence_parallel_width * HEAD_SIZE)
    key_head, value_head = (
        lax.all_to_all(key_replicas, "sp", split_axis=1, concat_axis=0, tiled=True),
        lax.all_to_all(value_replicas, "sp", split_axis=1, concat_axis=0, tiled=True),
    )
    grad_query_heads, key_total, value_total = attention_blocks(
        query_heads, grad_heads, key_head, value_head, segment_row
    )
    key_gradient, value_gradient = (
        lax.all_to_all(
            key_total.astype(jnp.bfloat16), "sp", split_axis=0, concat_axis=1, tiled=True
        ).astype(key_total.dtype),
        lax.all_to_all(
            value_total.astype(jnp.bfloat16), "sp", split_axis=0, concat_axis=1, tiled=True
        ).astype(value_total.dtype),
    )
    grad_key_sum = (
        key_gradient.reshape(local_tokens, KEY_VALUE_HEADS, head_copies, HEAD_SIZE)
        .sum(axis=2)
        .reshape(local_tokens, KEY_VALUE_HEADS * HEAD_SIZE)
    )
    grad_value_sum = (
        value_gradient.reshape(local_tokens, KEY_VALUE_HEADS, head_copies, HEAD_SIZE)
        .sum(axis=2)
        .reshape(local_tokens, KEY_VALUE_HEADS * HEAD_SIZE)
    )
    grad_query_local = lax.all_to_all(
        grad_query_heads, "sp", split_axis=0, concat_axis=1, tiled=True
    )
    value_reduced_precision = grad_value_sum.astype(jnp.bfloat16)
    norm_factor = 1.0 / math.sqrt(local_tokens * sequence_parallel_width * fsdp_size)
    weight_part = lax.psum_scatter(
        jnp.einsum(
            "td,tc->dc", input_local, value_reduced_precision, preferred_element_type=jnp.float32
        ),
        ("sp", "fsdp"),
        scatter_dimension=0,
        tiled=True,
    )
    return (
        grad_query_local[None],
        grad_key_sum.astype(jnp.bfloat16)[None],
        weight_part * norm_factor,
    )


def solution(mesh):
    return jax.shard_map(
        body,
        mesh=mesh,
        in_specs=(
            P("fsdp", "sp", None),
            P("fsdp", "sp", None),
            P("fsdp", "sp", None),
            P("fsdp", "sp", None),
            P("fsdp", "sp", None),
            P("fsdp", None),
        ),
        out_specs=(P("fsdp", "sp", None), P("fsdp", "sp", None), P(("sp", "fsdp"), None)),
        check_vma=False,
    )
```

profile of v0, /device:TPU:32, one launch (start us, length us, event | category | flops | bytes accessed | tf_op | source)
XLA Modules:
  0.0 575.2 jit_solution(16044306539854955816)
XLA Ops:
  7.2 1.1 copy.83
  9.2 9.6 %all-to-all-start.3 = ((bf16[128,16,128]{0,2,1:T(8,128)(2,1)}), bf16[128,16,128]{0,2,1:T(8,128)(2,1)S(1)}, u32[]{:S(2)}, u32[]{:S(2)}) async-start(bf16[128,16,128]{0,2,1:T(8,128)(2,1)} %bitcast.9), calls=%async_computation.3 | async-start | bytes 1048576 | tf_op jit(solution)/shard_map/all_to_all | solution.py:94
  18.8 2.3 copy.62
  21.1 12.7 %all-to-all-done.3 = bf16[128,16,128]{0,2,1:T(8,128)(2,1)S(1)} async-done(((bf16[128,16,128]{0,2,1:T(8,128)(2,1)}), bf16[128,16,128]{0,2,1:T(8,128)(2,1)S(1)}, u32[]{:S(2)}, u32[]{:S(2)}) %all-to-all-start.3) | async-done | bytes 524320 | tf_op jit(solution)/shard_map/all_to_all | solution.py:94
  33.9 5.7 all-to-all-start
  39.5 2.3 copy.65
  41.8 22.8 %all-to-all-done = bf16[128,16,256]{0,2,1:T(8,128)(2,1)S(1)} async-done(((bf16[128,16,256]{0,2,1:T(8,128)(2,1)}), bf16[128,16,256]{0,2,1:T(8,128)(2,1)S(1)}, u32[]{:S(2)}, u32[]{:S(2)}) %all-to-all-start) | async-done | bytes 1048608 | tf_op jit(solution)/shard_map/all_to_all | solution.py:82
  64.6 6.6 %all-to-all-start.2 = ((bf16[128,16,256]{0,2,1:T(8,128)(2,1)}), bf16[128,16,256]{0,2,1:T(8,128)(2,1)S(1)}, u32[]{:S(2)}, u32[]{:S(2)}) async-start(bf16[128,16,256]{0,2,1:T(8,128)(2,1)} %bitcast.150), calls=%async_computation.2 | async-start | bytes 2097152 | tf_op jit(solution)/shard_map/all_to_all | solution.py:83
  72.8 23.5 %all-to-all-done.2 = bf16[128,16,256]{0,2,1:T(8,128)(2,1)S(1)} async-done(((bf16[128,16,256]{0,2,1:T(8,128)(2,1)}), bf16[128,16,256]{0,2,1:T(8,128)(2,1)S(1)}, u32[]{:S(2)}, u32[]{:S(2)}) %all-to-all-start.2) | async-done | bytes 1048608 | tf_op jit(solution)/shard_map/all_to_all | solution.py:83
  97.3 7.1 %all-to-all-start.1 = ((bf16[128,16,128]{2,0,1:T(8,128)(2,1)}), bf16[128,16,128]{2,0,1:T(8,128)(2,1)}, u32[]{:S(2)}, u32[]{:S(2)}) async-start(bf16[128,16,128]{2,0,1:T(8,128)(2,1)} %bitcast.153), calls=%async_computation.1 | async-start | bytes 1048576 | tf_op jit(solution)/shard_map/all_to_all | solution.py:93
  104.4 2.1 copy.68
  106.5 2.0 copy.71
  108.6 1.7 copy.63
  110.3 2.3 reshape.126
  112.6 1.9 copy.66
  114.5 1.3 reshape.127
  115.8 3.8 all-to-all-done.1
  119.6 122.3 %while.15 = (s32[]{:T(128)}, f32[2048,128]{1,0:T(8,128)}, f32[2048,128]{1,0:T(8,128)S(1)}, bf16[4,512,2,128]{3,2,1,0:T(2,128)(2,1)}, s32[4]{0:T(128)S(1)}, /*ind...) while((s32[]{:T(128)}, f32[2048,128]{1,0:T(8,128)}, ...), condition=%wide.region_4.5_spmd.clone, body=%wide.region_0.4_spmd.clone.sunk | while | flops 3247310336 | bytes 97556840 | solution.py:67
  122.9 1.1 constant_dynamic-slice_fusion.2
  124.2 2.2 fusion.94
  126.4 8.1 %fusion.95 = (f32[2,512]{1,0:T(2,128)S(1)}, f32[2,512,2048]{2,1,0:T(8,128)}) fusion(pred[512,2048]{1,0:T(8,128)(4,1)} %fusion.94, bf16[2048,128]{1,0:T(8,128)(2,1)} %get-tuple-element.298, bf16[2048,2,128]{0,2,1:T(8,128)(2,1)} %get-tuple-element.297, s32[]{:T(128)S(6)} %select_n.30), kind=kOutput, calls=%fused_computation.52.clone.1 | convolution fusion | flops 545261568 | bytes 10227716 | tf_op jit(solution)/shard_map/while/body/eval_jaxpr/sub | solution.py:36
  134.5 4.8 fusion.96
  139.3 1.3 fusion.97
  140.6 1.5 fusion.100
  142.2 1.6 fusion.98
  143.9 2.4 fusion.101
  146.3 2.8 fusion.99
  153.4 1.1 constant_dynamic-slice_fusion.2
  154.7 2.2 fusion.94
  156.9 8.1 %fusion.95 = (f32[2,512]{1,0:T(2,128)S(1)}, f32[2,512,2048]{2,1,0:T(8,128)}) fusion(pred[512,2048]{1,0:T(8,128)(4,1)} %fusion.94, bf16[2048,128]{1,0:T(8,128)(2,1)} %get-tuple-element.298, bf16[2048,2,128]{0,2,1:T(8,128)(2,1)} %get-tuple-element.297, s32[]{:T(128)S(6)} %select_n.30), kind=kOutput, calls=%fused_computation.52.clone.1 | convolution fusion | flops 545261568 | bytes 10227716 | tf_op jit(solution)/shard_map/while/body/eval_jaxpr/sub | solution.py:36
  165.1 4.8 fusion.96
  169.9 1.3 fusion.97
  171.2 1.5 fusion.100
  172.8 1.6 fusion.98
  174.4 2.4 fusion.101
  176.8 2.8 fusion.99
  184.0 1.1 constant_dynamic-slice_fusion.2
  185.3 2.2 fusion.94
  187.5 8.1 %fusion.95 = (f32[2,512]{1,0:T(2,128)S(1)}, f32[2,512,2048]{2,1,0:T(8,128)}) fusion(pred[512,2048]{1,0:T(8,128)(4,1)} %fusion.94, bf16[2048,128]{1,0:T(8,128)(2,1)} %get-tuple-element.298, bf16[2048,2,128]{0,2,1:T(8,128)(2,1)} %get-tuple-element.297, s32[]{:T(128)S(6)} %select_n.30), kind=kOutput, calls=%fused_computation.52.clone.1 | convolution fusion | flops 545261568 | bytes 10227716 | tf_op jit(solution)/shard_map/while/body/eval_jaxpr/sub | solution.py:36
  195.7 4.8 fusion.96
  200.4 1.3 fusion.97
  201.8 1.5 fusion.100
  203.4 1.6 fusion.98
  205.0 2.4 fusion.101
  207.4 2.8 fusion.99
  215.9 2.2 fusion.94
  218.1 8.1 %fusion.95 = (f32[2,512]{1,0:T(2,128)S(1)}, f32[2,512,2048]{2,1,0:T(8,128)}) fusion(pred[512,2048]{1,0:T(8,128)(4,1)} %fusion.94, bf16[2048,128]{1,0:T(8,128)(2,1)} %get-tuple-element.298, bf16[2048,2,128]{0,2,1:T(8,128)(2,1)} %get-tuple-element.297, s32[]{:T(128)S(6)} %select_n.30), kind=kOutput, calls=%fused_computation.52.clone.1 | convolution fusion | flops 545261568 | bytes 10227716 | tf_op jit(solution)/shard_map/while/body/eval_jaxpr/sub | solution.py:36
  226.2 4.8 fusion.96
  231.0 1.3 fusion.97
  232.4 1.5 fusion.100
  233.9 1.6 fusion.98
  235.6 2.4 fusion.101
  238.0 2.8 fusion.99
  241.9 19.0 %all_to_all.118 = bf16[16,128,128]{2,1,0:T(8,128)(2,1)S(1)} all-to-all(bf16[16,128,128]{2,1,0:T(8,128)(2,1)S(1)} %bitcast.152), channel_id=1, replica_groups=mesh['sp'=16,'fsdp'=16] {'sp'}, dimensions={0} | all-to-all | bytes 1048576 | tf_op jit(solution)/shard_map/all_to_all | solution.py:103
  261.1 5.3 convolution_bitcast_fusion.3
  266.5 1.2 copy-done.3
  268.6 5.2 all-to-all-start.5
  273.8 2.5 all_to_all.102
  276.3 12.5 %all-to-all-done.5 = bf16[16,128,128]{2,1,0:T(8,128)(2,1)S(1)} async-done(((bf16[16,128,128]{2,1,0:T(8,128)(2,1)}), bf16[16,128,128]{2,1,0:T(8,128)(2,1)S(1)}, u32[]{:S(2)}, u32[]{:S(2)}) %all-to-all-start.5) | async-done | bytes 524320 | tf_op jit(solution)/shard_map/all_to_all | solution.py:100
  288.8 6.8 %all-to-all-start.4 = ((bf16[16,128,256]{2,1,0:T(8,128)(2,1)}), bf16[16,128,256]{2,1,0:T(8,128)(2,1)S(1)}, u32[]{:S(2)}, u32[]{:S(2)}) async-start(bf16[16,128,256]{2,1,0:T(8,128)(2,1)} %all_to_all.102), calls=%async_computation.4 | async-start | bytes 2097152 | tf_op jit(solution)/shard_map/all_to_all | solution.py:117
  296.6 25.5 %all-to-all-done.4 = bf16[16,128,256]{2,1,0:T(8,128)(2,1)S(1)} async-done(((bf16[16,128,256]{2,1,0:T(8,128)(2,1)}), bf16[16,128,256]{2,1,0:T(8,128)(2,1)S(1)}, u32[]{:S(2)}, u32[]{:S(2)}) %all-to-all-start.4) | async-done | bytes 1048608 | tf_op jit(solution)/shard_map/all_to_all | solution.py:117
  322.8 1.3 copy.76
  324.1 242.4 %all-reduce.3.cloned.1.call-done = f32[5120,512]{0,1:T(8,128)} async-done(((f32[5120,512]{0,1:T(8,128)}), f32[5120,512]{0,1:T(8,128)}) %all-reduce.3.cloned.1.call-update) | async-done | bytes 10485776
  566.5 1.2 dynamic-slice_multiply_fusion
  (95 shorter events, 18.4 us)
Async XLA Ops:
  7.2 253.9 %copy-start = (bf16[1,128,5120]{2,1,0:T(8,128)(2,1)S(1)}, bf16[1,128,5120]{2,1,0:T(8,128)(2,1)}, u32[]{:S(2)}) copy-start(bf16[1,128,5120]{2,1,0:T(8,128)(2,1)} %param.12) | copy-start | bytes 3932164
  9.2 24.6 %all-to-all-start.3 = ((bf16[128,16,128]{0,2,1:T(8,128)(2,1)}), bf16[128,16,128]{0,2,1:T(8,128)(2,1)S(1)}, u32[]{:S(2)}, u32[]{:S(2)}) async-start(bf16[128,16,128]{0,2,1:T(8,128)(2,1)} %bitcast.9), calls=%async_computation.3 | async-start | bytes 1048576 | tf_op jit(solution)/shard_map/all_to_all | solution.py:94
  18.8 52.3 %copy-start.8 = (bf16[1,128,512]{2,1,0:T(8,128)(2,1)S(1)}, bf16[1,128,512]{2,1,0:T(8,128)(2,1)}, u32[]{:S(2)}) copy-start(bf16[1,128,512]{2,1,0:T(8,128)(2,1)} %param.9) | copy-start | bytes 393220
  33.9 30.7 %copy-start.5 = (bf16[128,16,128]{0,2,1:T(8,128)(2,1)}, bf16[128,16,128]{0,2,1:T(8,128)(2,1)S(1)}, u32[]{:S(2)}) copy-start(bf16[128,16,128]{0,2,1:T(8,128)(2,1)S(1)} %all-to-all-done.3) | copy-start | bytes 1572868
  33.9 30.7 %all-to-all-start = ((bf16[128,16,256]{0,2,1:T(8,128)(2,1)}), bf16[128,16,256]{0,2,1:T(8,128)(2,1)S(1)}, u32[]{:S(2)}, u32[]{:S(2)}) async-start(bf16[128,16,256]{0,2,1:T(8,128)(2,1)} %bitcast.1), calls=%async_computation | async-start | bytes 2097152 | tf_op jit(solution)/shard_map/all_to_all | solution.py:82
  64.6 31.7 %all-to-all-start.2 = ((bf16[128,16,256]{0,2,1:T(8,128)(2,1)}), bf16[128,16,256]{0,2,1:T(8,128)(2,1)S(1)}, u32[]{:S(2)}, u32[]{:S(2)}) async-start(bf16[128,16,256]{0,2,1:T(8,128)(2,1)} %bitcast.150), calls=%async_computation.2 | async-start | bytes 2097152 | tf_op jit(solution)/shard_map/all_to_all | solution.py:83
  96.3 8.1 %copy-start.4 = (bf16[128,16,256]{0,2,1:T(8,128)(2,1)}, bf16[128,16,256]{0,2,1:T(8,128)(2,1)S(1)}, u32[]{:S(2)}) copy-start(bf16[128,16,256]{0,2,1:T(8,128)(2,1)S(1)} %all-to-all-done.2) | copy-start | bytes 3145732
  97.3 22.3 %all-to-all-start.1 = ((bf16[128,16,128]{2,0,1:T(8,128)(2,1)}), bf16[128,16,128]{2,0,1:T(8,128)(2,1)}, u32[]{:S(2)}, u32[]{:S(2)}) async-start(bf16[128,16,128]{2,0,1:T(8,128)(2,1)} %bitcast.153), calls=%async_computation.1 | async-start | bytes 1048576 | tf_op jit(solution)/shard_map/all_to_all | solution.py:93
  104.4 462.1 %all-reduce.3.cloned.1.call-start = ((), (), s32[]{:S(2)}) async-start(), calls=%async_computation.7 | async-start | bytes 20971520
  108.6 11.0 %copy-start.7 = (s32[1,2048]{1,0:T(1,128)S(1)}, s32[1,2048]{1,0:T(1,128)}, u32[]{:S(2)}) copy-start(s32[1,2048]{1,0:T(1,128)} %param.13) | copy-start | bytes 24580
  134.5 4.8 copy-start.6
  134.5 7.7 %slice-start = ((s8[8388608]{0:T(1024)(128)(4,1)}), s8[4194304]{0:T(1024)(128)(4,1)S(1)}, s32[]{:S(2)}) async-start(s8[8388608]{0:T(1024)(128)(4,1)} %bitcast.145), calls=%async_computation.8 | async-start | bytes 8388608 | tf_op jit(solution)/shard_map/while
  139.3 2.9 slice-start.1
  143.9 2.4 copy-start.1
  149.1 1.0 copy-start.2
  165.1 4.8 copy-start.6
  165.1 7.7 %slice-start = ((s8[8388608]{0:T(1024)(128)(4,1)}), s8[4194304]{0:T(1024)(128)(4,1)S(1)}, s32[]{:S(2)}) async-start(s8[8388608]{0:T(1024)(128)(4,1)} %bitcast.145), calls=%async_computation.8 | async-start | bytes 8388608 | tf_op jit(solution)/shard_map/while
  169.9 2.9 slice-start.1
  174.4 2.4 copy-start.1
  179.7 1.1 copy-start.2
  195.6 4.8 copy-start.6
  195.6 7.7 %slice-start = ((s8[8388608]{0:T(1024)(128)(4,1)}), s8[4194304]{0:T(1024)(128)(4,1)S(1)}, s32[]{:S(2)}) async-start(s8[8388608]{0:T(1024)(128)(4,1)} %bitcast.145), calls=%async_computation.8 | async-start | bytes 8388608 | tf_op jit(solution)/shard_map/while
  200.4 2.9 slice-start.1
  205.0 2.4 copy-start.1
  210.3 1.1 copy-start.2
  226.2 4.8 copy-start.6
  226.2 7.7 %slice-start = ((s8[8388608]{0:T(1024)(128)(4,1)}), s8[4194304]{0:T(1024)(128)(4,1)S(1)}, s32[]{:S(2)}) async-start(s8[8388608]{0:T(1024)(128)(4,1)} %bitcast.145), calls=%async_computation.8 | async-start | bytes 8388608 | tf_op jit(solution)/shard_map/while
  231.0 2.9 slice-start.1
  235.6 2.4 copy-start.1
  240.8 1.0 copy-start.2
  266.4 1.2 copy-start.3
  268.6 20.2 %all-to-all-start.5 = ((bf16[16,128,128]{2,1,0:T(8,128)(2,1)}), bf16[16,128,128]{2,1,0:T(8,128)(2,1)S(1)}, u32[]{:S(2)}, u32[]{:S(2)}) async-start(bf16[16,128,128]{2,1,0:T(8,128)(2,1)} %bitcast.14), calls=%async_computation.5 | async-start | bytes 1048576 | tf_op jit(solution)/shard_map/all_to_all | solution.py:100
  288.8 33.3 %all-to-all-start.4 = ((bf16[16,128,256]{2,1,0:T(8,128)(2,1)}), bf16[16,128,256]{2,1,0:T(8,128)(2,1)S(1)}, u32[]{:S(2)}, u32[]{:S(2)}) async-start(bf16[16,128,256]{2,1,0:T(8,128)(2,1)} %all_to_all.102), calls=%async_computation.4 | async-start | bytes 2097152 | tf_op jit(solution)/shard_map/all_to_all | solution.py:117
Sparse Core Ops, SparseCore 0:
  266.6 299.8 all-reduce.2
where the time goes:
time: 579 us; the launch traced here: 575 us
  waiting for transfers between devices  343 us (59%)
  matrix products  76.9 us (13%)
  starting transfers between devices  40.9 us (7%)
  local copies, waits for them, and re-layouts  40.1 us (7%)
  other arithmetic  32.7 us (6%)
  blocking collectives  19 us (3%)
  between operations  14.2 us (2%)
  loops' own time  8.27 us (1%)
    unnamed x2, waiting for transfers between devices  242 us
    sub x4, matrix products, block_step(): weights = jnp.exp(scores - largest)  32.6 us
    all_to_all x1, waiting for transfers between devices, body(): lax.all_to_all(grad_query_heads, 'sp', split_axis=0, concat_axis=1, tiled...  25.5 us
    all_to_all x1, waiting for transfers between devices, body(): lax.all_to_all(grad_local, 'sp', split_axis=1, concat_axis=0, tiled=True)  23.5 us
    all_to_all x1, waiting for transfers between devices, body(): lax.all_to_all(query_local, 'sp', split_axis=1, concat_axis=0, tiled=True)  22.8 us
    convert_element_type x4, other arithmetic, block_step(): weights_low = weights.astype(jnp.bfloat16)  19.1 us
    all_to_all x1, blocking collectives, body(): lax.all_to_all(value_total.astype(jnp.bfloat16), 'sp', split_axis=0, conc...  19 us
    all_to_all x1, waiting for transfers between devices, body(): lax.all_to_all(value_replicas, 'sp', split_axis=1, concat_axis=0, tiled=T...  12.7 us
  transfers between devices with their start and end apart: 7, of which 7 were waited for; matrix products, arithmetic and copies ran while one was open for 4% of the time, Pallas kernels for 0%

commit v1 on v0

v1 whole, which is shorter than its diff:
```python
import functools
import math

import jax
import jax.numpy as jnp
from jax import lax
from jax.experimental import pallas as pl
from jax.experimental.pallas import tpu as pltpu
from jax.sharding import Mesh
from jax.sharding import PartitionSpec as P

HEAD = 128
SCALE = 1.0 / math.sqrt(HEAD)
LOG2E = math.log2(math.e)
BF = jnp.bfloat16
F32 = jnp.float32
BACK = 4
TOK = 128
BLK = 256
WIN = (BACK + 1) * BLK
VMEM = 56 * 1024 * 1024
NT = (((1,), (1,)), ((), ()))


def heads_of(own_ref, recv_ref, count):
    rows = []
    for h in range(count):
        cols = slice(h * HEAD, (h + 1) * HEAD)
        rows += [own_ref[:, cols], recv_ref[:, cols]]
    return jnp.concatenate(rows, axis=0)


def probs_kernel(s_ref, qo, qr, go, gr, k0, k1, k2, k3, k4, bias, probs, d0, d1, d2, d3, d4, acc):
    step = pl.program_id(1)
    keys = jnp.concatenate([k[...] for k in (k0, k1, k2, k3, k4)], axis=0)
    queries = heads_of(qo, qr, 2)
    scores = lax.dot_general(keys, queries, NT, preferred_element_type=F32)
    for h in range(2):
        t = scores[:, h * BLK : (h + 1) * BLK] * (SCALE * LOG2E) + bias[...]
        e = jnp.exp2(t - jnp.max(t, axis=0, keepdims=True))
        p = e * (1.0 / jnp.sum(e, axis=0, keepdims=True))
        probs[0, 0, :, h * BLK : (h + 1) * BLK] = p.astype(BF)
    part = jnp.dot(probs[0, 0], heads_of(go, gr, 2), preferred_element_type=F32)

    @pl.when(step == 0)
    def _():
        acc[...] = part

    @pl.when(step > 0)
    def _():
        acc[...] += part

    @pl.when(step == pl.num_programs(1) - 1)
    def _():
        for i, out in enumerate((d0, d1, d2, d3, d4)):
            out[...] = acc[i * BLK : (i + 1) * BLK, :].astype(out.dtype)


def grads_kernel(
    s_ref, qo, qr, go, gr, k0, k1, k2, k3, k4, v0, v1, v2, v3, v4, probs,
    dqo, dqr, d0, d1, d2, d3, d4, acc, key_t,
):
    step = pl.program_id(1)

    @pl.when(step == 0)
    def _():
        for i, k in enumerate((k0, k1, k2, k3, k4)):
            key_t[:, i * BLK : (i + 1) * BLK] = k[...].T

    values = jnp.concatenate([v[...] for v in (v0, v1, v2, v3, v4)], axis=0)
    grad_probs = lax.dot_general(values, heads_of(go, gr, 2), NT, preferred_element_type=F32)
    p = probs[0, 0].astype(F32)
    row_terms = jnp.sum(p * grad_probs, axis=0, keepdims=True)
    ds = (p * (grad_probs - row_terms)).astype(BF)
    part = jnp.dot(ds, heads_of(qo, qr, 2), preferred_element_type=F32)
    dq = (jnp.dot(key_t[...], ds, preferred_element_type=F32) * SCALE).T.astype(BF)
    for h in range(2):
        cols = slice(h * HEAD, (h + 1) * HEAD)
        dqo[:, cols] = dq[h * BLK : h * BLK + TOK]
        dqr[:, cols] = dq[h * BLK + TOK : (h + 1) * BLK]

    @pl.when(step == 0)
    def _():
        acc[...] = part

    @pl.when(step > 0)
    def _():
        acc[...] += part

    @pl.when(step == pl.num_programs(1) - 1)
    def _():
        for i, out in enumerate((d0, d1, d2, d3, d4)):
            out[...] = (acc[i * BLK : (i + 1) * BLK, :] * SCALE).astype(out.dtype)


def own_spec():
    return pl.BlockSpec((TOK, 2 * HEAD), lambda j, i, s: (0, s[0] * 8 + j * 4 + i))


def recv_spec():
    return pl.BlockSpec((TOK, 2 * HEAD), lambda j, i, s: (0, j * 4 + i))


def block_spec():
    return pl.BlockSpec((BLK, HEAD), lambda j, i, s: (0, j))


def probs_spec():
    return pl.BlockSpec((1, 1, WIN, 2 * BLK), lambda j, i, s: (j, i, 0, 0))


def window_outs():
    first = jax.ShapeDtypeStruct((BLK, 2 * HEAD), F32)
    return [first] + [jax.ShapeDtypeStruct((BLK, 2 * HEAD), BF)] * BACK


def run_probs(place, qo, qr, go, gr, keys, bias):
    flops = 2 * 2 * 16 * WIN * BLK * HEAD
    outs = pl.pallas_call(
        probs_kernel,
        grid_spec=pltpu.PrefetchScalarGridSpec(
            num_scalar_prefetch=1,
            grid=(2, 4),
            in_specs=[own_spec(), recv_spec(), own_spec(), recv_spec()]
            + [block_spec()] * (BACK + 1)
            + [pl.BlockSpec((WIN, BLK), lambda j, i, s: (0, 0))],
            out_specs=[probs_spec()] + [block_spec()] * (BACK + 1),
            scratch_shapes=[pltpu.VMEM((WIN, HEAD), F32)],
        ),
        out_shape=[jax.ShapeDtypeStruct((2, 4, WIN, 2 * BLK), BF)] + window_outs(),
        compiler_params=pltpu.CompilerParams(vmem_limit_bytes=VMEM),
        cost_estimate=pl.CostEstimate(
            flops=flops, bytes_accessed=16 << 20, transcendentals=16 * WIN * BLK
        ),
        name="probs",
    )(place, qo, qr, go, gr, *keys, bias)
    return outs[0], outs[1:]


def run_grads(place, qo, qr, go, gr, keys, values, probs):
    flops = 3 * 2 * 16 * WIN * BLK * HEAD
    outs = pl.pallas_call(
        grads_kernel,
        grid_spec=pltpu.PrefetchScalarGridSpec(
            num_scalar_prefetch=1,
            grid=(2, 4),
            in_specs=[own_spec(), recv_spec(), own_spec(), recv_spec()]
            + [block_spec()] * (2 * BACK + 2)
            + [probs_spec()],
            out_specs=[recv_spec(), recv_spec()] + [block_spec()] * (BACK + 1),
            scratch_shapes=[pltpu.VMEM((WIN, HEAD), F32), pltpu.VMEM((HEAD, WIN), BF)],
        ),
        out_shape=[jax.ShapeDtypeStruct((TOK, 16 * HEAD), BF)] * 2 + window_outs(),
        compiler_params=pltpu.CompilerParams(vmem_limit_bytes=VMEM),
        cost_estimate=pl.CostEstimate(flops=flops, bytes_accessed=16 << 20, transcendentals=0),
        name="grads",
    )(place, qo, qr, go, gr, *keys, *values, probs)
    return outs[0], outs[1], outs[2:]


def weight_kernel(s_ref, xo, xr, mine, theirs, out):
    x, c = s_ref[1], s_ref[2]
    total = jnp.zeros(out.shape, F32)
    for other, ref in ((0, mine), (1, theirs)):
        core = c if other == 0 else 1 - c
        for d in range(4):
            seq = lax.rem(x - d + 4, 4) * 2 + core
            total += jnp.dot(xo[seq], ref[d, :TOK], preferred_element_type=F32)
            total += jnp.dot(xr[seq], ref[d, TOK:], preferred_element_type=F32)
    out[...] = total.astype(out.dtype)


def run_weight(place, xo, xr, mine, theirs):
    whole = pl.BlockSpec(memory_space=pltpu.VMEM)
    return pl.pallas_call(
        weight_kernel,
        in_specs=[pl.BlockSpec(memory_space=pltpu.SMEM)] + [whole] * 4,
        out_specs=whole,
        out_shape=jax.ShapeDtypeStruct((xo.shape[1], 2 * HEAD), BF),
        compiler_params=pltpu.CompilerParams(vmem_limit_bytes=VMEM),
        cost_estimate=pl.CostEstimate(
            flops=2 * 2048 * 640 * 256, bytes_accessed=4 << 20, transcendentals=0
        ),
        name="weight",
    )(place, xo, xr, mine, theirs)


def body(sizes, query, key, value, grad, layer_input, segment_ids):
    nz = sizes["z"]
    z, yl, x, c = (lax.axis_index(a) for a in ("z", "yl", "x", "c"))
    place = jnp.stack([yl, x, c]).astype(jnp.int32)
    q, k, v, g, xin, seg = (a[0] for a in (query, key, value, grad, layer_input, segment_ids))
    swap = [(0, 1), (1, 0)]

    def half(a, which, width):
        return lax.dynamic_slice_in_dim(a, which * width, width, 1)

    def to_pair(a):
        return lax.ppermute(a, "yl", swap)

    keys = [jnp.concatenate([half(k, yl, 256), to_pair(half(k, 1 - yl, 256))], 0)]
    values = [jnp.concatenate([half(v, yl, 256), to_pair(half(v, 1 - yl, 256))], 0)]
    q_recv = to_pair(half(q, 1 - yl, 2048))
    g_recv = to_pair(half(g, 1 - yl, 2048))
    onward = [(i, i + 1) for i in range(nz - 1)]
    for _ in range(BACK):
        keys.append(lax.ppermute(keys[-1], "z", onward))
        values.append(lax.ppermute(values[-1], "z", onward))

    groups = 8
    x_t = xin.T
    width = x_t.shape[0] // groups
    x_own = lax.all_to_all(x_t, ("x", "c"), split_axis=0, concat_axis=0, tiled=True)
    x_own = x_own.reshape(groups, width, TOK)
    x_recv = to_pair(x_own)

    offset = jnp.arange(TOK, dtype=jnp.int32)
    within = jnp.concatenate([yl * TOK + offset, (1 - yl) * TOK + offset])
    key_pos = ((z - jnp.arange(BACK + 1, dtype=jnp.int32))[:, None] * BLK + within[None]).reshape(WIN)
    query_pos = z * BLK + within
    padded = jnp.concatenate([jnp.full((BACK * BLK,), -1, jnp.int32), seg])
    window = lax.dynamic_slice_in_dim(padded, z * BLK, WIN).reshape(BACK + 1, 2, TOK)[::-1]
    window = jnp.where(yl == 0, window, window[:, ::-1])
    query_seg = window[0].reshape(BLK)
    allowed = (window.reshape(WIN)[:, None] == query_seg[None]) & (
        key_pos[:, None] <= query_pos[None]
    )
    bias = jnp.where(allowed, 0.0, -jnp.inf).astype(F32)

    def home(parts):
        total = parts[0]
        for d in range(1, BACK + 1):
            back = [(i, i - d) for i in range(d, nz)]
            total = total + lax.ppermute(parts[d], "z", back).astype(F32)
        return total.astype(BF)

    probs, value_parts = run_probs(place, q, q_recv, g, g_recv, keys, bias)
    value_low = home(value_parts)
    dq_own, dq_far, key_parts = run_grads(place, q, q_recv, g, g_recv, keys, values, probs)

    near = [value_low]
    for d in range(1, 4):
        near.append(lax.ppermute(value_low, "x", [(i, (i + d) % 4) for i in range(4)]))
    near = jnp.stack(near)
    far = lax.ppermute(near, "c", swap)
    part = run_weight(place, x_own, x_recv, near, far)
    rows = width // 32
    part = lax.all_to_all(
        part.reshape(32, rows, 256), ("z", "yl", "yh"), split_axis=0, concat_axis=0, tiled=True
    )
    total = part.reshape(nz, 2, 2, rows, 256).astype(F32).sum(axis=(0, 2))
    total = jnp.concatenate([total[0], total[1]], axis=1)
    total = total * (1.0 / math.sqrt(16 * 2048))
    moves = []
    for i in range(256):
        zy, xi, ci = i // 8, (i % 8) // 2, i % 2
        moves.append((i, (xi * 2 + ci) * 32 + zy))
    weight = lax.ppermute(total, ("z", "yl", "yh", "x", "c"), moves)

    def join(mine, theirs):
        return jnp.where(
            yl == 0,
            jnp.concatenate([mine, theirs], 1),
            jnp.concatenate([theirs, mine], 1),
        )

    dq = join(dq_own, to_pair(dq_far))
    key_low = home(key_parts)
    dk = join(key_low[:TOK], to_pair(key_low[TOK:]))
    return dq[None], dk[None], weight


def solution(mesh):
    fine = Mesh(mesh.devices.reshape(8, 2, 2, 4, 2), ("z", "yl", "yh", "x", "c"))
    sizes = dict(fine.shape)
    tokens = P(("yh", "x", "c"), ("z", "yl"), None)
    return jax.shard_map(
        functools.partial(body, sizes),
        mesh=fine,
        in_specs=(tokens,) * 5 + (P(("yh", "x", "c"), None),),
        out_specs=(tokens, tokens, P(("z", "yl", "yh", "x", "c"), None)),
        check_vma=False,
    )
```

time: 579 us -> 199 us (0.34)
  the two profiles are of different devices: /device:TPU:32 before, /device:TPU:30 now
where the time goes in v1:
time: 199 us; the launch traced here: 198 us
  starting transfers between devices  87.4 us (44%)
  waiting for transfers between devices  52.8 us (27%)
  Pallas kernels  41.4 us (21%)
  local copies, waits for them, and re-layouts  9.77 us (5%)
  other arithmetic  5.59 us (3%)
    ppermute x4, starting transfers between devices, body(): values.append(lax.ppermute(values[-1], 'z', onward))  23.2 us
    pallas_call x1, Pallas kernels, run_probs(): pl.pallas_call(probs_kernel, grid_spec=pltpu.PrefetchScalarGridSpec(num_s...  20.2 us
    ppermute x7, waiting for transfers between devices, to_pair(): return lax.ppermute(a, 'yl', swap)  20.1 us
    all_to_all x1, starting transfers between devices, body(): lax.all_to_all(part.reshape(32, rows, 256), ('z', 'yl', 'yh'), split_axis...  18.6 us
    pallas_call x1, Pallas kernels, run_grads(): pl.pallas_call(grads_kernel, grid_spec=pltpu.PrefetchScalarGridSpec(num_s...  16.9 us
    ppermute x4, starting transfers between devices, body(): keys.append(lax.ppermute(keys[-1], 'z', onward))  16.9 us
    ppermute x8, starting transfers between devices, home(): total = total + lax.ppermute(parts[d], 'z', back).astype(F32)  10.5 us
    ppermute x1, waiting for transfers between devices, body(): weight = lax.ppermute(total, ('z', 'yl', 'yh', 'x', 'c'), moves)  10.2 us
  transfers between devices with their start and end apart: 30, of which 13 were waited for; matrix products, arithmetic and copies ran while one was open for 5% of the time, Pallas kernels for 21%

profile of v1, /device:TPU:30, one launch (start us, length us, event | category | flops | bytes accessed | tf_op | source)
XLA Modules:
  0.0 198.1 jit_solution(5288989880829635047)
XLA Ops:
  0.7 2.0 %dynamic-slice_bitcast_fusion.1 = bf16[128,2048]{1,0:T(8,128)(2,1)} fusion(bf16[1,128,4096]{2,1,0:T(8,128)(2,1)} %param.6, s32[]{:T(128)S(6)} %select_n.58), kind=kLoop, calls=%fused_computation.5 | loop fusion | bytes 1048580 | tf_op jit(solution)/shard_map/dynamic_slice | solution.py:196
  2.7 0.7 collective-permute-start
  3.5 0.8 dynamic-slice_bitcast_fusion
  4.3 1.3 collective-permute-start.1
  5.6 0.8 collective-permute-start.2
  6.5 1.4 collective-permute-start.7
  7.8 1.4 copy.10
  9.3 4.9 %all-to-all-start = ((bf16[8,640,128]{2,1,0:T(8,128)(2,1)}), bf16[8,640,128]{2,1,0:T(8,128)(2,1)S(1)}, u32[]{:S(2)}, u32[]{:S(2)}) async-start(bf16[8,640,128]{2,1,0:T(8,128)(2,1)} %bitcast.19), calls=%async_computation | async-start | bytes 2621440 | tf_op jit(solution)/shard_map/all_to_all | solution.py:213
  14.2 0.1 broadcast_add_fusion
  14.3 0.1 pad_dynamic-slice_fusion
  14.4 15.5 %collective-permute-done.2 = bf16[128,256]{1,0:T(8,128)(2,1)S(1)} collective-permute-done((bf16[128,256]{1,0:T(8,128)(2,1)S(1)}, bf16[128,256]{1,0:T(8,128)(2,1)S(1)}, u32[]{:S(2)}, u32[]{:S(2)}) %collective-permute-start.2) | collective-permute-done | bytes 65568 | tf_op jit(solution)/shard_map/ppermute | solution.py:199
  30.0 3.8 %collective-permute-start.3 = (bf16[256,256]{1,0:T(8,128)(2,1)S(1)}, bf16[256,256]{1,0:T(8,128)(2,1)S(1)}, u32[]{:S(2)}, u32[]{:S(2)}) collective-permute-start(bf16[256,256]{1,0:T(8,128)(2,1)S(1)} %pad_maximum_fusion.1.k0), channel_id=1, source_target_pairs={{0,32},{32,64},{64,96},{96,128},{128,160},{160,192},{192,224},{1,3... | collective-permute-start | bytes 393224 | tf_op jit(solution)/shard_map/ppermute | solution.py:207
  33.8 2.5 %collective-permute-done.3.k1 = bf16[256,256]{1,0:T(8,128)(2,1)S(1)} collective-permute-done((bf16[256,256]{1,0:T(8,128)(2,1)S(1)}, bf16[256,256]{1,0:T(8,128)(2,1)S(1)}, u32[]{:S(2)}, u32[]{:S(2)}) %collective-permute-start.3) | collective-permute-done | bytes 131104 | tf_op jit(solution)/shard_map/ppermute | solution.py:207
  36.3 4.3 %collective-permute-start.4 = (bf16[256,256]{1,0:T(8,128)(2,1)S(1)}, bf16[256,256]{1,0:T(8,128)(2,1)S(1)}, u32[]{:S(2)}, u32[]{:S(2)}) collective-permute-start(bf16[256,256]{1,0:T(8,128)(2,1)S(1)} %collective-permute-done.3.k1), channel_id=1, source_target_pairs={{0,32},{32,64},{64,96},{96,128},{128,160},{160,192},{192,224},{1,3... | collective-permute-start | bytes 393224 | tf_op jit(solution)/shard_map/ppermute | solution.py:207
  40.7 2.5 %collective-permute-done.4.k2 = bf16[256,256]{1,0:T(8,128)(2,1)S(1)} collective-permute-done((bf16[256,256]{1,0:T(8,128)(2,1)S(1)}, bf16[256,256]{1,0:T(8,128)(2,1)S(1)}, u32[]{:S(2)}, u32[]{:S(2)}) %collective-permute-start.4) | collective-permute-done | bytes 131104 | tf_op jit(solution)/shard_map/ppermute | solution.py:207
  43.1 4.3 %collective-permute-start.5 = (bf16[256,256]{1,0:T(8,128)(2,1)S(1)}, bf16[256,256]{1,0:T(8,128)(2,1)S(1)}, u32[]{:S(2)}, u32[]{:S(2)}) collective-permute-start(bf16[256,256]{1,0:T(8,128)(2,1)S(1)} %collective-permute-done.4.k2), channel_id=1, source_target_pairs={{0,32},{32,64},{64,96},{96,128},{128,160},{160,192},{192,224},{1,3... | collective-permute-start | bytes 393224 | tf_op jit(solution)/shard_map/ppermute | solution.py:207
  47.5 1.7 and_select_fusion.bias
  49.2 0.9 collective-permute-done.5.k3
  50.1 4.4 %collective-permute-start.6 = (bf16[256,256]{1,0:T(8,128)(2,1)S(1)}, bf16[256,256]{1,0:T(8,128)(2,1)S(1)}, u32[]{:S(2)}, u32[]{:S(2)}) collective-permute-start(bf16[256,256]{1,0:T(8,128)(2,1)S(1)} %collective-permute-done.5.k3), channel_id=1, source_target_pairs={{0,32},{32,64},{64,96},{96,128},{128,160},{160,192},{192,224},{1,3... | collective-permute-start | bytes 393224 | tf_op jit(solution)/shard_map/ppermute | solution.py:207
  54.5 0.6 pad_add_fusion.1.s_ref
  55.2 5.0 %collective-permute-start.8 = (bf16[256,256]{1,0:T(8,128)(2,1)S(1)}, bf16[256,256]{1,0:T(8,128)(2,1)S(1)}, u32[]{:S(2)}, u32[]{:S(2)}) collective-permute-start(bf16[256,256]{1,0:T(8,128)(2,1)S(1)} %pad_maximum_fusion.2.v0), channel_id=1, source_target_pairs={{0,32},{32,64},{64,96},{96,128},{128,160},{160,192},{192,224},{1,3... | collective-permute-start | bytes 393224 | tf_op jit(solution)/shard_map/ppermute | solution.py:208
  60.2 0.8 collective-permute-start.18
  61.1 0.7 copy-done.7
  61.8 0.2 copy-done.8
  62.1 20.2 %probs.1 = (bf16[2,4,1280,512]{3,2,1,0:T(8,128)(2,1)}, f32[256,256]{1,0:T(8,128)}, bf16[256,256]{1,0:T(8,128)(2,1)}, bf16[256,256]{1,0:T(8,128)(2,1)}, bf16[256,...) custom-call(s32[3]{0:T(128)} %pad_add_fusion.1.s_ref, bf16[128,4096]{1,0:T(8,128)(2,1)} %bitcast.41, ...), custom_call_target="tpu_custom_call" | custom-call | flops 2684354560 | bytes 16777216 | tf_op jit(solution)/shard_map/probs/pallas_call | solution.py:119
  82.4 1.3 collective-permute-start.22
  83.7 1.3 collective-permute-start.21
  85.0 1.3 collective-permute-start.20
  86.3 1.3 collective-permute-start.19
  87.6 7.2 %collective-permute-done.22 = bf16[256,256]{1,0:T(8,128)(2,1)S(1)} collective-permute-done((bf16[256,256]{1,0:T(8,128)(2,1)}, bf16[256,256]{1,0:T(8,128)(2,1)S(1)}, u32[]{:S(2)}, u32[]{:S(2)}) %collective-permute-start.22) | collective-permute-done | bytes 131104 | tf_op jit(solution)/shard_map/ppermute | solution.py:234
  94.8 10.8 %collective-permute-start.9 = (bf16[256,256]{1,0:T(8,128)(2,1)S(1)}, bf16[256,256]{1,0:T(8,128)(2,1)S(1)}, u32[]{:S(2)}, u32[]{:S(2)}) collective-permute-start(bf16[256,256]{1,0:T(8,128)(2,1)S(1)} %collective-permute-done.8.v1), channel_id=1, source_target_pairs={{0,32},{32,64},{64,96},{96,128},{128,160},{160,192},{192,224},{1,3... | collective-permute-start | bytes 393224 | tf_op jit(solution)/shard_map/ppermute | solution.py:208
  105.6 1.0 add_convert_fusion
  106.6 0.9 collective-permute-start.25
  107.5 1.1 collective-permute-start.24
  108.7 2.1 %collective-permute-start.23 = (bf16[256,256]{1,0:T(8,128)(2,1)S(1)}, bf16[256,256]{1,0:T(8,128)(2,1)S(1)}, u32[]{:S(2)}, u32[]{:S(2)}) collective-permute-start(bf16[256,256]{1,0:T(8,128)(2,1)S(1)} %add_convert_fusion), channel_id=1, source_target_pairs={{0,2},{2,4},{4,6},{6,0},{1,3},{3,5},{5,7},{7,1},{8,10},{10,12},{12... | collective-permute-start | bytes 393224 | tf_op jit(solution)/shard_map/ppermute | solution.py:243
  110.8 2.2 %collective-permute-start.10 = (bf16[256,256]{1,0:T(8,128)(2,1)S(1)}, bf16[256,256]{1,0:T(8,128)(2,1)S(1)}, u32[]{:S(2)}, u32[]{:S(2)}) collective-permute-start(bf16[256,256]{1,0:T(8,128)(2,1)S(1)} %collective-permute-done.9.v2), channel_id=1, source_target_pairs={{0,32},{32,64},{64,96},{96,128},{128,160},{160,192},{192,224},{1,3... | collective-permute-start | bytes 393224 | tf_op jit(solution)/shard_map/ppermute | solution.py:208
  113.0 1.3 collective-permute-done.25
  114.3 0.9 collective-permute-done.23
  115.2 0.1 pad_maximum_fusion.mine
  115.2 0.1 collective-permute-start.26
  115.3 0.1 collective-permute-done.10.v3
  115.5 5.2 %collective-permute-start.11 = (bf16[256,256]{1,0:T(8,128)(2,1)S(1)}, bf16[256,256]{1,0:T(8,128)(2,1)S(1)}, u32[]{:S(2)}, u32[]{:S(2)}) collective-permute-start(bf16[256,256]{1,0:T(8,128)(2,1)S(1)} %collective-permute-done.10.v3), channel_id=1, source_target_pairs={{0,32},{32,64},{64,96},{96,128},{128,160},{160,192},{192,224},{1,3... | collective-permute-start | bytes 393224 | tf_op jit(solution)/shard_map/ppermute | solution.py:208
  120.7 2.5 %collective-permute-done.11.v4 = bf16[256,256]{1,0:T(8,128)(2,1)S(1)} collective-permute-done((bf16[256,256]{1,0:T(8,128)(2,1)S(1)}, bf16[256,256]{1,0:T(8,128)(2,1)S(1)}, u32[]{:S(2)}, u32[]{:S(2)}) %collective-permute-start.11) | collective-permute-done | bytes 131104 | tf_op jit(solution)/shard_map/ppermute | solution.py:208
  123.2 0.6 copy-done.19
  123.8 16.9 %grads.1 = (bf16[128,2048]{1,0:T(8,128)(2,1)}, bf16[128,2048]{1,0:T(8,128)(2,1)}, f32[256,256]{1,0:T(8,128)}, bf16[256,256]{1,0:T(8,128)(2,1)}, bf16[256,256]{1,...) custom-call(s32[3]{0:T(128)} %pad_add_fusion.1.s_ref, bf16[128,4096]{1,0:T(8,128)(2,1)} %bitcast.42, ...), custom_call_target="tpu_custom_call" | custom-call | flops 4026531840 | bytes 16777216 | tf_op jit(solution)/shard_map/grads/pallas_call | solution.py:142
  140.8 1.3 collective-permute-start.16
  142.1 1.3 collective-permute-start.15
  143.4 1.3 collective-permute-start.14
  144.7 1.5 collective-permute-start.13
  146.2 1.1 copy-done.4
  147.3 4.2 %weight.1 = bf16[640,256]{1,0:T(8,128)(2,1)} custom-call(s32[3]{0:T(128)} %pad_add_fusion.1.s_ref, bf16[8,640,128]{2,1,0:T(8,128)(2,1)} %copy-done, bf16[8,640,128]{2,1,0:T(8,128)(2,1)} %copy-done.4, bf16[4,256,256]{2,1,0:T(8,128)(2,1)} %copy-done.2, bf16[4,256,256]{2,1,0:T(8,128)(2,1)} %copy-done.10), custom_call_target="tpu_custom_call" | custom-call | flops 671088640 | bytes 4194304 | tf_op jit(solution)/shard_map/weight/pallas_call | solution.py:175
  151.5 1.9 reshape.172
  153.4 18.6 %all-to-all-start.1 = ((bf16[32,20,256]{2,1,0:T(8,128)(2,1)}), bf16[32,20,256]{2,1,0:T(8,128)(2,1)S(1)}, u32[]{:S(2)}, u32[]{:S(2)}) async-start(bf16[32,20,256]{2,1,0:T(8,128)(2,1)} %reshape.172), calls=%async_computation.1 | async-start | bytes 786432 | tf_op jit(solution)/shard_map/all_to_all | solution.py:248
  172.0 0.1 add_convert_fusion.1
  172.1 0.9 collective-permute-start.17
  173.0 1.2 collective-permute-start.12
  174.2 3.6 %collective-permute-done.17 = bf16[128,256]{1,0:T(8,128)(2,1)S(1)} collective-permute-done((bf16[128,256]{1,0:T(8,128)(2,1)S(1)}, bf16[128,256]{1,0:T(8,128)(2,1)S(1)}, u32[]{:S(2)}, u32[]{:S(2)}) %collective-permute-start.17) | collective-permute-done | bytes 65568 | tf_op jit(solution)/shard_map/ppermute | solution.py:199
  177.8 0.7 maximum_select_fusion.1
  178.5 4.6 %all-to-all-done.1 = bf16[32,20,256]{2,1,0:T(8,128)(2,1)S(1)} async-done(((bf16[32,20,256]{2,1,0:T(8,128)(2,1)}), bf16[32,20,256]{2,1,0:T(8,128)(2,1)S(1)}, u32[]{:S(2)}, u32[]{:S(2)}) %all-to-all-start.1) | async-done | bytes 327712 | tf_op jit(solution)/shard_map/all_to_all | solution.py:248
  183.2 1.9 collective-permute-start.27
  185.2 0.9 collective-permute-done.12
  186.1 1.2 maximum_select_fusion
  187.3 10.2 %collective-permute-done.27 = f32[20,512]{1,0:T(8,128)S(1)} collective-permute-done((f32[20,512]{1,0:T(8,128)S(1)}, f32[20,512]{1,0:T(8,128)S(1)}, u32[]{:S(2)}, u32[]{:S(2)}) %collective-permute-start.27) | collective-permute-done | bytes 40992 | tf_op jit(solution)/shard_map/ppermute | solution.py:258
  197.5 0.6 copy.14
  (79 shorter events, 0.4 us)
Async XLA Ops:
  0.6 2.8 %copy-start.1 = (bf16[1,128,4096]{2,1,0:T(8,128)(2,1)S(1)}, bf16[1,128,4096]{2,1,0:T(8,128)(2,1)}, u32[]{:S(2)}) copy-start(bf16[1,128,4096]{2,1,0:T(8,128)(2,1)} %param.9) | copy-start | bytes 3145732
  0.6 5.0 %copy-start.20 = (bf16[1,128,512]{2,1,0:T(8,128)(2,1)S(1)}, bf16[1,128,512]{2,1,0:T(8,128)(2,1)}, u32[]{:S(2)}) copy-start(bf16[1,128,512]{2,1,0:T(8,128)(2,1)} %param.7) | copy-start | bytes 393220
  0.7 5.8 %copy-start.21 = (bf16[1,128,512]{2,1,0:T(8,128)(2,1)S(1)}, bf16[1,128,512]{2,1,0:T(8,128)(2,1)}, u32[]{:S(2)}) copy-start(bf16[1,128,512]{2,1,0:T(8,128)(2,1)} %param.8) | copy-start | bytes 393220
  0.7 7.2 %copy-start.3 = (bf16[1,128,5120]{2,1,0:T(8,128)(2,1)S(1)}, bf16[1,128,5120]{2,1,0:T(8,128)(2,1)}, u32[]{:S(2)}) copy-start(bf16[1,128,5120]{2,1,0:T(8,128)(2,1)} %param.10) | copy-start | bytes 3932164
  2.7 58.3 %collective-permute-start = (bf16[128,2048]{1,0:T(8,128)(2,1)}, bf16[128,2048]{1,0:T(8,128)(2,1)S(1)}, u32[]{:S(2)}, u32[]{:S(2)}) collective-permute-start(bf16[128,2048]{1,0:T(8,128)(2,1)} %dynamic-slice_bitcast_fusion.1), channel_id=1, source_target_pairs={{0,16},{16,0},{1,17},{17,1},{2,18},{18,2},{3,19},{19,3},{4,20},{20... | collective-permute-start | bytes 1572872 | tf_op jit(solution)/shard_map/ppermute | solution.py:199
  4.3 56.7 %collective-permute-start.1 = (bf16[128,2048]{1,0:T(8,128)(2,1)}, bf16[128,2048]{1,0:T(8,128)(2,1)S(1)}, u32[]{:S(2)}, u32[]{:S(2)}) collective-permute-start(bf16[128,2048]{1,0:T(8,128)(2,1)} %dynamic-slice_bitcast_fusion), channel_id=1, source_target_pairs={{0,16},{16,0},{1,17},{17,1},{2,18},{18,2},{3,19},{19,3},{4,20},{20... | collective-permute-start | bytes 1572872 | tf_op jit(solution)/shard_map/ppermute | solution.py:199
  5.6 24.3 %collective-permute-start.2 = (bf16[128,256]{1,0:T(8,128)(2,1)S(1)}, bf16[128,256]{1,0:T(8,128)(2,1)S(1)}, u32[]{:S(2)}, u32[]{:S(2)}) collective-permute-start(bf16[128,256]{1,0:T(8,128)(2,1)S(1)} %get-tuple-element.34), channel_id=1, source_target_pairs={{0,16},{16,0},{1,17},{17,1},{2,18},{18,2},{3,19},{19,3},{4,20},{20... | collective-permute-start | bytes 196616 | tf_op jit(solution)/shard_map/ppermute | solution.py:199
  6.5 48.7 %collective-permute-start.7 = (bf16[128,256]{1,0:T(8,128)(2,1)S(1)}, bf16[128,256]{1,0:T(8,128)(2,1)S(1)}, u32[]{:S(2)}, u32[]{:S(2)}) collective-permute-start(bf16[128,256]{1,0:T(8,128)(2,1)S(1)} %get-tuple-element.32), channel_id=1, source_target_pairs={{0,16},{16,0},{1,17},{17,1},{2,18},{18,2},{3,19},{19,3},{4,20},{20... | collective-permute-start | bytes 196616 | tf_op jit(solution)/shard_map/ppermute | solution.py:199
  9.3 5.0 %copy-start.22 = (s32[1,2048]{1,0:T(1,128)S(1)}, s32[1,2048]{1,0:T(1,128)}, u32[]{:S(2)}) copy-start(s32[1,2048]{1,0:T(1,128)} %param.11) | copy-start | bytes 24580
  9.3 50.9 %all-to-all-start = ((bf16[8,640,128]{2,1,0:T(8,128)(2,1)}), bf16[8,640,128]{2,1,0:T(8,128)(2,1)S(1)}, u32[]{:S(2)}, u32[]{:S(2)}) async-start(bf16[8,640,128]{2,1,0:T(8,128)(2,1)} %bitcast.19), calls=%async_computation | async-start | bytes 2621440 | tf_op jit(solution)/shard_map/all_to_all | solution.py:213
  29.9 31.1 %copy-start.5 = (bf16[256,256]{1,0:T(8,128)(2,1)}, bf16[256,256]{1,0:T(8,128)(2,1)S(1)}, u32[]{:S(2)}) copy-start(bf16[256,256]{1,0:T(8,128)(2,1)S(1)} %pad_maximum_fusion.1.k0) | copy-start | bytes 393220
  30.0 6.3 %collective-permute-start.3 = (bf16[256,256]{1,0:T(8,128)(2,1)S(1)}, bf16[256,256]{1,0:T(8,128)(2,1)S(1)}, u32[]{:S(2)}, u32[]{:S(2)}) collective-permute-start(bf16[256,256]{1,0:T(8,128)(2,1)S(1)} %pad_maximum_fusion.1.k0), channel_id=1, source_target_pairs={{0,32},{32,64},{64,96},{96,128},{128,160},{160,192},{192,224},{1,3... | collective-permute-start | bytes 393224 | tf_op jit(solution)/shard_map/ppermute | solution.py:207
  36.3 24.8 %copy-start.12 = (bf16[256,256]{1,0:T(8,128)(2,1)}, bf16[256,256]{1,0:T(8,128)(2,1)S(1)}, u32[]{:S(2)}) copy-start(bf16[256,256]{1,0:T(8,128)(2,1)S(1)} %collective-permute-done.3.k1) | copy-start | bytes 393220
  36.3 6.8 %collective-permute-start.4 = (bf16[256,256]{1,0:T(8,128)(2,1)S(1)}, bf16[256,256]{1,0:T(8,128)(2,1)S(1)}, u32[]{:S(2)}, u32[]{:S(2)}) collective-permute-start(bf16[256,256]{1,0:T(8,128)(2,1)S(1)} %collective-permute-done.3.k1), channel_id=1, source_target_pairs={{0,32},{32,64},{64,96},{96,128},{128,160},{160,192},{192,224},{1,3... | collective-permute-start | bytes 393224 | tf_op jit(solution)/shard_map/ppermute | solution.py:207
  43.1 18.0 %copy-start.13 = (bf16[256,256]{1,0:T(8,128)(2,1)}, bf16[256,256]{1,0:T(8,128)(2,1)S(1)}, u32[]{:S(2)}) copy-start(bf16[256,256]{1,0:T(8,128)(2,1)S(1)} %collective-permute-done.4.k2) | copy-start | bytes 393220
  43.1 7.0 %collective-permute-start.5 = (bf16[256,256]{1,0:T(8,128)(2,1)S(1)}, bf16[256,256]{1,0:T(8,128)(2,1)S(1)}, u32[]{:S(2)}, u32[]{:S(2)}) collective-permute-start(bf16[256,256]{1,0:T(8,128)(2,1)S(1)} %collective-permute-done.4.k2), channel_id=1, source_target_pairs={{0,32},{32,64},{64,96},{96,128},{128,160},{160,192},{192,224},{1,3... | collective-permute-start | bytes 393224 | tf_op jit(solution)/shard_map/ppermute | solution.py:207
  50.1 11.0 %copy-start.14 = (bf16[256,256]{1,0:T(8,128)(2,1)}, bf16[256,256]{1,0:T(8,128)(2,1)S(1)}, u32[]{:S(2)}) copy-start(bf16[256,256]{1,0:T(8,128)(2,1)S(1)} %collective-permute-done.5.k3) | copy-start | bytes 393220
  50.1 10.9 %collective-permute-start.6 = (bf16[256,256]{1,0:T(8,128)(2,1)S(1)}, bf16[256,256]{1,0:T(8,128)(2,1)S(1)}, u32[]{:S(2)}, u32[]{:S(2)}) collective-permute-start(bf16[256,256]{1,0:T(8,128)(2,1)S(1)} %collective-permute-done.5.k3), channel_id=1, source_target_pairs={{0,32},{32,64},{64,96},{96,128},{128,160},{160,192},{192,224},{1,3... | collective-permute-start | bytes 393224 | tf_op jit(solution)/shard_map/ppermute | solution.py:207
  55.2 27.2 %copy-start.6 = (bf16[256,256]{1,0:T(8,128)(2,1)}, bf16[256,256]{1,0:T(8,128)(2,1)S(1)}, u32[]{:S(2)}) copy-start(bf16[256,256]{1,0:T(8,128)(2,1)S(1)} %pad_maximum_fusion.2.v0) | copy-start | bytes 393220
  55.2 31.1 %collective-permute-start.8 = (bf16[256,256]{1,0:T(8,128)(2,1)S(1)}, bf16[256,256]{1,0:T(8,128)(2,1)S(1)}, u32[]{:S(2)}, u32[]{:S(2)}) collective-permute-start(bf16[256,256]{1,0:T(8,128)(2,1)S(1)} %pad_maximum_fusion.2.v0), channel_id=1, source_target_pairs={{0,32},{32,64},{64,96},{96,128},{128,160},{160,192},{192,224},{1,3... | collective-permute-start | bytes 393224 | tf_op jit(solution)/shard_map/ppermute | solution.py:208
  60.2 22.2 %copy-start = (bf16[8,640,128]{2,1,0:T(8,128)(2,1)}, bf16[8,640,128]{2,1,0:T(8,128)(2,1)S(1)}, u32[]{:S(2)}) copy-start(bf16[8,640,128]{2,1,0:T(8,128)(2,1)S(1)} %all-to-all-done.xo) | copy-start | bytes 3932164
  60.2 86.0 %collective-permute-start.18 = (bf16[8,640,128]{2,1,0:T(8,128)(2,1)S(1)}, bf16[8,640,128]{2,1,0:T(8,128)(2,1)S(1)}, u32[]{:S(2)}, u32[]{:S(2)}) collective-permute-start(bf16[8,640,128]{2,1,0:T(8,128)(2,1)S(1)} %all-to-all-done.xo), channel_id=1, source_target_pairs={{0,16},{16,0},{1,17},{17,1},{2,18},{18,2},{3,19},{19,3},{4,20},{20... | collective-permute-start | bytes 3932168 | tf_op jit(solution)/shard_map/ppermute | solution.py:199
  61.0 0.8 copy-start.7
  61.1 1.0 copy-start.8
  61.1 1.0 copy-start.15
  82.4 12.4 %collective-permute-start.22 = (bf16[256,256]{1,0:T(8,128)(2,1)}, bf16[256,256]{1,0:T(8,128)(2,1)S(1)}, u32[]{:S(2)}, u32[]{:S(2)}) collective-permute-start(bf16[256,256]{1,0:T(8,128)(2,1)} %get-tuple-element.28), channel_id=1, source_target_pairs={{128,0},{160,32},{192,64},{224,96},{129,1},{161,33},{193,65},{225,... | collective-permute-start | bytes 393224 | tf_op jit(solution)/shard_map/ppermute | solution.py:234
  83.7 21.9 %collective-permute-start.21 = (bf16[256,256]{1,0:T(8,128)(2,1)}, bf16[256,256]{1,0:T(8,128)(2,1)S(1)}, u32[]{:S(2)}, u32[]{:S(2)}) collective-permute-start(bf16[256,256]{1,0:T(8,128)(2,1)} %get-tuple-element.27), channel_id=1, source_target_pairs={{96,0},{128,32},{160,64},{192,96},{224,128},{97,1},{129,33},{161,6... | collective-permute-start | bytes 393224 | tf_op jit(solution)/shard_map/ppermute | solution.py:234
  85.0 20.6 %collective-permute-start.20 = (bf16[256,256]{1,0:T(8,128)(2,1)}, bf16[256,256]{1,0:T(8,128)(2,1)S(1)}, u32[]{:S(2)}, u32[]{:S(2)}) collective-permute-start(bf16[256,256]{1,0:T(8,128)(2,1)} %get-tuple-element.26), channel_id=1, source_target_pairs={{64,0},{96,32},{128,64},{160,96},{192,128},{224,160},{65,1},{97,33... | collective-permute-start | bytes 393224 | tf_op jit(solution)/shard_map/ppermute | solution.py:234
  86.3 36.9 %copy-start.16 = (bf16[256,256]{1,0:T(8,128)(2,1)}, bf16[256,256]{1,0:T(8,128)(2,1)S(1)}, u32[]{:S(2)}) copy-start(bf16[256,256]{1,0:T(8,128)(2,1)S(1)} %collective-permute-done.8.v1) | copy-start | bytes 393220
  86.3 19.3 %collective-permute-start.19 = (bf16[256,256]{1,0:T(8,128)(2,1)}, bf16[256,256]{1,0:T(8,128)(2,1)S(1)}, u32[]{:S(2)}, u32[]{:S(2)}) collective-permute-start(bf16[256,256]{1,0:T(8,128)(2,1)} %get-tuple-element.25), channel_id=1, source_target_pairs={{32,0},{64,32},{96,64},{128,96},{160,128},{192,160},{224,192},{33,... | collective-permute-start | bytes 393224 | tf_op jit(solution)/shard_map/ppermute | solution.py:234
  94.8 16.0 %collective-permute-start.9 = (bf16[256,256]{1,0:T(8,128)(2,1)S(1)}, bf16[256,256]{1,0:T(8,128)(2,1)S(1)}, u32[]{:S(2)}, u32[]{:S(2)}) collective-permute-start(bf16[256,256]{1,0:T(8,128)(2,1)S(1)} %collective-permute-done.8.v1), channel_id=1, source_target_pairs={{0,32},{32,64},{64,96},{96,128},{128,160},{160,192},{192,224},{1,3... | collective-permute-start | bytes 393224 | tf_op jit(solution)/shard_map/ppermute | solution.py:208
  106.6 7.7 %collective-permute-start.25 = (bf16[256,256]{1,0:T(8,128)(2,1)S(1)}, bf16[256,256]{1,0:T(8,128)(2,1)S(1)}, u32[]{:S(2)}, u32[]{:S(2)}) collective-permute-start(bf16[256,256]{1,0:T(8,128)(2,1)S(1)} %add_convert_fusion), channel_id=1, source_target_pairs={{0,6},{2,0},{4,2},{6,4},{1,7},{3,1},{5,3},{7,5},{8,14},{10,8},{12,... | collective-permute-start | bytes 393224 | tf_op jit(solution)/shard_map/ppermute | solution.py:243
  107.5 6.8 %collective-permute-start.24 = (bf16[256,256]{1,0:T(8,128)(2,1)S(1)}, bf16[256,256]{1,0:T(8,128)(2,1)S(1)}, u32[]{:S(2)}, u32[]{:S(2)}) collective-permute-start(bf16[256,256]{1,0:T(8,128)(2,1)S(1)} %add_convert_fusion), channel_id=1, source_target_pairs={{0,4},{2,6},{4,0},{6,2},{1,5},{3,7},{5,1},{7,3},{8,12},{10,14},{12... | collective-permute-start | bytes 393224 | tf_op jit(solution)/shard_map/ppermute | solution.py:243
  108.7 6.5 %collective-permute-start.23 = (bf16[256,256]{1,0:T(8,128)(2,1)S(1)}, bf16[256,256]{1,0:T(8,128)(2,1)S(1)}, u32[]{:S(2)}, u32[]{:S(2)}) collective-permute-start(bf16[256,256]{1,0:T(8,128)(2,1)S(1)} %add_convert_fusion), channel_id=1, source_target_pairs={{0,2},{2,4},{4,6},{6,0},{1,3},{3,5},{5,7},{7,1},{8,10},{10,12},{12... | collective-permute-start | bytes 393224 | tf_op jit(solution)/shard_map/ppermute | solution.py:243
  110.8 12.4 %copy-start.17 = (bf16[256,256]{1,0:T(8,128)(2,1)}, bf16[256,256]{1,0:T(8,128)(2,1)S(1)}, u32[]{:S(2)}) copy-start(bf16[256,256]{1,0:T(8,128)(2,1)S(1)} %collective-permute-done.9.v2) | copy-start | bytes 393220
  110.8 4.7 %collective-permute-start.10 = (bf16[256,256]{1,0:T(8,128)(2,1)S(1)}, bf16[256,256]{1,0:T(8,128)(2,1)S(1)}, u32[]{:S(2)}, u32[]{:S(2)}) collective-permute-start(bf16[256,256]{1,0:T(8,128)(2,1)S(1)} %collective-permute-done.9.v2), channel_id=1, source_target_pairs={{0,32},{32,64},{64,96},{96,128},{128,160},{160,192},{192,224},{1,3... | collective-permute-start | bytes 393224 | tf_op jit(solution)/shard_map/ppermute | solution.py:208
  115.2 25.5 %copy-start.2 = (bf16[4,256,256]{2,1,0:T(8,128)(2,1)}, bf16[4,256,256]{2,1,0:T(8,128)(2,1)S(1)}, u32[]{:S(2)}) copy-start(bf16[4,256,256]{2,1,0:T(8,128)(2,1)S(1)} %pad_maximum_fusion.mine) | copy-start | bytes 1572868
  115.2 29.4 %collective-permute-start.26 = (bf16[4,256,256]{2,1,0:T(8,128)(2,1)S(1)}, bf16[4,256,256]{2,1,0:T(8,128)(2,1)S(1)}, u32[]{:S(2)}, u32[]{:S(2)}) collective-permute-start(bf16[4,256,256]{2,1,0:T(8,128)(2,1)S(1)} %pad_maximum_fusion.mine), channel_id=1, source_target_pairs={{0,1},{1,0},{2,3},{3,2},{4,5},{5,4},{6,7},{7,6},{8,9},{9,8},{10,11... | collective-permute-start | bytes 1572872 | tf_op jit(solution)/shard_map/ppermute | solution.py:245
  115.5 7.7 %copy-start.18 = (bf16[256,256]{1,0:T(8,128)(2,1)}, bf16[256,256]{1,0:T(8,128)(2,1)S(1)}, u32[]{:S(2)}) copy-start(bf16[256,256]{1,0:T(8,128)(2,1)S(1)} %collective-permute-done.10.v3) | copy-start | bytes 393220
  115.5 7.7 %collective-permute-start.11 = (bf16[256,256]{1,0:T(8,128)(2,1)S(1)}, bf16[256,256]{1,0:T(8,128)(2,1)S(1)}, u32[]{:S(2)}, u32[]{:S(2)}) collective-permute-start(bf16[256,256]{1,0:T(8,128)(2,1)S(1)} %collective-permute-done.10.v3), channel_id=1, source_target_pairs={{0,32},{32,64},{64,96},{96,128},{128,160},{160,192},{192,224},{1,3... | collective-permute-start | bytes 393224 | tf_op jit(solution)/shard_map/ppermute | solution.py:208
  123.2 0.7 copy-start.19
  140.8 31.2 %collective-permute-start.16 = (bf16[256,256]{1,0:T(8,128)(2,1)}, bf16[256,256]{1,0:T(8,128)(2,1)S(1)}, u32[]{:S(2)}, u32[]{:S(2)}) collective-permute-start(bf16[256,256]{1,0:T(8,128)(2,1)} %get-tuple-element.23), channel_id=1, source_target_pairs={{128,0},{160,32},{192,64},{224,96},{129,1},{161,33},{193,65},{225,... | collective-permute-start | bytes 393224 | tf_op jit(solution)/shard_map/ppermute | solution.py:234
  142.1 29.9 %collective-permute-start.15 = (bf16[256,256]{1,0:T(8,128)(2,1)}, bf16[256,256]{1,0:T(8,128)(2,1)S(1)}, u32[]{:S(2)}, u32[]{:S(2)}) collective-permute-start(bf16[256,256]{1,0:T(8,128)(2,1)} %get-tuple-element.22), channel_id=1, source_target_pairs={{96,0},{128,32},{160,64},{192,96},{224,128},{97,1},{129,33},{161,6... | collective-permute-start | bytes 393224 | tf_op jit(solution)/shard_map/ppermute | solution.py:234
  143.4 28.6 %collective-permute-start.14 = (bf16[256,256]{1,0:T(8,128)(2,1)}, bf16[256,256]{1,0:T(8,128)(2,1)S(1)}, u32[]{:S(2)}, u32[]{:S(2)}) collective-permute-start(bf16[256,256]{1,0:T(8,128)(2,1)} %get-tuple-element.21), channel_id=1, source_target_pairs={{64,0},{96,32},{128,64},{160,96},{192,128},{224,160},{65,1},{97,33... | collective-permute-start | bytes 393224 | tf_op jit(solution)/shard_map/ppermute | solution.py:234
  144.7 1.5 copy-start.10
  144.7 27.3 %collective-permute-start.13 = (bf16[256,256]{1,0:T(8,128)(2,1)}, bf16[256,256]{1,0:T(8,128)(2,1)S(1)}, u32[]{:S(2)}, u32[]{:S(2)}) collective-permute-start(bf16[256,256]{1,0:T(8,128)(2,1)} %get-tuple-element.20), channel_id=1, source_target_pairs={{32,0},{64,32},{96,64},{128,96},{160,128},{192,160},{224,192},{33,... | collective-permute-start | bytes 393224 | tf_op jit(solution)/shard_map/ppermute | solution.py:234
  146.2 1.1 copy-start.4
  151.5 20.5 %copy-start.11 = (f32[256,256]{1,0:T(8,128)S(1)}, f32[256,256]{1,0:T(8,128)}, u32[]{:S(2)}) copy-start(f32[256,256]{1,0:T(8,128)} %get-tuple-element.19) | copy-start | bytes 786436
  151.5 21.5 %copy-start.23 = (bf16[128,2048]{1,0:T(8,128)(2,1)S(1)}, bf16[128,2048]{1,0:T(8,128)(2,1)}, u32[]{:S(2)}) copy-start(bf16[128,2048]{1,0:T(8,128)(2,1)} %get-tuple-element.18) | copy-start | bytes 1572868
  153.3 32.8 %copy-start.9 = (bf16[128,2048]{1,0:T(8,128)(2,1)S(1)}, bf16[128,2048]{1,0:T(8,128)(2,1)}, u32[]{:S(2)}) copy-start(bf16[128,2048]{1,0:T(8,128)(2,1)} %get-tuple-element.17) | copy-start | bytes 1572868
  153.4 29.8 %all-to-all-start.1 = ((bf16[32,20,256]{2,1,0:T(8,128)(2,1)}), bf16[32,20,256]{2,1,0:T(8,128)(2,1)S(1)}, u32[]{:S(2)}, u32[]{:S(2)}) async-start(bf16[32,20,256]{2,1,0:T(8,128)(2,1)} %reshape.172), calls=%async_computation.1 | async-start | bytes 786432 | tf_op jit(solution)/shard_map/all_to_all | solution.py:248
  172.1 5.8 %collective-permute-start.17 = (bf16[128,256]{1,0:T(8,128)(2,1)S(1)}, bf16[128,256]{1,0:T(8,128)(2,1)S(1)}, u32[]{:S(2)}, u32[]{:S(2)}) collective-permute-start(bf16[128,256]{1,0:T(8,128)(2,1)S(1)} %get-tuple-element.30), channel_id=1, source_target_pairs={{0,16},{16,0},{1,17},{17,1},{2,18},{18,2},{3,19},{19,3},{4,20},{20... | collective-permute-start | bytes 196616 | tf_op jit(solution)/shard_map/ppermute | solution.py:199
  173.0 13.1 %collective-permute-start.12 = (bf16[128,2048]{1,0:T(8,128)(2,1)S(1)}, bf16[128,2048]{1,0:T(8,128)(2,1)S(1)}, u32[]{:S(2)}, u32[]{:S(2)}) collective-permute-start(bf16[128,2048]{1,0:T(8,128)(2,1)S(1)} %copy-done.23), channel_id=1, source_target_pairs={{0,16},{16,0},{1,17},{17,1},{2,18},{18,2},{3,19},{19,3},{4,20},{20... | collective-permute-start | bytes 1572872 | tf_op jit(solution)/shard_map/ppermute | solution.py:199
  183.2 14.2 %collective-permute-start.27 = (f32[20,512]{1,0:T(8,128)S(1)}, f32[20,512]{1,0:T(8,128)S(1)}, u32[]{:S(2)}, u32[]{:S(2)}) collective-permute-start(f32[20,512]{1,0:T(8,128)S(1)} %maximum_multiply_fusion), channel_id=1, source_target_pairs={{0,0},{1,32},{2,64},{3,96},{4,128},{5,160},{6,192},{7,224},{8,1},{... | collective-permute-start | bytes 122888 | tf_op jit(solution)/shard_map/ppermute | solution.py:258

commit v2 on v1

v2 whole, which is shorter than its diff:
```python
import functools
import math

import jax
import jax.numpy as jnp
from jax import lax
from jax.experimental import pallas as pl
from jax.experimental.pallas import tpu as pltpu
from jax.sharding import Mesh
from jax.sharding import PartitionSpec as P

HEAD = 128
SCALE = 1.0 / math.sqrt(HEAD)
BF = jnp.bfloat16
F32 = jnp.float32
BACK = 4
TOK = 128
BLK = 256
WIN = (BACK + 1) * BLK
GROUP = 8
ROWS = GROUP * BLK
CHUNK = 64
VMEM = 56 * 1024 * 1024
FAR = -(2.0**100)
NT = (((1,), (1,)), ((), ()))


def heads_of(own_ref, recv_ref):
    rows = []
    for h in range(GROUP):
        cols = slice(h * HEAD, (h + 1) * HEAD)
        rows += [own_ref[:, cols], recv_ref[:, cols]]
    return jnp.concatenate(rows, axis=0)


def fold(a, op):
    return op(a.reshape(a.shape[0] // 8, 8, a.shape[1]), axis=0)


def chunks():
    return [slice(c, c + CHUNK) for c in range(0, WIN, CHUNK)]


def score_all(qo, qr, blocks, key_code, query_code, tri, keys, queries, scores):
    for i, k in enumerate(blocks):
        keys[i * BLK : (i + 1) * BLK, :HEAD] = k[...]
    keys[:, HEAD:] = key_code[...]
    queries[:, :HEAD] = heads_of(qo, qr)
    for h in range(GROUP):
        queries[h * BLK : (h + 1) * BLK, HEAD:] = query_code[...]
    scores[...] = lax.dot_general(keys[...], queries[...], NT, preferred_element_type=F32)
    scores[:BLK] += jnp.concatenate([tri[...]] * GROUP, 1)


def probs_kernel(
    s_ref, qo, qr, go, gr, k0, k1, k2, k3, k4, key_code, query_code, tri,
    shift, d0, d1, d2, d3, d4, keys, queries, scores, weights,
):
    score_all(qo, qr, (k0, k1, k2, k3, k4), key_code, query_code, tri, keys, queries, scores)
    largest = jnp.full((8, ROWS), -jnp.inf, F32)
    for rows in chunks():
        largest = jnp.maximum(largest, fold(scores[rows], jnp.max))
    largest = jnp.max(largest, axis=0, keepdims=True)
    total = jnp.zeros((8, ROWS), F32)
    for rows in chunks():
        e = jnp.exp((scores[rows] - largest) * SCALE)
        total += fold(e, jnp.sum)
        weights[rows] = e.astype(BF)
    total = jnp.sum(total, axis=0, keepdims=True)
    shift[0] = jnp.broadcast_to(largest * SCALE + jnp.log(total), (8, ROWS))
    inverse = jnp.broadcast_to(1.0 / total, (8, ROWS)).T[:, :1]
    g = (heads_of(go, gr).astype(F32) * inverse).astype(BF)
    part = jnp.dot(weights[...], g, preferred_element_type=F32)
    for i, out in enumerate((d0, d1, d2, d3, d4)):
        out[...] = part[i * BLK : (i + 1) * BLK].astype(out.dtype)


def grads_kernel(
    s_ref, qo, qr, go, gr, k0, k1, k2, k3, k4, v0, v1, v2, v3, v4, key_code, query_code, tri, shift,
    dqo, dqr, d0, d1, d2, d3, d4, keys, queries, scores, key_t, values, grad_probs, grad_scores,
):
    score_all(qo, qr, (k0, k1, k2, k3, k4), key_code, query_code, tri, keys, queries, scores)
    for i, (k, v) in enumerate(zip((k0, k1, k2, k3, k4), (v0, v1, v2, v3, v4))):
        key_t[:, i * BLK : (i + 1) * BLK] = k[...].T
        values[i * BLK : (i + 1) * BLK] = v[...]
    grad_probs[...] = lax.dot_general(
        values[...], heads_of(go, gr), NT, preferred_element_type=F32
    )
    row_terms = jnp.zeros((8, ROWS), F32)
    for rows in chunks():
        p = jnp.exp(scores[rows] * SCALE - shift[0, :1])
        scores[rows] = p
        row_terms += fold(p * grad_probs[rows], jnp.sum)
    row_terms = jnp.sum(row_terms, axis=0, keepdims=True)
    for rows in chunks():
        grad_scores[rows] = (scores[rows] * (grad_probs[rows] - row_terms)).astype(BF)
    part = jnp.dot(grad_scores[...], heads_of(qo, qr), preferred_element_type=F32)
    dq = jnp.dot(key_t[...], grad_scores[...], preferred_element_type=F32)
    dq = (dq * SCALE).T.astype(BF)
    for h in range(GROUP):
        cols = slice(h * HEAD, (h + 1) * HEAD)
        dqo[:, cols] = dq[h * BLK : h * BLK + TOK]
        dqr[:, cols] = dq[h * BLK + TOK : (h + 1) * BLK]
    for i, out in enumerate((d0, d1, d2, d3, d4)):
        out[...] = (part[i * BLK : (i + 1) * BLK] * SCALE).astype(out.dtype)


def own_spec():
    return pl.BlockSpec((TOK, GROUP * HEAD), lambda j, s: (0, s[0] * 2 + j))


def recv_spec():
    return pl.BlockSpec((TOK, GROUP * HEAD), lambda j, s: (0, j))


def window_specs():
    second = pl.BlockSpec((BLK, HEAD), lambda j, s: (1, j))
    return [block_spec(), block_spec(), block_spec(), second, block_spec()]


def block_spec():
    return pl.BlockSpec((BLK, HEAD), lambda j, s: (0, j))


def same_spec(*shape):
    return pl.BlockSpec(shape, lambda j, s: (0, 0))


def shift_spec():
    return pl.BlockSpec((1, 8, ROWS), lambda j, s: (j, 0, 0))


def code_specs():
    return [same_spec(WIN, HEAD), same_spec(BLK, HEAD), same_spec(BLK, BLK)]


def score_scratch():
    return [
        pltpu.VMEM((WIN, 2 * HEAD), BF),
        pltpu.VMEM((ROWS, 2 * HEAD), BF),
        pltpu.VMEM((WIN, ROWS), F32),
    ]


def vmem_spec():
    return pl.BlockSpec(memory_space=pltpu.VMEM)


def window_outs():
    first = jax.ShapeDtypeStruct((BLK, 2 * HEAD), F32)
    return [first] + [jax.ShapeDtypeStruct((BLK, 2 * HEAD), BF)] * BACK


def run_probs(place, qo, qr, go, gr, keys, codes):
    outs = pl.pallas_call(
        probs_kernel,
        grid_spec=pltpu.PrefetchScalarGridSpec(
            num_scalar_prefetch=1,
            grid=(2,),
            in_specs=[own_spec(), recv_spec(), own_spec(), recv_spec()]
            + window_specs()
            + code_specs(),
            out_specs=[shift_spec()] + [block_spec()] * (BACK + 1),
            scratch_shapes=score_scratch() + [pltpu.VMEM((WIN, ROWS), BF)],
        ),
        out_shape=[jax.ShapeDtypeStruct((2, 8, ROWS), F32)] + window_outs(),
        compiler_params=pltpu.CompilerParams(vmem_limit_bytes=VMEM),
        cost_estimate=pl.CostEstimate(
            flops=2 * 3 * 16 * WIN * BLK * HEAD,
            bytes_accessed=16 << 20,
            transcendentals=16 * WIN * BLK,
        ),
        name="probs",
    )(place, qo, qr, go, gr, *keys, *codes)
    return outs[0], outs[1:]


def run_grads(place, qo, qr, go, gr, keys, values, codes, shift):
    outs = pl.pallas_call(
        grads_kernel,
        grid_spec=pltpu.PrefetchScalarGridSpec(
            num_scalar_prefetch=1,
            grid=(2,),
            in_specs=[own_spec(), recv_spec(), own_spec(), recv_spec()]
            + window_specs()
            + window_specs()
            + code_specs()
            + [shift_spec()],
            out_specs=[recv_spec(), recv_spec()] + [block_spec()] * (BACK + 1),
            scratch_shapes=score_scratch()
            + [
                pltpu.VMEM((HEAD, WIN), BF),
                pltpu.VMEM((WIN, HEAD), BF),
                pltpu.VMEM((WIN, ROWS), F32),
                pltpu.VMEM((WIN, ROWS), BF),
            ],
        ),
        out_shape=[jax.ShapeDtypeStruct((TOK, 16 * HEAD), BF)] * 2 + window_outs(),
        compiler_params=pltpu.CompilerParams(vmem_limit_bytes=VMEM),
        cost_estimate=pl.CostEstimate(
            flops=2 * 5 * 16 * WIN * BLK * HEAD,
            bytes_accessed=16 << 20,
            transcendentals=16 * WIN * BLK,
        ),
        name="grads",
    )(place, qo, qr, go, gr, *keys, *values, *codes, shift)
    return outs[0], outs[1], outs[2:]


def weight_kernel(s_ref, xo, xr, mine, theirs, out):
    x, c = s_ref[1], s_ref[2]
    total = jnp.zeros((xo.shape[1], 2 * HEAD), F32)
    for other, ref in ((0, mine), (1, theirs)):
        core = c if other == 0 else 1 - c
        for d in range(4):
            seq = lax.rem(x - d + 4, 4) * 2 + core
            total += jnp.dot(xo[seq], ref[d, :TOK], preferred_element_type=F32)
            total += jnp.dot(xr[seq], ref[d, TOK:], preferred_element_type=F32)
    out[...] = total.astype(out.dtype)


def run_weight(place, xo, xr, mine, theirs):
    return pl.pallas_call(
        weight_kernel,
        in_specs=[pl.BlockSpec(memory_space=pltpu.SMEM)] + [vmem_spec()] * 4,
        out_specs=vmem_spec(),
        out_shape=jax.ShapeDtypeStruct((xo.shape[1], 2 * HEAD), BF),
        compiler_params=pltpu.CompilerParams(vmem_limit_bytes=16 << 20),
        cost_estimate=pl.CostEstimate(
            flops=2 * 2048 * 640 * 256, bytes_accessed=4 << 20, transcendentals=0
        ),
        name="weight",
    )(place, xo, xr, mine, theirs)


def after(value, *others):
    return lax.optimization_barrier((value, *others))


def small_call(kernel, out_shape, name, args, tokens=()):
    def run(*refs):
        kernel(*refs[: len(args)], *refs[len(args) + len(tokens) :])

    return pl.pallas_call(
        run,
        in_specs=[vmem_spec()] * len(args) + [pl.BlockSpec(memory_space=pl.ANY)] * len(tokens),
        out_specs=vmem_spec(),
        out_shape=out_shape,
        compiler_params=pltpu.CompilerParams(vmem_limit_bytes=16 << 20),
        cost_estimate=pl.CostEstimate(flops=0, bytes_accessed=2 << 20, transcendentals=0),
        name=name,
    )(*args, *tokens)


def sum_kernel(first, a, b, c, d, out):
    total = first[...] + a[...].astype(F32) + b[...].astype(F32)
    out[...] = (total + c[...].astype(F32) + d[...].astype(F32)).astype(BF)


def body(sizes, query, key, value, grad, layer_input, segment_ids):
    nz = sizes["z"]
    z, yl, x, c = (lax.axis_index(a) for a in ("z", "yl", "x", "c"))
    place = jnp.stack([yl, x, c, z]).astype(jnp.int32)
    q, k, v, g, xin, seg = (a[0] for a in (query, key, value, grad, layer_input, segment_ids))
    swap = [(0, 1), (1, 0)]

    def half(a, which, width):
        return lax.dynamic_slice_in_dim(a, which * width, width, 1)

    def to_pair(a):
        return lax.ppermute(a, "yl", swap)

    kv_send = jnp.concatenate([half(k, 1 - yl, 256), half(v, 1 - yl, 256)], 1)
    kv_send, q, g, xin = after(kv_send, q, g, xin)
    kv_recv = to_pair(kv_send)
    q_recv = to_pair(half(q, 1 - yl, 2048))
    g_recv = to_pair(half(g, 1 - yl, 2048))

    def fetch_first(own):
        one = lax.ppermute(own, "z", [(i, i + 1) for i in range(nz - 1)])
        round_first = [(i, (i - 2) % nz) for i in range(nz - BACK)]
        return one, lax.ppermute(own, "z", round_first)

    def fetch_rest(own, one, half_way):
        both = jnp.concatenate([own, one], 0)
        both = lax.ppermute(both, "z", [(i, i + 2) for i in range(nz - 2)])
        round_rest = [((i - 2) % nz, (i - 4) % nz) for i in range(nz - BACK)]
        return [own, one, both, both, lax.ppermute(half_way, "z", round_rest)]

    own_keys = jnp.concatenate([half(k, yl, 256), kv_recv[:, :256]], 0)
    own_values = jnp.concatenate([half(v, yl, 256), kv_recv[:, 256:]], 0)
    first_keys = fetch_first(own_keys)
    first_values = fetch_first(own_values)
    keys = fetch_rest(own_keys, *first_keys)
    values = fetch_rest(own_values, *first_values)

    groups = 8
    x_t = xin.T
    width = x_t.shape[0] // groups
    rows = width // 32
    x_t = x_t.reshape(32, groups, rows, TOK).transpose(1, 0, 2, 3).reshape(groups * width, TOK)
    x_own = lax.all_to_all(x_t, ("x", "c"), split_axis=0, concat_axis=0, tiled=True)
    x_own, q_recv, g_recv = after(x_own, q_recv, g_recv)
    x_own = x_own.reshape(groups, width, TOK)
    x_recv = to_pair(x_own)

    offset = jnp.arange(TOK, dtype=jnp.int32)
    within = jnp.concatenate([yl * TOK + offset, (1 - yl) * TOK + offset])
    padded = jnp.concatenate([jnp.full((BACK * BLK,), -1, jnp.int32), seg])
    window = lax.dynamic_slice_in_dim(padded, z * BLK, WIN).reshape(BACK + 1, 2, TOK)[::-1]
    window = jnp.where(yl == 0, window, window[:, ::-1])
    query_seg = window[0].reshape(BLK, 1)
    lanes = jnp.arange(HEAD, dtype=jnp.int32)[None]
    key_code = jnp.where((lanes < 4) & (window.reshape(WIN, 1) != lanes), FAR, 0.0).astype(BF)
    query_code = (query_seg == lanes).astype(BF)
    tri = jnp.where(within[:, None] <= within[None], 0.0, -jnp.inf).astype(F32)

    def travel(parts):
        sent = []
        for d in range(1, BACK + 1):
            sent.append(lax.ppermute(parts[d], "z", [(i, i - d) for i in range(d, nz)]))
        return sent

    def add_up(first, rest):
        for a in rest:
            first = first + a.astype(F32)
        return first.astype(BF)

    codes = (key_code, query_code, tri)
    shift, value_parts = run_probs(place, q, q_recv, g, g_recv, keys, codes)
    value_sent = travel(value_parts)
    dq_own, dq_far, key_parts = run_grads(
        place, q, q_recv, g, g_recv, keys, values, codes, shift
    )
    value_first, dq_far, key_parts, *value_sent = after(
        value_parts[0], dq_far, key_parts, *value_sent
    )
    value_low = add_up(value_first, value_sent)

    near = [value_low]
    for d in range(1, 4):
        near.append(lax.ppermute(value_low, "x", [(i, (i + d) % 4) for i in range(4)]))
    near = jnp.stack(near)
    far = lax.ppermute(near, "c", swap)
    part = run_weight(place, x_own, x_recv, near, far)
    dq_recv = to_pair(dq_far)
    key_sent = travel(key_parts)
    key_block = jax.ShapeDtypeStruct((BLK, 2 * HEAD), BF)
    key_low = small_call(sum_kernel, key_block, "key_sum", (key_parts[0], *key_sent), (part,))
    part = lax.all_to_all(
        part.reshape(32, rows, 256), ("z", "yl", "yh"), split_axis=0, concat_axis=0, tiled=True
    )
    total = part.reshape(nz, 2, 2, rows, 256).astype(F32).sum(axis=(0, 2))
    total = jnp.concatenate([total[0], total[1]], axis=1)
    weight = total * (1.0 / math.sqrt(16 * 2048))

    def join(mine, theirs):
        return jnp.where(
            yl == 0,
            jnp.concatenate([mine, theirs], 1),
            jnp.concatenate([theirs, mine], 1),
        )

    dq = join(dq_own, dq_recv)
    dk = join(key_low[:TOK], to_pair(key_low[TOK:]))
    return dq[None], dk[None], weight


def solution(mesh):
    fine = Mesh(mesh.devices.reshape(8, 2, 2, 4, 2), ("z", "yl", "yh", "x", "c"))
    sizes = dict(fine.shape)
    tokens = P(("yh", "x", "c"), ("z", "yl"), None)
    return jax.shard_map(
        functools.partial(body, sizes),
        mesh=fine,
        in_specs=(tokens,) * 5 + (P(("yh", "x", "c"), None),),
        out_specs=(tokens, tokens, P(("z", "yl", "yh", "x", "c"), None)),
        check_vma=False,
    )
```

time: 199 us -> 148 us (0.74)
  the two profiles are of different devices: /device:TPU:30 before, /device:TPU:32 now
where the time goes in v2:
time: 148 us; the launch traced here: 147 us
  starting transfers between devices  70.3 us (48%)
  Pallas kernels  31.4 us (21%)
  waiting for transfers between devices  28.3 us (19%)
  local copies, waits for them, and re-layouts  9.19 us (6%)
  other arithmetic  6.59 us (4%)
    pallas_call x1, Pallas kernels, run_grads(): pl.pallas_call(grads_kernel, grid_spec=pltpu.PrefetchScalarGridSpec(num_s...  16.2 us
    ppermute x8, starting transfers between devices, travel(): sent.append(lax.ppermute(parts[d], 'z', [(i, i - d) for i in range(d, nz)]))  15.5 us
    ppermute x8, waiting for transfers between devices, travel(): sent.append(lax.ppermute(parts[d], 'z', [(i, i - d) for i in range(d, nz)]))  13.7 us
    all_to_all x1, starting transfers between devices, body(): lax.all_to_all(part.reshape(32, rows, 256), ('z', 'yl', 'yh'), split_axis...  13 us
    pallas_call x1, Pallas kernels, run_probs(): pl.pallas_call(probs_kernel, grid_spec=pltpu.PrefetchScalarGridSpec(num_s...  13 us
    ppermute x2, starting transfers between devices, fetch_rest(): return [own, one, both, both, lax.ppermute(half_way, 'z', round_rest)]  7.83 us
    ppermute x3, waiting for transfers between devices, body(): lax.ppermute(value_low, 'x', [(i, (i + d) % 4) for i in range(4)])  7.32 us
    ppermute x2, starting transfers between devices, fetch_first(): return (one, lax.ppermute(own, 'z', round_first))  6.96 us
  transfers between devices with their start and end apart: 28, of which 10 were waited for; matrix products, arithmetic and copies ran while one was open for 9% of the time, Pallas kernels for 21%

profile of v2, /device:TPU:32, one launch (start us, length us, event | category | flops | bytes accessed | tf_op | source)
XLA Modules:
  0.0 146.9 jit_solution(15903020484645576334)
XLA Ops:
  0.6 1.1 dynamic-slice_bitcast_fusion
  1.7 0.7 pad_maximum_fusion.3
  2.4 1.6 %collective-permute-start.2 = (bf16[128,512]{1,0:T(8,128)(2,1)}, bf16[128,512]{1,0:T(8,128)(2,1)}, u32[]{:S(2)}, u32[]{:S(2)}) collective-permute-start(bf16[128,512]{1,0:T(8,128)(2,1)} %pad_maximum_fusion.3), channel_id=1, source_target_pairs={{0,16},{16,0},{1,17},{17,1},{2,18},{18,2},{3,19},{19,3},{4,20},{20... | collective-permute-start | bytes 393224 | tf_op jit(solution)/shard_map/ppermute | solution.py:271
  4.0 1.9 %constant_dynamic-slice_fusion = bf16[128,2048]{1,0:T(8,128)(2,1)} fusion(bf16[128,4096]{1,0:T(8,128)(2,1)} %bitcast.50, s32[]{:T(128)S(6)} %select_n.63), kind=kLoop, calls=%fused_computation.26 | loop fusion | bytes 1048580 | tf_op jit(solution)/shard_map/dynamic_slice | solution.py:268
  5.8 0.4 collective-permute-start.1
  6.3 1.1 constant_dynamic-slice_fusion.1
  7.4 1.7 %collective-permute-start = (bf16[128,2048]{1,0:T(8,128)(2,1)S(1)}, bf16[128,2048]{1,0:T(8,128)(2,1)}, u32[]{:S(2)}, u32[]{:S(2)}) collective-permute-start(bf16[128,2048]{1,0:T(8,128)(2,1)S(1)} %constant_dynamic-slice_fusion.1), channel_id=1, source_target_pairs={{0,16},{16,0},{1,17},{17,1},{2,18},{18,2},{3,19},{19,3},{4,20},{20... | collective-permute-start | bytes 1572872 | tf_op jit(solution)/shard_map/ppermute | solution.py:271
  9.0 0.8 copy.14
  9.8 0.3 reshape.149
  10.1 0.2 copy.15
  10.3 1.3 copy.16
  11.6 4.4 %all-to-all-start = ((bf16[8,640,128]{2,1,0:T(8,128)(2,1)}), bf16[8,640,128]{2,1,0:T(8,128)(2,1)S(1)}, u32[]{:S(2)}, u32[]{:S(2)}) async-start(bf16[8,640,128]{2,1,0:T(8,128)(2,1)} %copy.16), calls=%async_computation | async-start | bytes 2621440 | tf_op jit(solution)/shard_map/all_to_all | solution.py:302
  16.1 0.1 pad_dynamic-slice_fusion
  16.3 1.0 select_convert_fusion.key_code
  17.2 0.8 compare_select_fusion.tri
  18.0 0.9 fusion.2
  18.9 3.8 %collective-permute-start.3 = (bf16[256,256]{1,0:T(8,128)(2,1)S(1)}, bf16[256,256]{1,0:T(8,128)(2,1)S(1)}, u32[]{:S(2)}, u32[]{:S(2)}) collective-permute-start(bf16[256,256]{1,0:T(8,128)(2,1)S(1)} %pad_maximum_fusion.4.k0), channel_id=1, source_target_pairs={{0,32},{32,64},{64,96},{96,128},{128,160},{160,192},{192,224},{1,3... | collective-permute-start | bytes 393224 | tf_op jit(solution)/shard_map/ppermute | solution.py:280
  22.8 4.8 %collective-permute-start.5 = (bf16[256,256]{1,0:T(8,128)(2,1)S(1)}, bf16[256,256]{1,0:T(8,128)(2,1)}, u32[]{:S(2)}, u32[]{:S(2)}) collective-permute-start(bf16[256,256]{1,0:T(8,128)(2,1)S(1)} %pad_maximum_fusion.4.k0), channel_id=1, source_target_pairs={{0,192},{32,224},{64,0},{96,32},{1,193},{33,225},{65,1},{97,33},{2... | collective-permute-start | bytes 393224 | tf_op jit(solution)/shard_map/ppermute | solution.py:282
  27.6 1.9 %collective-permute-start.7 = (bf16[256,256]{1,0:T(8,128)(2,1)S(1)}, bf16[256,256]{1,0:T(8,128)(2,1)S(1)}, u32[]{:S(2)}, u32[]{:S(2)}) collective-permute-start(bf16[256,256]{1,0:T(8,128)(2,1)S(1)} %pad_maximum_fusion.5.v0), channel_id=1, source_target_pairs={{0,32},{32,64},{64,96},{96,128},{128,160},{160,192},{192,224},{1,3... | collective-permute-start | bytes 393224 | tf_op jit(solution)/shard_map/ppermute | solution.py:280
  29.6 3.9 %collective-permute-start.4 = (bf16[512,256]{1,0:T(8,128)(2,1)S(1)}, bf16[512,256]{1,0:T(8,128)(2,1)S(1)}, u32[]{:S(2)}, u32[]{:S(2)}) collective-permute-start(bf16[512,256]{1,0:T(8,128)(2,1)S(1)} %pad_maximum_fusion.1), channel_id=1, source_target_pairs={{0,64},{32,96},{64,128},{96,160},{128,192},{160,224},{1,65},{33,97... | collective-permute-start | bytes 786440 | tf_op jit(solution)/shard_map/ppermute | solution.py:286
  33.5 0.7 fusion.1.query_code
  34.3 0.9 collective-permute-done.7.v1
  35.1 2.2 %collective-permute-start.9 = (bf16[256,256]{1,0:T(8,128)(2,1)S(1)}, bf16[256,256]{1,0:T(8,128)(2,1)}, u32[]{:S(2)}, u32[]{:S(2)}) collective-permute-start(bf16[256,256]{1,0:T(8,128)(2,1)S(1)} %pad_maximum_fusion.5.v0), channel_id=1, source_target_pairs={{0,192},{32,224},{64,0},{96,32},{1,193},{33,225},{65,1},{97,33},{2... | collective-permute-start | bytes 393224 | tf_op jit(solution)/shard_map/ppermute | solution.py:282
  37.3 1.9 %collective-permute-start.6 = (bf16[256,256]{1,0:T(8,128)(2,1)}, bf16[256,256]{1,0:T(8,128)(2,1)}, u32[]{:S(2)}, u32[]{:S(2)}) collective-permute-start(bf16[256,256]{1,0:T(8,128)(2,1)} %collective-permute-done.5), channel_id=1, source_target_pairs={{192,128},{224,160},{0,192},{32,224},{193,129},{225,161},{1,193},{... | collective-permute-start | bytes 393224 | tf_op jit(solution)/shard_map/ppermute | solution.py:288
  39.3 0.6 pad_add_fusion.1.s_ref
  39.9 3.1 %collective-permute-done.9 = bf16[256,256]{1,0:T(8,128)(2,1)} collective-permute-done((bf16[256,256]{1,0:T(8,128)(2,1)S(1)}, bf16[256,256]{1,0:T(8,128)(2,1)}, u32[]{:S(2)}, u32[]{:S(2)}) %collective-permute-start.9) | collective-permute-done | bytes 131104 | tf_op jit(solution)/shard_map/ppermute | solution.py:282
  43.0 1.5 %collective-permute-start.8 = (bf16[512,256]{1,0:T(8,128)(2,1)S(1)}, bf16[512,256]{1,0:T(8,128)(2,1)S(1)}, u32[]{:S(2)}, u32[]{:S(2)}) collective-permute-start(bf16[512,256]{1,0:T(8,128)(2,1)S(1)} %pad_maximum_fusion.2), channel_id=1, source_target_pairs={{0,64},{32,96},{64,128},{96,160},{128,192},{160,224},{1,65},{33,97... | collective-permute-start | bytes 786440 | tf_op jit(solution)/shard_map/ppermute | solution.py:286
  44.5 5.9 %collective-permute-start.10 = (bf16[256,256]{1,0:T(8,128)(2,1)}, bf16[256,256]{1,0:T(8,128)(2,1)}, u32[]{:S(2)}, u32[]{:S(2)}) collective-permute-start(bf16[256,256]{1,0:T(8,128)(2,1)} %collective-permute-done.9), channel_id=1, source_target_pairs={{192,128},{224,160},{0,192},{32,224},{193,129},{225,161},{1,193},{... | collective-permute-start | bytes 393224 | tf_op jit(solution)/shard_map/ppermute | solution.py:288
  50.4 0.7 copy-done.11
  51.1 13.0 %probs.1 = (f32[2,8,2048]{2,1,0:T(8,128)}, f32[256,256]{1,0:T(8,128)}, bf16[256,256]{1,0:T(8,128)(2,1)}, bf16[256,256]{1,0:T(8,128)(2,1)}, bf16[256,256]{1,0:T(8,128)(2,1)}, /*index=5*/bf16[256,256]{1,0:T(8,128)(2,1)}) custom-call(s32[4]{0:T(128)} %pad_add_fusion.1.s_ref, bf16[128,4096]{1,0:T(8,128)(2,1)} %bitcast.48, ...), custom_call_target="tpu_custom_call" | custom-call | flops 4026531840 | bytes 16777216 | tf_op jit(solution)/shard_map/probs/pallas_call | solution.py:155
  64.2 5.8 %collective-permute-start.11 = (bf16[256,256]{1,0:T(8,128)(2,1)}, bf16[256,256]{1,0:T(8,128)(2,1)S(1)}, u32[]{:S(2)}, u32[]{:S(2)}) collective-permute-start(bf16[256,256]{1,0:T(8,128)(2,1)} %get-tuple-element.49), channel_id=1, source_target_pairs={{32,0},{64,32},{96,64},{128,96},{160,128},{192,160},{224,192},{33,... | collective-permute-start | bytes 393224 | tf_op jit(solution)/shard_map/ppermute | solution.py:321
  70.0 1.3 collective-permute-start.12
  71.3 1.3 collective-permute-start.13
  72.6 1.3 collective-permute-start.14
  73.9 0.7 collective-permute-start.20
  74.7 16.2 %grads.1 = (bf16[128,2048]{1,0:T(8,128)(2,1)}, bf16[128,2048]{1,0:T(8,128)(2,1)}, f32[256,256]{1,0:T(8,128)}, bf16[256,256]{1,0:T(8,128)(2,1)}, bf16[256,256]{1,...) custom-call(s32[4]{0:T(128)} %pad_add_fusion.1.s_ref, bf16[128,4096]{1,0:T(8,128)(2,1)} %bitcast.49, ...), custom_call_target="tpu_custom_call" | custom-call | flops 6710886400 | bytes 16777216 | tf_op jit(solution)/shard_map/grads/pallas_call | solution.py:179
  91.0 3.6 %collective-permute-done.14 = bf16[256,256]{1,0:T(8,128)(2,1)S(1)} collective-permute-done((bf16[256,256]{1,0:T(8,128)(2,1)}, bf16[256,256]{1,0:T(8,128)(2,1)S(1)}, u32[]{:S(2)}, u32[]{:S(2)}) %collective-permute-start.14) | collective-permute-done | bytes 131104 | tf_op jit(solution)/shard_map/ppermute | solution.py:321
  94.5 0.1 add_convert_fusion
  94.6 3.0 %collective-permute-start.23 = (bf16[256,256]{1,0:T(8,128)(2,1)S(1)}, bf16[256,256]{1,0:T(8,128)(2,1)S(1)}, u32[]{:S(2)}, u32[]{:S(2)}) collective-permute-start(bf16[256,256]{1,0:T(8,128)(2,1)S(1)} %add_convert_fusion), channel_id=1, source_target_pairs={{0,6},{2,0},{4,2},{6,4},{1,7},{3,1},{5,3},{7,5},{8,14},{10,8},{12,... | collective-permute-start | bytes 393224 | tf_op jit(solution)/shard_map/ppermute | solution.py:342
  97.6 0.9 collective-permute-start.22
  98.4 0.9 collective-permute-start.21
  99.3 3.6 %collective-permute-done.23 = bf16[256,256]{1,0:T(8,128)(2,1)S(1)} collective-permute-done((bf16[256,256]{1,0:T(8,128)(2,1)S(1)}, bf16[256,256]{1,0:T(8,128)(2,1)S(1)}, u32[]{:S(2)}, u32[]{:S(2)}) %collective-permute-start.23) | collective-permute-done | bytes 131104 | tf_op jit(solution)/shard_map/ppermute | solution.py:342
  102.9 2.3 %collective-permute-done.22 = bf16[256,256]{1,0:T(8,128)(2,1)S(1)} collective-permute-done((bf16[256,256]{1,0:T(8,128)(2,1)S(1)}, bf16[256,256]{1,0:T(8,128)(2,1)S(1)}, u32[]{:S(2)}, u32[]{:S(2)}) %collective-permute-start.22) | collective-permute-done | bytes 131104 | tf_op jit(solution)/shard_map/ppermute | solution.py:342
  105.2 1.4 collective-permute-done.21
  106.6 0.1 pad_maximum_fusion.mine
  106.7 0.1 collective-permute-start.24
  106.8 0.5 collective-permute-start.15
  107.3 1.9 %collective-permute-start.16 = (bf16[256,256]{1,0:T(8,128)(2,1)}, bf16[256,256]{1,0:T(8,128)(2,1)S(1)}, u32[]{:S(2)}, u32[]{:S(2)}) collective-permute-start(bf16[256,256]{1,0:T(8,128)(2,1)} %get-tuple-element.55), channel_id=1, source_target_pairs={{32,0},{64,32},{96,64},{128,96},{160,128},{192,160},{224,192},{33,... | collective-permute-start | bytes 393224 | tf_op jit(solution)/shard_map/ppermute | solution.py:321
  109.2 1.3 collective-permute-start.17
  110.6 1.3 collective-permute-start.18
  111.9 1.3 collective-permute-start.19
  113.2 2.0 %weight.1.refs_5_ = bf16[640,256]{1,0:T(8,128)(2,1)S(1)} custom-call(s32[4]{0:T(128)S(1)} %copy-done.1, bf16[8,640,128]{2,1,0:T(8,128)(2,1)S(1)} %all-to-all-done, bf16[8,640,128]{2,1,0:T(8,128)(2,1)S(1)} %collective-permute-done.20.xr, bf16[4,256,256]{2,1,0:T(8,128)(2,1)S(1)} %pad_maximum_fusion.mine, bf16[4,256,256]{2,1,0:T(8,128)(2,1)S(1)} %collective-permute-done.24.theirs), custom_call_target="tpu_custom_call" | custom-call | flops 671088640 | bytes 4194304 | tf_op jit(solution)/shard_map/weight/pallas_call | solution.py:223
  115.2 0.8 reshape.152
  116.1 13.0 %all-to-all-start.1 = ((bf16[32,20,256]{2,1,0:T(8,128)(2,1)}), bf16[32,20,256]{2,1,0:T(8,128)(2,1)S(1)}, u32[]{:S(2)}, u32[]{:S(2)}) async-start(bf16[32,20,256]{2,1,0:T(8,128)(2,1)} %reshape.152), calls=%async_computation.1 | async-start | bytes 786432 | tf_op jit(solution)/shard_map/all_to_all | solution.py:350
  129.1 1.0 collective-permute-done.18.refs_3_
  130.1 9.1 %collective-permute-done.19.refs_4_ = bf16[256,256]{1,0:T(8,128)(2,1)S(1)} collective-permute-done((bf16[256,256]{1,0:T(8,128)(2,1)S(1)}, bf16[256,256]{1,0:T(8,128)(2,1)S(1)}, u32[]{:S(2)}, u32[]{:S(2)}) %collective-permute-start.19) | collective-permute-done | bytes 131104 | tf_op jit(solution)/shard_map/ppermute | solution.py:321
  139.3 0.1 key_sum.1
  139.4 1.6 %collective-permute-start.25 = (bf16[128,256]{1,0:T(8,128)(2,1)S(1)}, bf16[128,256]{1,0:T(8,128)(2,1)S(1)}, u32[]{:S(2)}, u32[]{:S(2)}) collective-permute-start(bf16[128,256]{1,0:T(8,128)(2,1)S(1)} %get-tuple-element.66), channel_id=1, source_target_pairs={{0,16},{16,0},{1,17},{17,1},{2,18},{18,2},{3,19},{19,3},{4,20},{20... | collective-permute-start | bytes 196616 | tf_op jit(solution)/shard_map/ppermute | solution.py:271
  141.0 1.2 maximum_select_fusion
  142.2 1.7 %collective-permute-done.25 = bf16[128,256]{1,0:T(8,128)(2,1)S(1)} collective-permute-done((bf16[128,256]{1,0:T(8,128)(2,1)S(1)}, bf16[128,256]{1,0:T(8,128)(2,1)S(1)}, u32[]{:S(2)}, u32[]{:S(2)}) %collective-permute-start.25) | collective-permute-done | bytes 65568 | tf_op jit(solution)/shard_map/ppermute | solution.py:271
  144.0 0.7 maximum_select_fusion.1
  144.6 1.6 %all-to-all-done.1 = bf16[32,20,256]{2,1,0:T(8,128)(2,1)S(1)} async-done(((bf16[32,20,256]{2,1,0:T(8,128)(2,1)}), bf16[32,20,256]{2,1,0:T(8,128)(2,1)S(1)}, u32[]{:S(2)}, u32[]{:S(2)}) %all-to-all-start.1) | async-done | bytes 327712 | tf_op jit(solution)/shard_map/all_to_all | solution.py:350
  146.2 0.1 convert_reduce_fusion
  146.3 0.6 maximum_multiply_fusion
  (62 shorter events, 0.3 us)
Async XLA Ops:
  0.6 8.4 %copy-start.2 = (bf16[1,128,5120]{2,1,0:T(8,128)(2,1)S(1)}, bf16[1,128,5120]{2,1,0:T(8,128)(2,1)}, u32[]{:S(2)}) copy-start(bf16[1,128,5120]{2,1,0:T(8,128)(2,1)} %param.10) | copy-start | bytes 3932164
  2.4 15.7 %collective-permute-start.2 = (bf16[128,512]{1,0:T(8,128)(2,1)}, bf16[128,512]{1,0:T(8,128)(2,1)}, u32[]{:S(2)}, u32[]{:S(2)}) collective-permute-start(bf16[128,512]{1,0:T(8,128)(2,1)} %pad_maximum_fusion.3), channel_id=1, source_target_pairs={{0,16},{16,0},{1,17},{17,1},{2,18},{18,2},{3,19},{19,3},{4,20},{20... | collective-permute-start | bytes 393224 | tf_op jit(solution)/shard_map/ppermute | solution.py:271
  5.8 38.6 %collective-permute-start.1 = (bf16[128,2048]{1,0:T(8,128)(2,1)}, bf16[128,2048]{1,0:T(8,128)(2,1)}, u32[]{:S(2)}, u32[]{:S(2)}) collective-permute-start(bf16[128,2048]{1,0:T(8,128)(2,1)} %constant_dynamic-slice_fusion), channel_id=1, source_target_pairs={{0,16},{16,0},{1,17},{17,1},{2,18},{18,2},{3,19},{19,3},{4,20},{20... | collective-permute-start | bytes 1572872 | tf_op jit(solution)/shard_map/ppermute | solution.py:271
  7.4 43.0 %collective-permute-start = (bf16[128,2048]{1,0:T(8,128)(2,1)S(1)}, bf16[128,2048]{1,0:T(8,128)(2,1)}, u32[]{:S(2)}, u32[]{:S(2)}) collective-permute-start(bf16[128,2048]{1,0:T(8,128)(2,1)S(1)} %constant_dynamic-slice_fusion.1), channel_id=1, source_target_pairs={{0,16},{16,0},{1,17},{17,1},{2,18},{18,2},{3,19},{19,3},{4,20},{20... | collective-permute-start | bytes 1572872 | tf_op jit(solution)/shard_map/ppermute | solution.py:271
  11.6 4.5 %copy-start.9 = (s32[1,2048]{1,0:T(1,128)S(1)}, s32[1,2048]{1,0:T(1,128)}, u32[]{:S(2)}) copy-start(s32[1,2048]{1,0:T(1,128)} %param.11) | copy-start | bytes 24580
  11.6 38.7 %all-to-all-start = ((bf16[8,640,128]{2,1,0:T(8,128)(2,1)}), bf16[8,640,128]{2,1,0:T(8,128)(2,1)S(1)}, u32[]{:S(2)}, u32[]{:S(2)}) async-start(bf16[8,640,128]{2,1,0:T(8,128)(2,1)} %copy.16), calls=%async_computation | async-start | bytes 2621440 | tf_op jit(solution)/shard_map/all_to_all | solution.py:302
  18.9 31.4 %copy-start.5 = (bf16[256,256]{1,0:T(8,128)(2,1)}, bf16[256,256]{1,0:T(8,128)(2,1)S(1)}, u32[]{:S(2)}) copy-start(bf16[256,256]{1,0:T(8,128)(2,1)S(1)} %pad_maximum_fusion.4.k0) | copy-start | bytes 393220
  18.9 10.6 %collective-permute-start.3 = (bf16[256,256]{1,0:T(8,128)(2,1)S(1)}, bf16[256,256]{1,0:T(8,128)(2,1)S(1)}, u32[]{:S(2)}, u32[]{:S(2)}) collective-permute-start(bf16[256,256]{1,0:T(8,128)(2,1)S(1)} %pad_maximum_fusion.4.k0), channel_id=1, source_target_pairs={{0,32},{32,64},{64,96},{96,128},{128,160},{160,192},{192,224},{1,3... | collective-permute-start | bytes 393224 | tf_op jit(solution)/shard_map/ppermute | solution.py:280
  22.8 14.5 %collective-permute-start.5 = (bf16[256,256]{1,0:T(8,128)(2,1)S(1)}, bf16[256,256]{1,0:T(8,128)(2,1)}, u32[]{:S(2)}, u32[]{:S(2)}) collective-permute-start(bf16[256,256]{1,0:T(8,128)(2,1)S(1)} %pad_maximum_fusion.4.k0), channel_id=1, source_target_pairs={{0,192},{32,224},{64,0},{96,32},{1,193},{33,225},{65,1},{97,33},{2... | collective-permute-start | bytes 393224 | tf_op jit(solution)/shard_map/ppermute | solution.py:282
  27.6 36.5 %copy-start.6 = (bf16[256,256]{1,0:T(8,128)(2,1)}, bf16[256,256]{1,0:T(8,128)(2,1)S(1)}, u32[]{:S(2)}) copy-start(bf16[256,256]{1,0:T(8,128)(2,1)S(1)} %pad_maximum_fusion.5.v0) | copy-start | bytes 393220
  27.6 7.5 %collective-permute-start.7 = (bf16[256,256]{1,0:T(8,128)(2,1)S(1)}, bf16[256,256]{1,0:T(8,128)(2,1)S(1)}, u32[]{:S(2)}, u32[]{:S(2)}) collective-permute-start(bf16[256,256]{1,0:T(8,128)(2,1)S(1)} %pad_maximum_fusion.5.v0), channel_id=1, source_target_pairs={{0,32},{32,64},{64,96},{96,128},{128,160},{160,192},{192,224},{1,3... | collective-permute-start | bytes 393224 | tf_op jit(solution)/shard_map/ppermute | solution.py:280
  29.5 20.8 %copy-start.7 = (bf16[256,256]{1,0:T(8,128)(2,1)}, bf16[256,256]{1,0:T(8,128)(2,1)S(1)}, u32[]{:S(2)}) copy-start(bf16[256,256]{1,0:T(8,128)(2,1)S(1)} %collective-permute-done.3.k1) | copy-start | bytes 393220
  29.6 20.8 %collective-permute-start.4 = (bf16[512,256]{1,0:T(8,128)(2,1)S(1)}, bf16[512,256]{1,0:T(8,128)(2,1)S(1)}, u32[]{:S(2)}, u32[]{:S(2)}) collective-permute-start(bf16[512,256]{1,0:T(8,128)(2,1)S(1)} %pad_maximum_fusion.1), channel_id=1, source_target_pairs={{0,64},{32,96},{64,128},{96,160},{128,192},{160,224},{1,65},{33,97... | collective-permute-start | bytes 786440 | tf_op jit(solution)/shard_map/ppermute | solution.py:286
  35.1 29.0 %copy-start.8 = (bf16[256,256]{1,0:T(8,128)(2,1)}, bf16[256,256]{1,0:T(8,128)(2,1)S(1)}, u32[]{:S(2)}) copy-start(bf16[256,256]{1,0:T(8,128)(2,1)S(1)} %collective-permute-done.7.v1) | copy-start | bytes 393220
  35.1 7.9 %collective-permute-start.9 = (bf16[256,256]{1,0:T(8,128)(2,1)S(1)}, bf16[256,256]{1,0:T(8,128)(2,1)}, u32[]{:S(2)}, u32[]{:S(2)}) collective-permute-start(bf16[256,256]{1,0:T(8,128)(2,1)S(1)} %pad_maximum_fusion.5.v0), channel_id=1, source_target_pairs={{0,192},{32,224},{64,0},{96,32},{1,193},{33,225},{65,1},{97,33},{2... | collective-permute-start | bytes 393224 | tf_op jit(solution)/shard_map/ppermute | solution.py:282
  37.3 13.0 %collective-permute-start.6 = (bf16[256,256]{1,0:T(8,128)(2,1)}, bf16[256,256]{1,0:T(8,128)(2,1)}, u32[]{:S(2)}, u32[]{:S(2)}) collective-permute-start(bf16[256,256]{1,0:T(8,128)(2,1)} %collective-permute-done.5), channel_id=1, source_target_pairs={{192,128},{224,160},{0,192},{32,224},{193,129},{225,161},{1,193},{... | collective-permute-start | bytes 393224 | tf_op jit(solution)/shard_map/ppermute | solution.py:288
  43.0 30.9 %collective-permute-start.8 = (bf16[512,256]{1,0:T(8,128)(2,1)S(1)}, bf16[512,256]{1,0:T(8,128)(2,1)S(1)}, u32[]{:S(2)}, u32[]{:S(2)}) collective-permute-start(bf16[512,256]{1,0:T(8,128)(2,1)S(1)} %pad_maximum_fusion.2), channel_id=1, source_target_pairs={{0,64},{32,96},{64,128},{96,160},{128,192},{160,224},{1,65},{33,97... | collective-permute-start | bytes 786440 | tf_op jit(solution)/shard_map/ppermute | solution.py:286
  44.5 28.1 %collective-permute-start.10 = (bf16[256,256]{1,0:T(8,128)(2,1)}, bf16[256,256]{1,0:T(8,128)(2,1)}, u32[]{:S(2)}, u32[]{:S(2)}) collective-permute-start(bf16[256,256]{1,0:T(8,128)(2,1)} %collective-permute-done.9), channel_id=1, source_target_pairs={{192,128},{224,160},{0,192},{32,224},{193,129},{225,161},{1,193},{... | collective-permute-start | bytes 393224 | tf_op jit(solution)/shard_map/ppermute | solution.py:288
  50.4 0.7 copy-start.11
  64.2 26.8 %collective-permute-start.11 = (bf16[256,256]{1,0:T(8,128)(2,1)}, bf16[256,256]{1,0:T(8,128)(2,1)S(1)}, u32[]{:S(2)}, u32[]{:S(2)}) collective-permute-start(bf16[256,256]{1,0:T(8,128)(2,1)} %get-tuple-element.49), channel_id=1, source_target_pairs={{32,0},{64,32},{96,64},{128,96},{160,128},{192,160},{224,192},{33,... | collective-permute-start | bytes 393224 | tf_op jit(solution)/shard_map/ppermute | solution.py:321
  70.0 20.9 %collective-permute-start.12 = (bf16[256,256]{1,0:T(8,128)(2,1)}, bf16[256,256]{1,0:T(8,128)(2,1)S(1)}, u32[]{:S(2)}, u32[]{:S(2)}) collective-permute-start(bf16[256,256]{1,0:T(8,128)(2,1)} %get-tuple-element.50), channel_id=1, source_target_pairs={{64,0},{96,32},{128,64},{160,96},{192,128},{224,160},{65,1},{97,33... | collective-permute-start | bytes 393224 | tf_op jit(solution)/shard_map/ppermute | solution.py:321
  71.3 19.7 %collective-permute-start.13 = (bf16[256,256]{1,0:T(8,128)(2,1)}, bf16[256,256]{1,0:T(8,128)(2,1)S(1)}, u32[]{:S(2)}, u32[]{:S(2)}) collective-permute-start(bf16[256,256]{1,0:T(8,128)(2,1)} %get-tuple-element.51), channel_id=1, source_target_pairs={{96,0},{128,32},{160,64},{192,96},{224,128},{97,1},{129,33},{161,6... | collective-permute-start | bytes 393224 | tf_op jit(solution)/shard_map/ppermute | solution.py:321
  72.6 21.9 %collective-permute-start.14 = (bf16[256,256]{1,0:T(8,128)(2,1)}, bf16[256,256]{1,0:T(8,128)(2,1)S(1)}, u32[]{:S(2)}, u32[]{:S(2)}) collective-permute-start(bf16[256,256]{1,0:T(8,128)(2,1)} %get-tuple-element.52), channel_id=1, source_target_pairs={{128,0},{160,32},{192,64},{224,96},{129,1},{161,33},{193,65},{225,... | collective-permute-start | bytes 393224 | tf_op jit(solution)/shard_map/ppermute | solution.py:321
  73.9 0.7 copy-start.12
  73.9 37.9 %collective-permute-start.20 = (bf16[8,640,128]{2,1,0:T(8,128)(2,1)S(1)}, bf16[8,640,128]{2,1,0:T(8,128)(2,1)S(1)}, u32[]{:S(2)}, u32[]{:S(2)}) collective-permute-start(bf16[8,640,128]{2,1,0:T(8,128)(2,1)S(1)} %all-to-all-done), channel_id=1, source_target_pairs={{0,16},{16,0},{1,17},{17,1},{2,18},{18,2},{3,19},{19,3},{4,20},{20... | collective-permute-start | bytes 3932168 | tf_op jit(solution)/shard_map/ppermute | solution.py:271
  74.6 19.9 %copy-start.4 = (f32[256,256]{1,0:T(8,128)S(1)}, f32[256,256]{1,0:T(8,128)}, u32[]{:S(2)}) copy-start(f32[256,256]{1,0:T(8,128)} %get-tuple-element.60) | copy-start | bytes 786436
  90.9 15.9 %copy-start.10 = (bf16[128,2048]{1,0:T(8,128)(2,1)S(1)}, bf16[128,2048]{1,0:T(8,128)(2,1)}, u32[]{:S(2)}) copy-start(bf16[128,2048]{1,0:T(8,128)(2,1)} %get-tuple-element.53) | copy-start | bytes 1572868
  90.9 19.7 %copy-start.14 = (bf16[256,256]{1,0:T(8,128)(2,1)S(1)}, bf16[256,256]{1,0:T(8,128)(2,1)}, u32[]{:S(2)}) copy-start(bf16[256,256]{1,0:T(8,128)(2,1)} %get-tuple-element.57) | copy-start | bytes 393220
  90.9 21.0 %copy-start.13 = (bf16[256,256]{1,0:T(8,128)(2,1)S(1)}, bf16[256,256]{1,0:T(8,128)(2,1)}, u32[]{:S(2)}) copy-start(bf16[256,256]{1,0:T(8,128)(2,1)} %get-tuple-element.58) | copy-start | bytes 393220
  90.9 22.3 %copy-start.1 = (s32[4]{0:T(128)S(1)}, s32[4]{0:T(128)}, u32[]{:S(2)}) copy-start(s32[4]{0:T(128)} %pad_add_fusion.1.s_ref) | copy-start | bytes 52
  94.6 8.3 %collective-permute-start.23 = (bf16[256,256]{1,0:T(8,128)(2,1)S(1)}, bf16[256,256]{1,0:T(8,128)(2,1)S(1)}, u32[]{:S(2)}, u32[]{:S(2)}) collective-permute-start(bf16[256,256]{1,0:T(8,128)(2,1)S(1)} %add_convert_fusion), channel_id=1, source_target_pairs={{0,6},{2,0},{4,2},{6,4},{1,7},{3,1},{5,3},{7,5},{8,14},{10,8},{12,... | collective-permute-start | bytes 393224 | tf_op jit(solution)/shard_map/ppermute | solution.py:342
  97.6 7.7 %collective-permute-start.22 = (bf16[256,256]{1,0:T(8,128)(2,1)S(1)}, bf16[256,256]{1,0:T(8,128)(2,1)S(1)}, u32[]{:S(2)}, u32[]{:S(2)}) collective-permute-start(bf16[256,256]{1,0:T(8,128)(2,1)S(1)} %add_convert_fusion), channel_id=1, source_target_pairs={{0,4},{2,6},{4,0},{6,2},{1,5},{3,7},{5,1},{7,3},{8,12},{10,14},{12... | collective-permute-start | bytes 393224 | tf_op jit(solution)/shard_map/ppermute | solution.py:342
  98.4 8.2 %collective-permute-start.21 = (bf16[256,256]{1,0:T(8,128)(2,1)S(1)}, bf16[256,256]{1,0:T(8,128)(2,1)S(1)}, u32[]{:S(2)}, u32[]{:S(2)}) collective-permute-start(bf16[256,256]{1,0:T(8,128)(2,1)S(1)} %add_convert_fusion), channel_id=1, source_target_pairs={{0,2},{2,4},{4,6},{6,0},{1,3},{3,5},{5,7},{7,1},{8,10},{10,12},{12... | collective-permute-start | bytes 393224 | tf_op jit(solution)/shard_map/ppermute | solution.py:342
  106.7 3.9 %collective-permute-start.24 = (bf16[4,256,256]{2,1,0:T(8,128)(2,1)S(1)}, bf16[4,256,256]{2,1,0:T(8,128)(2,1)S(1)}, u32[]{:S(2)}, u32[]{:S(2)}) collective-permute-start(bf16[4,256,256]{2,1,0:T(8,128)(2,1)S(1)} %pad_maximum_fusion.mine), channel_id=1, source_target_pairs={{0,1},{1,0},{2,3},{3,2},{4,5},{5,4},{6,7},{7,6},{8,9},{9,8},{10,11... | collective-permute-start | bytes 1572872 | tf_op jit(solution)/shard_map/ppermute | solution.py:344
  106.8 34.2 %collective-permute-start.15 = (bf16[128,2048]{1,0:T(8,128)(2,1)S(1)}, bf16[128,2048]{1,0:T(8,128)(2,1)S(1)}, u32[]{:S(2)}, u32[]{:S(2)}) collective-permute-start(bf16[128,2048]{1,0:T(8,128)(2,1)S(1)} %copy-done.10), channel_id=1, source_target_pairs={{0,16},{16,0},{1,17},{17,1},{2,18},{18,2},{3,19},{19,3},{4,20},{20... | collective-permute-start | bytes 1572872 | tf_op jit(solution)/shard_map/ppermute | solution.py:271
  107.3 21.8 %collective-permute-start.16 = (bf16[256,256]{1,0:T(8,128)(2,1)}, bf16[256,256]{1,0:T(8,128)(2,1)S(1)}, u32[]{:S(2)}, u32[]{:S(2)}) collective-permute-start(bf16[256,256]{1,0:T(8,128)(2,1)} %get-tuple-element.55), channel_id=1, source_target_pairs={{32,0},{64,32},{96,64},{128,96},{160,128},{192,160},{224,192},{33,... | collective-permute-start | bytes 393224 | tf_op jit(solution)/shard_map/ppermute | solution.py:321
  109.2 19.9 %collective-permute-start.17 = (bf16[256,256]{1,0:T(8,128)(2,1)}, bf16[256,256]{1,0:T(8,128)(2,1)S(1)}, u32[]{:S(2)}, u32[]{:S(2)}) collective-permute-start(bf16[256,256]{1,0:T(8,128)(2,1)} %get-tuple-element.56), channel_id=1, source_target_pairs={{64,0},{96,32},{128,64},{160,96},{192,128},{224,160},{65,1},{97,33... | collective-permute-start | bytes 393224 | tf_op jit(solution)/shard_map/ppermute | solution.py:321
  110.6 19.6 %collective-permute-start.18 = (bf16[256,256]{1,0:T(8,128)(2,1)S(1)}, bf16[256,256]{1,0:T(8,128)(2,1)S(1)}, u32[]{:S(2)}, u32[]{:S(2)}) collective-permute-start(bf16[256,256]{1,0:T(8,128)(2,1)S(1)} %copy-done.14), channel_id=1, source_target_pairs={{96,0},{128,32},{160,64},{192,96},{224,128},{97,1},{129,33},{161,6... | collective-permute-start | bytes 393224 | tf_op jit(solution)/shard_map/ppermute | solution.py:321
  111.9 27.4 %collective-permute-start.19 = (bf16[256,256]{1,0:T(8,128)(2,1)S(1)}, bf16[256,256]{1,0:T(8,128)(2,1)S(1)}, u32[]{:S(2)}, u32[]{:S(2)}) collective-permute-start(bf16[256,256]{1,0:T(8,128)(2,1)S(1)} %copy-done.13), channel_id=1, source_target_pairs={{128,0},{160,32},{192,64},{224,96},{129,1},{161,33},{193,65},{225,... | collective-permute-start | bytes 393224 | tf_op jit(solution)/shard_map/ppermute | solution.py:321
  115.2 24.0 %copy-start = (f32[256,256]{1,0:T(8,128)S(1)}, f32[256,256]{1,0:T(8,128)}, u32[]{:S(2)}) copy-start(f32[256,256]{1,0:T(8,128)} %get-tuple-element.54.refs_0_) | copy-start | bytes 786436
  115.2 25.8 %copy-start.3 = (bf16[128,2048]{1,0:T(8,128)(2,1)S(1)}, bf16[128,2048]{1,0:T(8,128)(2,1)}, u32[]{:S(2)}) copy-start(bf16[128,2048]{1,0:T(8,128)(2,1)} %get-tuple-element.41) | copy-start | bytes 1572868
  116.1 30.2 %all-to-all-start.1 = ((bf16[32,20,256]{2,1,0:T(8,128)(2,1)}), bf16[32,20,256]{2,1,0:T(8,128)(2,1)S(1)}, u32[]{:S(2)}, u32[]{:S(2)}) async-start(bf16[32,20,256]{2,1,0:T(8,128)(2,1)} %reshape.152), calls=%async_computation.1 | async-start | bytes 786432 | tf_op jit(solution)/shard_map/all_to_all | solution.py:350
  139.4 4.6 %collective-permute-start.25 = (bf16[128,256]{1,0:T(8,128)(2,1)S(1)}, bf16[128,256]{1,0:T(8,128)(2,1)S(1)}, u32[]{:S(2)}, u32[]{:S(2)}) collective-permute-start(bf16[128,256]{1,0:T(8,128)(2,1)S(1)} %get-tuple-element.66), channel_id=1, source_target_pairs={{0,16},{16,0},{1,17},{17,1},{2,18},{18,2},{3,19},{19,3},{4,20},{20... | collective-permute-start | bytes 196616 | tf_op jit(solution)/shard_map/ppermute | solution.py:271

commit v3 on v2

--- a/solution.py
+++ b/solution.py
@@ -41,22 +41,32 @@
     return [slice(c, c + CHUNK) for c in range(0, WIN, CHUNK)]
 
 
-def score_all(qo, qr, blocks, key_code, query_code, tri, keys, queries, scores):
+def score_all(s_ref, qo, qr, blocks, key_seg, query_seg, keys, queries, scores):
+    lanes = lax.broadcasted_iota(jnp.int32, (1, HEAD), 1)
     for i, k in enumerate(blocks):
-        keys[i * BLK : (i + 1) * BLK, :HEAD] = k[...]
-    keys[:, HEAD:] = key_code[...]
+        rows = slice(i * BLK, (i + 1) * BLK)
+        keys[rows, :HEAD] = k[...]
+        seg = jnp.broadcast_to(key_seg[:, rows], (8, BLK)).T[:, :1]
+        keys[rows, HEAD:] = jnp.where((lanes < 4) & (seg != lanes), FAR, 0.0).astype(BF)
     queries[:, :HEAD] = heads_of(qo, qr)
+    query_code = jnp.broadcast_to(query_seg[...], (8, BLK)).T[:, :1] == lanes
+    query_code = query_code.astype(BF)
     for h in range(GROUP):
-        queries[h * BLK : (h + 1) * BLK, HEAD:] = query_code[...]
+        queries[h * BLK : (h + 1) * BLK, HEAD:] = query_code
     scores[...] = lax.dot_general(keys[...], queries[...], NT, preferred_element_type=F32)
-    scores[:BLK] += jnp.concatenate([tri[...]] * GROUP, 1)
+    row = lax.broadcasted_iota(jnp.int32, (BLK, BLK), 0)
+    col = lax.broadcasted_iota(jnp.int32, (BLK, BLK), 1)
+    swapped = TOK * s_ref[0]
+    place = lax.rem(row + swapped, BLK) <= lax.rem(col + swapped, BLK)
+    tri = jnp.where(place, 0.0, -jnp.inf)
+    scores[:BLK] += jnp.concatenate([tri] * GROUP, 1)
 
 
 def probs_kernel(
-    s_ref, qo, qr, go, gr, k0, k1, k2, k3, k4, key_code, query_code, tri,
+    s_ref, qo, qr, go, gr, k0, k1, k2, k3, k4, key_seg, query_seg,
     shift, d0, d1, d2, d3, d4, keys, queries, scores, weights,
 ):
-    score_all(qo, qr, (k0, k1, k2, k3, k4), key_code, query_code, tri, keys, queries, scores)
+    score_all(s_ref, qo, qr, (k0, k1, k2, k3, k4), key_seg, query_seg, keys, queries, scores)
     largest = jnp.full((8, ROWS), -jnp.inf, F32)
     for rows in chunks():
         largest = jnp.maximum(largest, fold(scores[rows], jnp.max))
@@ -76,10 +86,10 @@
 
 
 def grads_kernel(
-    s_ref, qo, qr, go, gr, k0, k1, k2, k3, k4, v0, v1, v2, v3, v4, key_code, query_code, tri, shift,
+    s_ref, qo, qr, go, gr, k0, k1, k2, k3, k4, v0, v1, v2, v3, v4, key_seg, query_seg, shift,
     dqo, dqr, d0, d1, d2, d3, d4, keys, queries, scores, key_t, values, grad_probs, grad_scores,
 ):
-    score_all(qo, qr, (k0, k1, k2, k3, k4), key_code, query_code, tri, keys, queries, scores)
+    score_all(s_ref, qo, qr, (k0, k1, k2, k3, k4), key_seg, query_seg, keys, queries, scores)
     for i, (k, v) in enumerate(zip((k0, k1, k2, k3, k4), (v0, v1, v2, v3, v4))):
         key_t[:, i * BLK : (i + 1) * BLK] = k[...].T
         values[i * BLK : (i + 1) * BLK] = v[...]
@@ -131,7 +141,7 @@
 
 
 def code_specs():
-    return [same_spec(WIN, HEAD), same_spec(BLK, HEAD), same_spec(BLK, BLK)]
+    return [same_spec(1, WIN), same_spec(1, BLK)]
 
 
 def score_scratch():
@@ -290,9 +300,12 @@
     own_keys = jnp.concatenate([half(k, yl, 256), kv_recv[:, :256]], 0)
     own_values = jnp.concatenate([half(v, yl, 256), kv_recv[:, 256:]], 0)
     first_keys = fetch_first(own_keys)
-    first_values = fetch_first(own_values)
     keys = fetch_rest(own_keys, *first_keys)
-    values = fetch_rest(own_values, *first_values)
+    next_value = lax.ppermute(own_values, "z", [(i, i + 1) for i in range(nz - 1)])
+    far_value = lax.ppermute(own_values, "z", [(i, i + BACK) for i in range(nz - BACK)])
+    both = jnp.concatenate([own_values, next_value], 0)
+    both = lax.ppermute(both, "z", [(i, i + 2) for i in range(nz - 2)])
+    values = [own_values, next_value, both, both, far_value]
 
     groups = 8
     x_t = xin.T
@@ -304,16 +317,11 @@
     x_own = x_own.reshape(groups, width, TOK)
     x_recv = to_pair(x_own)
 
-    offset = jnp.arange(TOK, dtype=jnp.int32)
-    within = jnp.concatenate([yl * TOK + offset, (1 - yl) * TOK + offset])
     padded = jnp.concatenate([jnp.full((BACK * BLK,), -1, jnp.int32), seg])
     window = lax.dynamic_slice_in_dim(padded, z * BLK, WIN).reshape(BACK + 1, 2, TOK)[::-1]
     window = jnp.where(yl == 0, window, window[:, ::-1])
-    query_seg = window[0].reshape(BLK, 1)
-    lanes = jnp.arange(HEAD, dtype=jnp.int32)[None]
-    key_code = jnp.where((lanes < 4) & (window.reshape(WIN, 1) != lanes), FAR, 0.0).astype(BF)
-    query_code = (query_seg == lanes).astype(BF)
-    tri = jnp.where(within[:, None] <= within[None], 0.0, -jnp.inf).astype(F32)
+    key_seg = window.reshape(1, WIN)
+    query_seg = window[0].reshape(1, BLK)
 
     def travel(parts):
         sent = []
@@ -326,7 +334,7 @@
             first = first + a.astype(F32)
         return first.astype(BF)
 
-    codes = (key_code, query_code, tri)
+    codes = (key_seg, query_seg)
     shift, value_parts = run_probs(place, q, q_recv, g, g_recv, keys, codes)
     value_sent = travel(value_parts)
     dq_own, dq_far, key_parts = run_grads(

time: 148 us -> 144 us (0.973)
  waiting for transfers between devices: 28.3 us -> 25.1 us
  other arithmetic: 6.59 us -> 4.14 us
    ppermute x0 -> x3, starting transfers between devices: none -> 10.1 us  [the longest x1 6.17 us: body(): both = lax.ppermute(both, 'z', [(i, i + 2) for i in range(nz - 2)])]
    ppermute x2 -> x1, starting transfers between devices: 7.83 us -> 4.64 us  [fetch_rest(): return [own, one, both, both, lax.ppermute(half_way, 'z', round_rest)]]
    ppermute x2 -> x1, waiting for transfers between devices: 3.09 us -> 0.01 us  [fetch_first(): return (one, lax.ppermute(own, 'z', round_first))]
    ppermute x2 -> x1, starting transfers between devices: 6.96 us -> 4.77 us  [fetch_first(): return (one, lax.ppermute(own, 'z', round_first))]
    ppermute x2 -> x1, starting transfers between devices: 5.75 us -> 3.83 us  [fetch_first(): one = lax.ppermute(own, 'z', [(i, i + 1) for i in range(nz - 1)])]
    convert_element_type x2 -> x0, other arithmetic: 1.7 us -> none  [the longest x1 0.96 us: body(): jnp.where((lanes < 4) & (window.reshape(WIN, 1) != lanes), FAR, 0.0)]
    ppermute x2 -> x1, starting transfers between devices: 5.42 us -> 3.93 us  [fetch_rest(): both = lax.ppermute(both, 'z', [(i, i + 2) for i in range(nz - 2)])]
  transfers between devices with their start and end apart: 28 -> 27, of which waited for: 10 -> 8; matrix products, arithmetic and copies ran while one was open for 9% -> 7% of each run, Pallas kernels for 21% -> 22%
where the time goes in v3:
time: 144 us
  starting transfers between devices  71.1 us (49%)
  Pallas kernels  32.3 us (22%)
  waiting for transfers between devices  25.1 us (17%)
  local copies, waits for them, and re-layouts  9.75 us (7%)
  other arithmetic  4.14 us (3%)
    pallas_call x1, Pallas kernels, run_grads(): pl.pallas_call(grads_kernel, grid_spec=pltpu.PrefetchScalarGridSpec(num_s...  16.7 us
    ppermute x8, starting transfers between devices, travel(): sent.append(lax.ppermute(parts[d], 'z', [(i, i - d) for i in range(d, nz)]))  15.2 us
    ppermute x8, waiting for transfers between devices, travel(): sent.append(lax.ppermute(parts[d], 'z', [(i, i - d) for i in range(d, nz)]))  14.8 us
    pallas_call x1, Pallas kernels, run_probs(): pl.pallas_call(probs_kernel, grid_spec=pltpu.PrefetchScalarGridSpec(num_s...  13.5 us
    all_to_all x1, starting transfers between devices, body(): lax.all_to_all(part.reshape(32, rows, 256), ('z', 'yl', 'yh'), split_axis...  13 us
    ppermute x3, waiting for transfers between devices, body(): lax.ppermute(value_low, 'x', [(i, (i + d) % 4) for i in range(4)])  7.08 us
    ppermute x6, starting transfers between devices, to_pair(): return lax.ppermute(a, 'yl', swap)  6.72 us
    ppermute x1, starting transfers between devices, body(): both = lax.ppermute(both, 'z', [(i, i + 2) for i in range(nz - 2)])  6.17 us
  transfers between devices with their start and end apart: 27, of which 8 were waited for; matrix products, arithmetic and copies ran while one was open for 7% of the time, Pallas kernels for 22%

profile of v3, /device:TPU:32, one launch (start us, length us, event | category | flops | bytes accessed | tf_op | source)
XLA Modules:
  0.0 143.5 jit_solution(9509278339522666288)
XLA Ops:
  0.6 1.1 dynamic-slice_bitcast_fusion
  1.7 0.7 pad_maximum_fusion.3
  2.4 1.6 %collective-permute-start.2 = (bf16[128,512]{1,0:T(8,128)(2,1)}, bf16[128,512]{1,0:T(8,128)(2,1)}, u32[]{:S(2)}, u32[]{:S(2)}) collective-permute-start(bf16[128,512]{1,0:T(8,128)(2,1)} %pad_maximum_fusion.3), channel_id=1, source_target_pairs={{0,16},{16,0},{1,17},{17,1},{2,18},{18,2},{3,19},{19,3},{4,20},{20... | collective-permute-start | bytes 393224 | tf_op jit(solution)/shard_map/ppermute | solution.py:281
  4.0 1.9 %constant_dynamic-slice_fusion = bf16[128,2048]{1,0:T(8,128)(2,1)} fusion(bf16[128,4096]{1,0:T(8,128)(2,1)} %bitcast.48, s32[]{:T(128)S(6)} %select_n.55), kind=kLoop, calls=%fused_computation.20 | loop fusion | bytes 1048580 | tf_op jit(solution)/shard_map/dynamic_slice | solution.py:278
  5.8 0.4 collective-permute-start.1
  6.3 1.1 constant_dynamic-slice_fusion.1
  7.4 1.7 %collective-permute-start = (bf16[128,2048]{1,0:T(8,128)(2,1)S(1)}, bf16[128,2048]{1,0:T(8,128)(2,1)}, u32[]{:S(2)}, u32[]{:S(2)}) collective-permute-start(bf16[128,2048]{1,0:T(8,128)(2,1)S(1)} %constant_dynamic-slice_fusion.1), channel_id=1, source_target_pairs={{0,16},{16,0},{1,17},{17,1},{2,18},{18,2},{3,19},{19,3},{4,20},{20... | collective-permute-start | bytes 1572872 | tf_op jit(solution)/shard_map/ppermute | solution.py:281
  9.0 0.8 copy.14
  9.8 0.3 reshape.142
  10.1 0.2 copy.15
  10.3 1.3 copy.16
  11.6 4.4 %all-to-all-start = ((bf16[8,640,128]{2,1,0:T(8,128)(2,1)}), bf16[8,640,128]{2,1,0:T(8,128)(2,1)S(1)}, u32[]{:S(2)}, u32[]{:S(2)}) async-start(bf16[8,640,128]{2,1,0:T(8,128)(2,1)} %copy.16), calls=%async_computation | async-start | bytes 2621440 | tf_op jit(solution)/shard_map/all_to_all | solution.py:315
  16.0 0.0 collective-permute-done.2
  16.1 0.9 fusion
  17.0 0.0 copy-start.5
  17.0 3.8 %collective-permute-start.3 = (bf16[256,256]{1,0:T(8,128)(2,1)S(1)}, bf16[256,256]{1,0:T(8,128)(2,1)S(1)}, u32[]{:S(2)}, u32[]{:S(2)}) collective-permute-start(bf16[256,256]{1,0:T(8,128)(2,1)S(1)} %pad_maximum_fusion.4.k0), channel_id=1, source_target_pairs={{0,32},{32,64},{64,96},{96,128},{128,160},{160,192},{192,224},{1,3... | collective-permute-start | bytes 393224 | tf_op jit(solution)/shard_map/ppermute | solution.py:290
  20.8 0.1 pad_dynamic-slice_fusion
  20.9 4.8 %collective-permute-start.5 = (bf16[256,256]{1,0:T(8,128)(2,1)S(1)}, bf16[256,256]{1,0:T(8,128)(2,1)}, u32[]{:S(2)}, u32[]{:S(2)}) collective-permute-start(bf16[256,256]{1,0:T(8,128)(2,1)S(1)} %pad_maximum_fusion.4.k0), channel_id=1, source_target_pairs={{0,192},{32,224},{64,0},{96,32},{1,193},{33,225},{65,1},{97,33},{2... | collective-permute-start | bytes 393224 | tf_op jit(solution)/shard_map/ppermute | solution.py:292
  25.8 1.9 %collective-permute-start.7 = (bf16[256,256]{1,0:T(8,128)(2,1)S(1)}, bf16[256,256]{1,0:T(8,128)(2,1)S(1)}, u32[]{:S(2)}, u32[]{:S(2)}) collective-permute-start(bf16[256,256]{1,0:T(8,128)(2,1)S(1)} %pad_maximum_fusion.5.v0), channel_id=1, source_target_pairs={{0,32},{32,64},{64,96},{96,128},{128,160},{160,192},{192,224},{1,3... | collective-permute-start | bytes 393224 | tf_op jit(solution)/shard_map/ppermute | solution.py:304
  27.7 3.9 %collective-permute-start.4 = (bf16[512,256]{1,0:T(8,128)(2,1)S(1)}, bf16[512,256]{1,0:T(8,128)(2,1)S(1)}, u32[]{:S(2)}, u32[]{:S(2)}) collective-permute-start(bf16[512,256]{1,0:T(8,128)(2,1)S(1)} %pad_maximum_fusion.1), channel_id=1, source_target_pairs={{0,64},{32,96},{64,128},{96,160},{128,192},{160,224},{1,65},{33,97... | collective-permute-start | bytes 786440 | tf_op jit(solution)/shard_map/ppermute | solution.py:296
  31.7 0.0 copy-start.10
  31.7 4.6 %collective-permute-start.6 = (bf16[256,256]{1,0:T(8,128)(2,1)}, bf16[256,256]{1,0:T(8,128)(2,1)S(1)}, u32[]{:S(2)}, u32[]{:S(2)}) collective-permute-start(bf16[256,256]{1,0:T(8,128)(2,1)} %collective-permute-done.5), channel_id=1, source_target_pairs={{192,128},{224,160},{0,192},{32,224},{193,129},{225,161},{1,193},{... | collective-permute-start | bytes 393224 | tf_op jit(solution)/shard_map/ppermute | solution.py:298
  36.4 0.7 pad_add_fusion.s_ref
  37.0 0.6 slice.30
  37.6 2.0 %collective-permute-start.9 = (bf16[256,256]{1,0:T(8,128)(2,1)S(1)}, bf16[256,256]{1,0:T(8,128)(2,1)}, u32[]{:S(2)}, u32[]{:S(2)}) collective-permute-start(bf16[256,256]{1,0:T(8,128)(2,1)S(1)} %pad_maximum_fusion.5.v0), channel_id=1, source_target_pairs={{0,128},{32,160},{64,192},{96,224},{1,129},{33,161},{65,193},{97,2... | collective-permute-start | bytes 393224 | tf_op jit(solution)/shard_map/ppermute | solution.py:305
  39.6 6.2 %collective-permute-start.8 = (bf16[512,256]{1,0:T(8,128)(2,1)S(1)}, bf16[512,256]{1,0:T(8,128)(2,1)}, u32[]{:S(2)}, u32[]{:S(2)}) collective-permute-start(bf16[512,256]{1,0:T(8,128)(2,1)S(1)} %pad_maximum_fusion.2), channel_id=1, source_target_pairs={{0,64},{32,96},{64,128},{96,160},{128,192},{160,224},{1,65},{33,97... | collective-permute-start | bytes 786440 | tf_op jit(solution)/shard_map/ppermute | solution.py:307
  45.9 0.6 copy-done.15
  46.5 0.1 copy-done.12
  46.6 13.5 %probs.1 = (f32[2,8,2048]{2,1,0:T(8,128)}, f32[256,256]{1,0:T(8,128)}, bf16[256,256]{1,0:T(8,128)(2,1)}, bf16[256,256]{1,0:T(8,128)(2,1)}, bf16[256,256]{1,0:T(8,128)(2,1)}, /*index=5*/bf16[256,256]{1,0:T(8,128)(2,1)}) custom-call(s32[4]{0:T(128)} %pad_add_fusion.s_ref, bf16[128,4096]{1,0:T(8,128)(2,1)} %bitcast.46, ...), custom_call_target="tpu_custom_call" | custom-call | flops 4026531840 | bytes 16777216 | tf_op jit(solution)/shard_map/probs/pallas_call | solution.py:165
  60.1 5.6 %collective-permute-start.10 = (bf16[256,256]{1,0:T(8,128)(2,1)}, bf16[256,256]{1,0:T(8,128)(2,1)S(1)}, u32[]{:S(2)}, u32[]{:S(2)}) collective-permute-start(bf16[256,256]{1,0:T(8,128)(2,1)} %get-tuple-element.49), channel_id=1, source_target_pairs={{32,0},{64,32},{96,64},{128,96},{160,128},{192,160},{224,192},{33,... | collective-permute-start | bytes 393224 | tf_op jit(solution)/shard_map/ppermute | solution.py:329
  65.6 1.3 collective-permute-start.11
  66.9 1.3 collective-permute-start.12
  68.3 1.3 collective-permute-start.13
  69.6 0.8 collective-permute-start.19
  70.3 16.7 %grads.1 = (bf16[128,2048]{1,0:T(8,128)(2,1)}, bf16[128,2048]{1,0:T(8,128)(2,1)}, f32[256,256]{1,0:T(8,128)}, bf16[256,256]{1,0:T(8,128)(2,1)}, bf16[256,256]{1,...) custom-call(s32[4]{0:T(128)} %pad_add_fusion.s_ref, bf16[128,4096]{1,0:T(8,128)(2,1)} %bitcast.47, ...), custom_call_target="tpu_custom_call" | custom-call | flops 6710886400 | bytes 16777216 | tf_op jit(solution)/shard_map/grads/pallas_call | solution.py:189
  87.1 4.5 %collective-permute-done.13 = bf16[256,256]{1,0:T(8,128)(2,1)S(1)} collective-permute-done((bf16[256,256]{1,0:T(8,128)(2,1)}, bf16[256,256]{1,0:T(8,128)(2,1)S(1)}, u32[]{:S(2)}, u32[]{:S(2)}) %collective-permute-start.13) | collective-permute-done | bytes 131104 | tf_op jit(solution)/shard_map/ppermute | solution.py:329
  91.5 0.1 add_convert_fusion
  91.6 2.7 %collective-permute-start.22 = (bf16[256,256]{1,0:T(8,128)(2,1)S(1)}, bf16[256,256]{1,0:T(8,128)(2,1)S(1)}, u32[]{:S(2)}, u32[]{:S(2)}) collective-permute-start(bf16[256,256]{1,0:T(8,128)(2,1)S(1)} %add_convert_fusion), channel_id=1, source_target_pairs={{0,6},{2,0},{4,2},{6,4},{1,7},{3,1},{5,3},{7,5},{8,14},{10,8},{12,... | collective-permute-start | bytes 393224 | tf_op jit(solution)/shard_map/ppermute | solution.py:350
  94.3 0.9 collective-permute-start.21
  95.2 0.9 collective-permute-start.20
  96.1 3.4 %collective-permute-done.22 = bf16[256,256]{1,0:T(8,128)(2,1)S(1)} collective-permute-done((bf16[256,256]{1,0:T(8,128)(2,1)S(1)}, bf16[256,256]{1,0:T(8,128)(2,1)S(1)}, u32[]{:S(2)}, u32[]{:S(2)}) %collective-permute-start.22) | collective-permute-done | bytes 131104 | tf_op jit(solution)/shard_map/ppermute | solution.py:350
  99.5 2.3 %collective-permute-done.21 = bf16[256,256]{1,0:T(8,128)(2,1)S(1)} collective-permute-done((bf16[256,256]{1,0:T(8,128)(2,1)S(1)}, bf16[256,256]{1,0:T(8,128)(2,1)S(1)}, u32[]{:S(2)}, u32[]{:S(2)}) %collective-permute-start.21) | collective-permute-done | bytes 131104 | tf_op jit(solution)/shard_map/ppermute | solution.py:350
  101.8 1.3 collective-permute-done.20
  103.1 0.1 pad_maximum_fusion.mine
  103.2 0.1 collective-permute-start.23
  103.3 0.6 collective-permute-start.14
  103.9 1.9 %collective-permute-start.15 = (bf16[256,256]{1,0:T(8,128)(2,1)}, bf16[256,256]{1,0:T(8,128)(2,1)S(1)}, u32[]{:S(2)}, u32[]{:S(2)}) collective-permute-start(bf16[256,256]{1,0:T(8,128)(2,1)} %get-tuple-element.55), channel_id=1, source_target_pairs={{32,0},{64,32},{96,64},{128,96},{160,128},{192,160},{224,192},{33,... | collective-permute-start | bytes 393224 | tf_op jit(solution)/shard_map/ppermute | solution.py:329
  105.8 1.3 collective-permute-start.16
  107.1 1.3 collective-permute-start.17
  108.5 1.3 collective-permute-start.18
  109.8 2.0 %weight.1.refs_5_ = bf16[640,256]{1,0:T(8,128)(2,1)S(1)} custom-call(s32[4]{0:T(128)S(1)} %copy-done.1, bf16[8,640,128]{2,1,0:T(8,128)(2,1)S(1)} %all-to-all-done, bf16[8,640,128]{2,1,0:T(8,128)(2,1)S(1)} %collective-permute-done.19.xr, bf16[4,256,256]{2,1,0:T(8,128)(2,1)S(1)} %pad_maximum_fusion.mine, bf16[4,256,256]{2,1,0:T(8,128)(2,1)S(1)} %collective-permute-done.23.theirs), custom_call_target="tpu_custom_call" | custom-call | flops 671088640 | bytes 4194304 | tf_op jit(solution)/shard_map/weight/pallas_call | solution.py:233
  111.8 0.0 copy-start.3
  111.8 0.8 reshape.146
  112.6 13.0 %all-to-all-start.1 = ((bf16[32,20,256]{2,1,0:T(8,128)(2,1)}), bf16[32,20,256]{2,1,0:T(8,128)(2,1)S(1)}, u32[]{:S(2)}, u32[]{:S(2)}) async-start(bf16[32,20,256]{2,1,0:T(8,128)(2,1)} %reshape.146), calls=%async_computation.1 | async-start | bytes 786432 | tf_op jit(solution)/shard_map/all_to_all | solution.py:358
  125.6 0.8 collective-permute-done.17.refs_3_
  126.4 9.5 %collective-permute-done.18.refs_4_ = bf16[256,256]{1,0:T(8,128)(2,1)S(1)} collective-permute-done((bf16[256,256]{1,0:T(8,128)(2,1)S(1)}, bf16[256,256]{1,0:T(8,128)(2,1)S(1)}, u32[]{:S(2)}, u32[]{:S(2)}) %collective-permute-start.18) | collective-permute-done | bytes 131104 | tf_op jit(solution)/shard_map/ppermute | solution.py:329
  135.9 0.1 key_sum.1
  136.0 1.7 %collective-permute-start.24 = (bf16[128,256]{1,0:T(8,128)(2,1)S(1)}, bf16[128,256]{1,0:T(8,128)(2,1)S(1)}, u32[]{:S(2)}, u32[]{:S(2)}) collective-permute-start(bf16[128,256]{1,0:T(8,128)(2,1)S(1)} %get-tuple-element.66), channel_id=1, source_target_pairs={{0,16},{16,0},{1,17},{17,1},{2,18},{18,2},{3,19},{19,3},{4,20},{20... | collective-permute-start | bytes 196616 | tf_op jit(solution)/shard_map/ppermute | solution.py:281
  137.7 1.2 maximum_select_fusion
  138.9 1.7 %collective-permute-done.24 = bf16[128,256]{1,0:T(8,128)(2,1)S(1)} collective-permute-done((bf16[128,256]{1,0:T(8,128)(2,1)S(1)}, bf16[128,256]{1,0:T(8,128)(2,1)S(1)}, u32[]{:S(2)}, u32[]{:S(2)}) %collective-permute-start.24) | collective-permute-done | bytes 65568 | tf_op jit(solution)/shard_map/ppermute | solution.py:281
  140.6 0.7 maximum_select_fusion.1
  141.3 1.5 %all-to-all-done.1 = bf16[32,20,256]{2,1,0:T(8,128)(2,1)S(1)} async-done(((bf16[32,20,256]{2,1,0:T(8,128)(2,1)}), bf16[32,20,256]{2,1,0:T(8,128)(2,1)S(1)}, u32[]{:S(2)}, u32[]{:S(2)}) %all-to-all-start.1) | async-done | bytes 327712 | tf_op jit(solution)/shard_map/all_to_all | solution.py:358
  142.8 0.1 convert_reduce_fusion
  142.9 0.6 maximum_multiply_fusion
  (54 shorter events, 0.2 us)
Async XLA Ops:
  0.6 8.4 %copy-start.2 = (bf16[1,128,5120]{2,1,0:T(8,128)(2,1)S(1)}, bf16[1,128,5120]{2,1,0:T(8,128)(2,1)}, u32[]{:S(2)}) copy-start(bf16[1,128,5120]{2,1,0:T(8,128)(2,1)} %param.10) | copy-start | bytes 3932164
  2.4 13.7 %collective-permute-start.2 = (bf16[128,512]{1,0:T(8,128)(2,1)}, bf16[128,512]{1,0:T(8,128)(2,1)}, u32[]{:S(2)}, u32[]{:S(2)}) collective-permute-start(bf16[128,512]{1,0:T(8,128)(2,1)} %pad_maximum_fusion.3), channel_id=1, source_target_pairs={{0,16},{16,0},{1,17},{17,1},{2,18},{18,2},{3,19},{19,3},{4,20},{20... | collective-permute-start | bytes 393224 | tf_op jit(solution)/shard_map/ppermute | solution.py:281
  5.8 33.8 %collective-permute-start.1 = (bf16[128,2048]{1,0:T(8,128)(2,1)}, bf16[128,2048]{1,0:T(8,128)(2,1)}, u32[]{:S(2)}, u32[]{:S(2)}) collective-permute-start(bf16[128,2048]{1,0:T(8,128)(2,1)} %constant_dynamic-slice_fusion), channel_id=1, source_target_pairs={{0,16},{16,0},{1,17},{17,1},{2,18},{18,2},{3,19},{19,3},{4,20},{20... | collective-permute-start | bytes 1572872 | tf_op jit(solution)/shard_map/ppermute | solution.py:281
  7.4 38.5 %collective-permute-start = (bf16[128,2048]{1,0:T(8,128)(2,1)S(1)}, bf16[128,2048]{1,0:T(8,128)(2,1)}, u32[]{:S(2)}, u32[]{:S(2)}) collective-permute-start(bf16[128,2048]{1,0:T(8,128)(2,1)S(1)} %constant_dynamic-slice_fusion.1), channel_id=1, source_target_pairs={{0,16},{16,0},{1,17},{17,1},{2,18},{18,2},{3,19},{19,3},{4,20},{20... | collective-permute-start | bytes 1572872 | tf_op jit(solution)/shard_map/ppermute | solution.py:281
  11.6 9.2 %copy-start.9 = (s32[1,2048]{1,0:T(1,128)S(1)}, s32[1,2048]{1,0:T(1,128)}, u32[]{:S(2)}) copy-start(s32[1,2048]{1,0:T(1,128)} %param.11) | copy-start | bytes 24580
  11.6 34.2 %all-to-all-start = ((bf16[8,640,128]{2,1,0:T(8,128)(2,1)}), bf16[8,640,128]{2,1,0:T(8,128)(2,1)S(1)}, u32[]{:S(2)}, u32[]{:S(2)}) async-start(bf16[8,640,128]{2,1,0:T(8,128)(2,1)} %copy.16), calls=%async_computation | async-start | bytes 2621440 | tf_op jit(solution)/shard_map/all_to_all | solution.py:315
  17.0 28.9 %copy-start.5 = (bf16[256,256]{1,0:T(8,128)(2,1)}, bf16[256,256]{1,0:T(8,128)(2,1)S(1)}, u32[]{:S(2)}) copy-start(bf16[256,256]{1,0:T(8,128)(2,1)S(1)} %pad_maximum_fusion.4.k0) | copy-start | bytes 393220
  17.0 10.7 %collective-permute-start.3 = (bf16[256,256]{1,0:T(8,128)(2,1)S(1)}, bf16[256,256]{1,0:T(8,128)(2,1)S(1)}, u32[]{:S(2)}, u32[]{:S(2)}) collective-permute-start(bf16[256,256]{1,0:T(8,128)(2,1)S(1)} %pad_maximum_fusion.4.k0), channel_id=1, source_target_pairs={{0,32},{32,64},{64,96},{96,128},{128,160},{160,192},{192,224},{1,3... | collective-permute-start | bytes 393224 | tf_op jit(solution)/shard_map/ppermute | solution.py:290
  20.9 10.8 %collective-permute-start.5 = (bf16[256,256]{1,0:T(8,128)(2,1)S(1)}, bf16[256,256]{1,0:T(8,128)(2,1)}, u32[]{:S(2)}, u32[]{:S(2)}) collective-permute-start(bf16[256,256]{1,0:T(8,128)(2,1)S(1)} %pad_maximum_fusion.4.k0), channel_id=1, source_target_pairs={{0,192},{32,224},{64,0},{96,32},{1,193},{33,225},{65,1},{97,33},{2... | collective-permute-start | bytes 393224 | tf_op jit(solution)/shard_map/ppermute | solution.py:292
  25.7 34.3 %copy-start.6 = (bf16[256,256]{1,0:T(8,128)(2,1)}, bf16[256,256]{1,0:T(8,128)(2,1)S(1)}, u32[]{:S(2)}) copy-start(bf16[256,256]{1,0:T(8,128)(2,1)S(1)} %pad_maximum_fusion.5.v0) | copy-start | bytes 393220
  25.8 11.9 %collective-permute-start.7 = (bf16[256,256]{1,0:T(8,128)(2,1)S(1)}, bf16[256,256]{1,0:T(8,128)(2,1)S(1)}, u32[]{:S(2)}, u32[]{:S(2)}) collective-permute-start(bf16[256,256]{1,0:T(8,128)(2,1)S(1)} %pad_maximum_fusion.5.v0), channel_id=1, source_target_pairs={{0,32},{32,64},{64,96},{96,128},{128,160},{160,192},{192,224},{1,3... | collective-permute-start | bytes 393224 | tf_op jit(solution)/shard_map/ppermute | solution.py:304
  27.7 18.2 %copy-start.7 = (bf16[256,256]{1,0:T(8,128)(2,1)}, bf16[256,256]{1,0:T(8,128)(2,1)S(1)}, u32[]{:S(2)}) copy-start(bf16[256,256]{1,0:T(8,128)(2,1)S(1)} %collective-permute-done.3.k1) | copy-start | bytes 393220
  27.7 18.1 %collective-permute-start.4 = (bf16[512,256]{1,0:T(8,128)(2,1)S(1)}, bf16[512,256]{1,0:T(8,128)(2,1)S(1)}, u32[]{:S(2)}, u32[]{:S(2)}) collective-permute-start(bf16[512,256]{1,0:T(8,128)(2,1)S(1)} %pad_maximum_fusion.1), channel_id=1, source_target_pairs={{0,64},{32,96},{64,128},{96,160},{128,192},{160,224},{1,65},{33,97... | collective-permute-start | bytes 786440 | tf_op jit(solution)/shard_map/ppermute | solution.py:296
  31.7 14.2 %copy-start.10 = (s32[5,2,128]{2,1,0:T(2,128)}, s32[5,2,128]{2,1,0:T(2,128)S(1)}, u32[]{:S(2)}) copy-start(s32[5,2,128]{2,1,0:T(2,128)S(1)} %reverse_select_fusion) | copy-start | bytes 15364
  31.7 14.1 %collective-permute-start.6 = (bf16[256,256]{1,0:T(8,128)(2,1)}, bf16[256,256]{1,0:T(8,128)(2,1)S(1)}, u32[]{:S(2)}, u32[]{:S(2)}) collective-permute-start(bf16[256,256]{1,0:T(8,128)(2,1)} %collective-permute-done.5), channel_id=1, source_target_pairs={{192,128},{224,160},{0,192},{32,224},{193,129},{225,161},{1,193},{... | collective-permute-start | bytes 393224 | tf_op jit(solution)/shard_map/ppermute | solution.py:298
  37.6 22.5 %copy-start.8 = (bf16[256,256]{1,0:T(8,128)(2,1)}, bf16[256,256]{1,0:T(8,128)(2,1)S(1)}, u32[]{:S(2)}) copy-start(bf16[256,256]{1,0:T(8,128)(2,1)S(1)} %collective-permute-done.7.v1) | copy-start | bytes 393220
  37.6 30.6 %collective-permute-start.9 = (bf16[256,256]{1,0:T(8,128)(2,1)S(1)}, bf16[256,256]{1,0:T(8,128)(2,1)}, u32[]{:S(2)}, u32[]{:S(2)}) collective-permute-start(bf16[256,256]{1,0:T(8,128)(2,1)S(1)} %pad_maximum_fusion.5.v0), channel_id=1, source_target_pairs={{0,128},{32,160},{64,192},{96,224},{1,129},{33,161},{65,193},{97,2... | collective-permute-start | bytes 393224 | tf_op jit(solution)/shard_map/ppermute | solution.py:305
  39.6 29.9 %collective-permute-start.8 = (bf16[512,256]{1,0:T(8,128)(2,1)S(1)}, bf16[512,256]{1,0:T(8,128)(2,1)}, u32[]{:S(2)}, u32[]{:S(2)}) collective-permute-start(bf16[512,256]{1,0:T(8,128)(2,1)S(1)} %pad_maximum_fusion.2), channel_id=1, source_target_pairs={{0,64},{32,96},{64,128},{96,160},{128,192},{160,224},{1,65},{33,97... | collective-permute-start | bytes 786440 | tf_op jit(solution)/shard_map/ppermute | solution.py:307
  45.8 0.7 copy-start.15
  45.8 0.7 copy-start.12
  60.1 27.0 %collective-permute-start.10 = (bf16[256,256]{1,0:T(8,128)(2,1)}, bf16[256,256]{1,0:T(8,128)(2,1)S(1)}, u32[]{:S(2)}, u32[]{:S(2)}) collective-permute-start(bf16[256,256]{1,0:T(8,128)(2,1)} %get-tuple-element.49), channel_id=1, source_target_pairs={{32,0},{64,32},{96,64},{128,96},{160,128},{192,160},{224,192},{33,... | collective-permute-start | bytes 393224 | tf_op jit(solution)/shard_map/ppermute | solution.py:329
  65.6 21.4 %collective-permute-start.11 = (bf16[256,256]{1,0:T(8,128)(2,1)}, bf16[256,256]{1,0:T(8,128)(2,1)S(1)}, u32[]{:S(2)}, u32[]{:S(2)}) collective-permute-start(bf16[256,256]{1,0:T(8,128)(2,1)} %get-tuple-element.50), channel_id=1, source_target_pairs={{64,0},{96,32},{128,64},{160,96},{192,128},{224,160},{65,1},{97,33... | collective-permute-start | bytes 393224 | tf_op jit(solution)/shard_map/ppermute | solution.py:329
  66.9 20.1 %collective-permute-start.12 = (bf16[256,256]{1,0:T(8,128)(2,1)}, bf16[256,256]{1,0:T(8,128)(2,1)S(1)}, u32[]{:S(2)}, u32[]{:S(2)}) collective-permute-start(bf16[256,256]{1,0:T(8,128)(2,1)} %get-tuple-element.51), channel_id=1, source_target_pairs={{96,0},{128,32},{160,64},{192,96},{224,128},{97,1},{129,33},{161,6... | collective-permute-start | bytes 393224 | tf_op jit(solution)/shard_map/ppermute | solution.py:329
  68.3 23.3 %collective-permute-start.13 = (bf16[256,256]{1,0:T(8,128)(2,1)}, bf16[256,256]{1,0:T(8,128)(2,1)S(1)}, u32[]{:S(2)}, u32[]{:S(2)}) collective-permute-start(bf16[256,256]{1,0:T(8,128)(2,1)} %get-tuple-element.52), channel_id=1, source_target_pairs={{128,0},{160,32},{192,64},{224,96},{129,1},{161,33},{193,65},{225,... | collective-permute-start | bytes 393224 | tf_op jit(solution)/shard_map/ppermute | solution.py:329
  69.6 38.9 %collective-permute-start.19 = (bf16[8,640,128]{2,1,0:T(8,128)(2,1)S(1)}, bf16[8,640,128]{2,1,0:T(8,128)(2,1)S(1)}, u32[]{:S(2)}, u32[]{:S(2)}) collective-permute-start(bf16[8,640,128]{2,1,0:T(8,128)(2,1)S(1)} %all-to-all-done), channel_id=1, source_target_pairs={{0,16},{16,0},{1,17},{17,1},{2,18},{18,2},{3,19},{19,3},{4,20},{20... | collective-permute-start | bytes 3932168 | tf_op jit(solution)/shard_map/ppermute | solution.py:281
  70.3 21.2 %copy-start.4 = (f32[256,256]{1,0:T(8,128)S(1)}, f32[256,256]{1,0:T(8,128)}, u32[]{:S(2)}) copy-start(f32[256,256]{1,0:T(8,128)} %get-tuple-element.60) | copy-start | bytes 786436
  87.0 16.3 %copy-start.11 = (bf16[128,2048]{1,0:T(8,128)(2,1)S(1)}, bf16[128,2048]{1,0:T(8,128)(2,1)}, u32[]{:S(2)}) copy-start(bf16[128,2048]{1,0:T(8,128)(2,1)} %get-tuple-element.53) | copy-start | bytes 1572868
  87.0 20.1 %copy-start.14 = (bf16[256,256]{1,0:T(8,128)(2,1)S(1)}, bf16[256,256]{1,0:T(8,128)(2,1)}, u32[]{:S(2)}) copy-start(bf16[256,256]{1,0:T(8,128)(2,1)} %get-tuple-element.57) | copy-start | bytes 393220
  87.0 21.4 %copy-start.13 = (bf16[256,256]{1,0:T(8,128)(2,1)S(1)}, bf16[256,256]{1,0:T(8,128)(2,1)}, u32[]{:S(2)}) copy-start(bf16[256,256]{1,0:T(8,128)(2,1)} %get-tuple-element.58) | copy-start | bytes 393220
  87.0 22.7 %copy-start.1 = (s32[4]{0:T(128)S(1)}, s32[4]{0:T(128)}, u32[]{:S(2)}) copy-start(s32[4]{0:T(128)} %pad_add_fusion.s_ref) | copy-start | bytes 52
  91.6 7.8 %collective-permute-start.22 = (bf16[256,256]{1,0:T(8,128)(2,1)S(1)}, bf16[256,256]{1,0:T(8,128)(2,1)S(1)}, u32[]{:S(2)}, u32[]{:S(2)}) collective-permute-start(bf16[256,256]{1,0:T(8,128)(2,1)S(1)} %add_convert_fusion), channel_id=1, source_target_pairs={{0,6},{2,0},{4,2},{6,4},{1,7},{3,1},{5,3},{7,5},{8,14},{10,8},{12,... | collective-permute-start | bytes 393224 | tf_op jit(solution)/shard_map/ppermute | solution.py:350
  94.3 7.5 %collective-permute-start.21 = (bf16[256,256]{1,0:T(8,128)(2,1)S(1)}, bf16[256,256]{1,0:T(8,128)(2,1)S(1)}, u32[]{:S(2)}, u32[]{:S(2)}) collective-permute-start(bf16[256,256]{1,0:T(8,128)(2,1)S(1)} %add_convert_fusion), channel_id=1, source_target_pairs={{0,4},{2,6},{4,0},{6,2},{1,5},{3,7},{5,1},{7,3},{8,12},{10,14},{12... | collective-permute-start | bytes 393224 | tf_op jit(solution)/shard_map/ppermute | solution.py:350
  95.2 7.9 %collective-permute-start.20 = (bf16[256,256]{1,0:T(8,128)(2,1)S(1)}, bf16[256,256]{1,0:T(8,128)(2,1)S(1)}, u32[]{:S(2)}, u32[]{:S(2)}) collective-permute-start(bf16[256,256]{1,0:T(8,128)(2,1)S(1)} %add_convert_fusion), channel_id=1, source_target_pairs={{0,2},{2,4},{4,6},{6,0},{1,3},{3,5},{5,7},{7,1},{8,10},{10,12},{12... | collective-permute-start | bytes 393224 | tf_op jit(solution)/shard_map/ppermute | solution.py:350
  103.2 3.9 %collective-permute-start.23 = (bf16[4,256,256]{2,1,0:T(8,128)(2,1)S(1)}, bf16[4,256,256]{2,1,0:T(8,128)(2,1)S(1)}, u32[]{:S(2)}, u32[]{:S(2)}) collective-permute-start(bf16[4,256,256]{2,1,0:T(8,128)(2,1)S(1)} %pad_maximum_fusion.mine), channel_id=1, source_target_pairs={{0,1},{1,0},{2,3},{3,2},{4,5},{5,4},{6,7},{7,6},{8,9},{9,8},{10,11... | collective-permute-start | bytes 1572872 | tf_op jit(solution)/shard_map/ppermute | solution.py:352
  103.3 34.4 %collective-permute-start.14 = (bf16[128,2048]{1,0:T(8,128)(2,1)S(1)}, bf16[128,2048]{1,0:T(8,128)(2,1)S(1)}, u32[]{:S(2)}, u32[]{:S(2)}) collective-permute-start(bf16[128,2048]{1,0:T(8,128)(2,1)S(1)} %copy-done.11), channel_id=1, source_target_pairs={{0,16},{16,0},{1,17},{17,1},{2,18},{18,2},{3,19},{19,3},{4,20},{20... | collective-permute-start | bytes 1572872 | tf_op jit(solution)/shard_map/ppermute | solution.py:281
  103.9 21.7 %collective-permute-start.15 = (bf16[256,256]{1,0:T(8,128)(2,1)}, bf16[256,256]{1,0:T(8,128)(2,1)S(1)}, u32[]{:S(2)}, u32[]{:S(2)}) collective-permute-start(bf16[256,256]{1,0:T(8,128)(2,1)} %get-tuple-element.55), channel_id=1, source_target_pairs={{32,0},{64,32},{96,64},{128,96},{160,128},{192,160},{224,192},{33,... | collective-permute-start | bytes 393224 | tf_op jit(solution)/shard_map/ppermute | solution.py:329
  105.8 19.8 %collective-permute-start.16 = (bf16[256,256]{1,0:T(8,128)(2,1)}, bf16[256,256]{1,0:T(8,128)(2,1)S(1)}, u32[]{:S(2)}, u32[]{:S(2)}) collective-permute-start(bf16[256,256]{1,0:T(8,128)(2,1)} %get-tuple-element.56), channel_id=1, source_target_pairs={{64,0},{96,32},{128,64},{160,96},{192,128},{224,160},{65,1},{97,33... | collective-permute-start | bytes 393224 | tf_op jit(solution)/shard_map/ppermute | solution.py:329
  107.1 19.3 %collective-permute-start.17 = (bf16[256,256]{1,0:T(8,128)(2,1)S(1)}, bf16[256,256]{1,0:T(8,128)(2,1)S(1)}, u32[]{:S(2)}, u32[]{:S(2)}) collective-permute-start(bf16[256,256]{1,0:T(8,128)(2,1)S(1)} %copy-done.14), channel_id=1, source_target_pairs={{96,0},{128,32},{160,64},{192,96},{224,128},{97,1},{129,33},{161,6... | collective-permute-start | bytes 393224 | tf_op jit(solution)/shard_map/ppermute | solution.py:329
  108.5 27.5 %collective-permute-start.18 = (bf16[256,256]{1,0:T(8,128)(2,1)S(1)}, bf16[256,256]{1,0:T(8,128)(2,1)S(1)}, u32[]{:S(2)}, u32[]{:S(2)}) collective-permute-start(bf16[256,256]{1,0:T(8,128)(2,1)S(1)} %copy-done.13), channel_id=1, source_target_pairs={{128,0},{160,32},{192,64},{224,96},{129,1},{161,33},{193,65},{225,... | collective-permute-start | bytes 393224 | tf_op jit(solution)/shard_map/ppermute | solution.py:329
  111.8 24.1 %copy-start = (f32[256,256]{1,0:T(8,128)S(1)}, f32[256,256]{1,0:T(8,128)}, u32[]{:S(2)}) copy-start(f32[256,256]{1,0:T(8,128)} %get-tuple-element.54.refs_0_) | copy-start | bytes 786436
  111.8 25.9 %copy-start.3 = (bf16[128,2048]{1,0:T(8,128)(2,1)S(1)}, bf16[128,2048]{1,0:T(8,128)(2,1)}, u32[]{:S(2)}) copy-start(bf16[128,2048]{1,0:T(8,128)(2,1)} %get-tuple-element.41) | copy-start | bytes 1572868
  112.6 30.2 %all-to-all-start.1 = ((bf16[32,20,256]{2,1,0:T(8,128)(2,1)}), bf16[32,20,256]{2,1,0:T(8,128)(2,1)S(1)}, u32[]{:S(2)}, u32[]{:S(2)}) async-start(bf16[32,20,256]{2,1,0:T(8,128)(2,1)} %reshape.146), calls=%async_computation.1 | async-start | bytes 786432 | tf_op jit(solution)/shard_map/all_to_all | solution.py:358
  136.0 4.6 %collective-permute-start.24 = (bf16[128,256]{1,0:T(8,128)(2,1)S(1)}, bf16[128,256]{1,0:T(8,128)(2,1)S(1)}, u32[]{:S(2)}, u32[]{:S(2)}) collective-permute-start(bf16[128,256]{1,0:T(8,128)(2,1)S(1)} %get-tuple-element.66), channel_id=1, source_target_pairs={{0,16},{16,0},{1,17},{17,1},{2,18},{18,2},{3,19},{19,3},{4,20},{20... | collective-permute-start | bytes 196616 | tf_op jit(solution)/shard_map/ppermute | solution.py:281

commit v4 on v3

--- a/solution.py
+++ b/solution.py
@@ -325,7 +325,7 @@
 
     def travel(parts):
         sent = []
-        for d in range(1, BACK + 1):
+        for d in range(BACK, 0, -1):
             sent.append(lax.ppermute(parts[d], "z", [(i, i - d) for i in range(d, nz)]))
         return sent
 
@@ -340,9 +340,7 @@
     dq_own, dq_far, key_parts = run_grads(
         place, q, q_recv, g, g_recv, keys, values, codes, shift
     )
-    value_first, dq_far, key_parts, *value_sent = after(
-        value_parts[0], dq_far, key_parts, *value_sent
-    )
+    value_first, dq_far, *value_sent = after(value_parts[0], dq_far, *value_sent)
     value_low = add_up(value_first, value_sent)
 
     near = [value_low]

time: 144 us -> 144 us (level)
    ppermute x8, waiting for transfers between devices: 14.8 us -> 2.08 us  [travel(): sent.append(lax.ppermute(parts[d], 'z', [(i, i - d) for i in range(d, nz)]))]
    all_to_all x1, waiting for transfers between devices: 1.47 us -> 11.4 us  [body(): lax.all_to_all(part.reshape(32, rows, 256), ('z', 'yl', 'yh'), split_axis...]
    ppermute x6, waiting for transfers between devices: 1.71 us -> 3.29 us  [to_pair(): return lax.ppermute(a, 'yl', swap)]
  transfers between devices with their start and end apart: 27 -> 27, of which waited for: 8 -> 6; matrix products, arithmetic and copies ran while one was open for 7% -> 7% of each run, Pallas kernels for 22% -> 22%
where the time goes in v4:
time: 144 us
  starting transfers between devices  72.4 us (50%)
  Pallas kernels  32.3 us (22%)
  waiting for transfers between devices  23.8 us (17%)
  local copies, waits for them, and re-layouts  9.75 us (7%)
  other arithmetic  4.14 us (3%)
    pallas_call x1, Pallas kernels, run_grads(): pl.pallas_call(grads_kernel, grid_spec=pltpu.PrefetchScalarGridSpec(num_s...  16.7 us
    ppermute x8, starting transfers between devices, travel(): sent.append(lax.ppermute(parts[d], 'z', [(i, i - d) for i in range(d, nz)]))  15.2 us
    all_to_all x1, starting transfers between devices, body(): lax.all_to_all(part.reshape(32, rows, 256), ('z', 'yl', 'yh'), split_axis...  14 us
    pallas_call x1, Pallas kernels, run_probs(): pl.pallas_call(probs_kernel, grid_spec=pltpu.PrefetchScalarGridSpec(num_s...  13.5 us
    all_to_all x1, waiting for transfers between devices, body(): lax.all_to_all(part.reshape(32, rows, 256), ('z', 'yl', 'yh'), split_axis...  11.4 us
    ppermute x3, waiting for transfers between devices, body(): lax.ppermute(value_low, 'x', [(i, (i + d) % 4) for i in range(4)])  7.02 us
    ppermute x6, starting transfers between devices, to_pair(): return lax.ppermute(a, 'yl', swap)  6.88 us
    ppermute x1, starting transfers between devices, body(): both = lax.ppermute(both, 'z', [(i, i + 2) for i in range(nz - 2)])  6.17 us
  transfers between devices with their start and end apart: 27, of which 6 were waited for; matrix products, arithmetic and copies ran while one was open for 7% of the time, Pallas kernels for 22%

profile of v4, /device:TPU:32, one launch (start us, length us, event | category | flops | bytes accessed | tf_op | source)
XLA Modules:
  0.0 143.6 jit_solution(13481448853612571977)
XLA Ops:
  0.6 1.1 dynamic-slice_bitcast_fusion
  1.7 0.7 pad_maximum_fusion.3
  2.4 1.6 %collective-permute-start.2 = (bf16[128,512]{1,0:T(8,128)(2,1)}, bf16[128,512]{1,0:T(8,128)(2,1)}, u32[]{:S(2)}, u32[]{:S(2)}) collective-permute-start(bf16[128,512]{1,0:T(8,128)(2,1)} %pad_maximum_fusion.3), channel_id=1, source_target_pairs={{0,16},{16,0},{1,17},{17,1},{2,18},{18,2},{3,19},{19,3},{4,20},{20... | collective-permute-start | bytes 393224 | tf_op jit(solution)/shard_map/ppermute | solution.py:281
  4.0 1.9 %constant_dynamic-slice_fusion = bf16[128,2048]{1,0:T(8,128)(2,1)} fusion(bf16[128,4096]{1,0:T(8,128)(2,1)} %bitcast.48, s32[]{:T(128)S(6)} %select_n.55), kind=kLoop, calls=%fused_computation.20 | loop fusion | bytes 1048580 | tf_op jit(solution)/shard_map/dynamic_slice | solution.py:278
  5.8 0.4 collective-permute-start.1
  6.3 1.1 constant_dynamic-slice_fusion.1
  7.4 1.7 %collective-permute-start = (bf16[128,2048]{1,0:T(8,128)(2,1)S(1)}, bf16[128,2048]{1,0:T(8,128)(2,1)}, u32[]{:S(2)}, u32[]{:S(2)}) collective-permute-start(bf16[128,2048]{1,0:T(8,128)(2,1)S(1)} %constant_dynamic-slice_fusion.1), channel_id=1, source_target_pairs={{0,16},{16,0},{1,17},{17,1},{2,18},{18,2},{3,19},{19,3},{4,20},{20... | collective-permute-start | bytes 1572872 | tf_op jit(solution)/shard_map/ppermute | solution.py:281
  9.0 0.8 copy.14
  9.8 0.3 reshape.142
  10.1 0.2 copy.15
  10.3 1.3 copy.16
  11.6 4.4 %all-to-all-start = ((bf16[8,640,128]{2,1,0:T(8,128)(2,1)}), bf16[8,640,128]{2,1,0:T(8,128)(2,1)S(1)}, u32[]{:S(2)}, u32[]{:S(2)}) async-start(bf16[8,640,128]{2,1,0:T(8,128)(2,1)} %copy.16), calls=%async_computation | async-start | bytes 2621440 | tf_op jit(solution)/shard_map/all_to_all | solution.py:315
  16.1 0.9 fusion
  17.0 0.0 copy-start.5
  17.0 3.8 %collective-permute-start.3 = (bf16[256,256]{1,0:T(8,128)(2,1)S(1)}, bf16[256,256]{1,0:T(8,128)(2,1)S(1)}, u32[]{:S(2)}, u32[]{:S(2)}) collective-permute-start(bf16[256,256]{1,0:T(8,128)(2,1)S(1)} %pad_maximum_fusion.4.k0), channel_id=1, source_target_pairs={{0,32},{32,64},{64,96},{96,128},{128,160},{160,192},{192,224},{1,3... | collective-permute-start | bytes 393224 | tf_op jit(solution)/shard_map/ppermute | solution.py:290
  20.8 0.1 pad_dynamic-slice_fusion
  20.9 4.8 %collective-permute-start.5 = (bf16[256,256]{1,0:T(8,128)(2,1)S(1)}, bf16[256,256]{1,0:T(8,128)(2,1)}, u32[]{:S(2)}, u32[]{:S(2)}) collective-permute-start(bf16[256,256]{1,0:T(8,128)(2,1)S(1)} %pad_maximum_fusion.4.k0), channel_id=1, source_target_pairs={{0,192},{32,224},{64,0},{96,32},{1,193},{33,225},{65,1},{97,33},{2... | collective-permute-start | bytes 393224 | tf_op jit(solution)/shard_map/ppermute | solution.py:292
  25.8 1.9 %collective-permute-start.7 = (bf16[256,256]{1,0:T(8,128)(2,1)S(1)}, bf16[256,256]{1,0:T(8,128)(2,1)S(1)}, u32[]{:S(2)}, u32[]{:S(2)}) collective-permute-start(bf16[256,256]{1,0:T(8,128)(2,1)S(1)} %pad_maximum_fusion.5.v0), channel_id=1, source_target_pairs={{0,32},{32,64},{64,96},{96,128},{128,160},{160,192},{192,224},{1,3... | collective-permute-start | bytes 393224 | tf_op jit(solution)/shard_map/ppermute | solution.py:304
  27.7 0.0 collective-permute-done.3.k1
  27.7 3.9 %collective-permute-start.4 = (bf16[512,256]{1,0:T(8,128)(2,1)S(1)}, bf16[512,256]{1,0:T(8,128)(2,1)S(1)}, u32[]{:S(2)}, u32[]{:S(2)}) collective-permute-start(bf16[512,256]{1,0:T(8,128)(2,1)S(1)} %pad_maximum_fusion.1), channel_id=1, source_target_pairs={{0,64},{32,96},{64,128},{96,160},{128,192},{160,224},{1,65},{33,97... | collective-permute-start | bytes 786440 | tf_op jit(solution)/shard_map/ppermute | solution.py:296
  31.7 0.0 copy-start.10
  31.7 0.0 collective-permute-done.5
  31.7 4.6 %collective-permute-start.6 = (bf16[256,256]{1,0:T(8,128)(2,1)}, bf16[256,256]{1,0:T(8,128)(2,1)S(1)}, u32[]{:S(2)}, u32[]{:S(2)}) collective-permute-start(bf16[256,256]{1,0:T(8,128)(2,1)} %collective-permute-done.5), channel_id=1, source_target_pairs={{192,128},{224,160},{0,192},{32,224},{193,129},{225,161},{1,193},{... | collective-permute-start | bytes 393224 | tf_op jit(solution)/shard_map/ppermute | solution.py:298
  36.4 0.7 pad_add_fusion.s_ref
  37.0 0.6 slice.30
  37.6 2.0 %collective-permute-start.9 = (bf16[256,256]{1,0:T(8,128)(2,1)S(1)}, bf16[256,256]{1,0:T(8,128)(2,1)}, u32[]{:S(2)}, u32[]{:S(2)}) collective-permute-start(bf16[256,256]{1,0:T(8,128)(2,1)S(1)} %pad_maximum_fusion.5.v0), channel_id=1, source_target_pairs={{0,128},{32,160},{64,192},{96,224},{1,129},{33,161},{65,193},{97,2... | collective-permute-start | bytes 393224 | tf_op jit(solution)/shard_map/ppermute | solution.py:305
  39.6 0.0 collective-permute-done.1.gr
  39.6 6.2 %collective-permute-start.8 = (bf16[512,256]{1,0:T(8,128)(2,1)S(1)}, bf16[512,256]{1,0:T(8,128)(2,1)}, u32[]{:S(2)}, u32[]{:S(2)}) collective-permute-start(bf16[512,256]{1,0:T(8,128)(2,1)S(1)} %pad_maximum_fusion.2), channel_id=1, source_target_pairs={{0,64},{32,96},{64,128},{96,160},{128,192},{160,224},{1,65},{33,97... | collective-permute-start | bytes 786440 | tf_op jit(solution)/shard_map/ppermute | solution.py:307
  45.9 0.6 copy-done.15
  46.5 0.1 copy-done.12
  46.6 13.5 %probs.1 = (f32[2,8,2048]{2,1,0:T(8,128)}, f32[256,256]{1,0:T(8,128)}, bf16[256,256]{1,0:T(8,128)(2,1)}, bf16[256,256]{1,0:T(8,128)(2,1)}, bf16[256,256]{1,0:T(8,128)(2,1)}, /*index=5*/bf16[256,256]{1,0:T(8,128)(2,1)}) custom-call(s32[4]{0:T(128)} %pad_add_fusion.s_ref, bf16[128,4096]{1,0:T(8,128)(2,1)} %bitcast.46, ...), custom_call_target="tpu_custom_call" | custom-call | flops 4026531840 | bytes 16777216 | tf_op jit(solution)/shard_map/probs/pallas_call | solution.py:165
  60.1 1.3 collective-permute-start.10
  61.4 1.3 collective-permute-start.11
  62.7 1.3 collective-permute-start.12
  64.0 5.6 %collective-permute-start.13 = (bf16[256,256]{1,0:T(8,128)(2,1)}, bf16[256,256]{1,0:T(8,128)(2,1)S(1)}, u32[]{:S(2)}, u32[]{:S(2)}) collective-permute-start(bf16[256,256]{1,0:T(8,128)(2,1)} %get-tuple-element.42), channel_id=1, source_target_pairs={{32,0},{64,32},{96,64},{128,96},{160,128},{192,160},{224,192},{33,... | collective-permute-start | bytes 393224 | tf_op jit(solution)/shard_map/ppermute | solution.py:329
  69.6 0.8 collective-permute-start.19
  70.3 16.7 %grads.1 = (bf16[128,2048]{1,0:T(8,128)(2,1)}, bf16[128,2048]{1,0:T(8,128)(2,1)}, f32[256,256]{1,0:T(8,128)}, bf16[256,256]{1,0:T(8,128)(2,1)}, bf16[256,256]{1,...) custom-call(s32[4]{0:T(128)} %pad_add_fusion.s_ref, bf16[128,4096]{1,0:T(8,128)(2,1)} %bitcast.47, ...), custom_call_target="tpu_custom_call" | custom-call | flops 6710886400 | bytes 16777216 | tf_op jit(solution)/shard_map/grads/pallas_call | solution.py:189
  87.1 0.1 add_convert_fusion
  87.2 2.8 %collective-permute-start.22 = (bf16[256,256]{1,0:T(8,128)(2,1)S(1)}, bf16[256,256]{1,0:T(8,128)(2,1)S(1)}, u32[]{:S(2)}, u32[]{:S(2)}) collective-permute-start(bf16[256,256]{1,0:T(8,128)(2,1)S(1)} %add_convert_fusion), channel_id=1, source_target_pairs={{0,6},{2,0},{4,2},{6,4},{1,7},{3,1},{5,3},{7,5},{8,14},{10,8},{12,... | collective-permute-start | bytes 393224 | tf_op jit(solution)/shard_map/ppermute | solution.py:348
  90.0 0.9 collective-permute-start.21
  90.9 0.9 collective-permute-start.20
  91.7 3.4 %collective-permute-done.22 = bf16[256,256]{1,0:T(8,128)(2,1)S(1)} collective-permute-done((bf16[256,256]{1,0:T(8,128)(2,1)S(1)}, bf16[256,256]{1,0:T(8,128)(2,1)S(1)}, u32[]{:S(2)}, u32[]{:S(2)}) %collective-permute-start.22) | collective-permute-done | bytes 131104 | tf_op jit(solution)/shard_map/ppermute | solution.py:348
  95.1 2.3 %collective-permute-done.21 = bf16[256,256]{1,0:T(8,128)(2,1)S(1)} collective-permute-done((bf16[256,256]{1,0:T(8,128)(2,1)S(1)}, bf16[256,256]{1,0:T(8,128)(2,1)S(1)}, u32[]{:S(2)}, u32[]{:S(2)}) %collective-permute-start.21) | collective-permute-done | bytes 131104 | tf_op jit(solution)/shard_map/ppermute | solution.py:348
  97.4 1.3 collective-permute-done.20
  98.8 0.1 pad_maximum_fusion.mine
  98.8 0.1 collective-permute-start.23
  98.9 1.6 %collective-permute-start.14 = (bf16[128,2048]{1,0:T(8,128)(2,1)S(1)}, bf16[128,2048]{1,0:T(8,128)(2,1)S(1)}, u32[]{:S(2)}, u32[]{:S(2)}) collective-permute-start(bf16[128,2048]{1,0:T(8,128)(2,1)S(1)} %copy-done.11), channel_id=1, source_target_pairs={{0,16},{16,0},{1,17},{17,1},{2,18},{18,2},{3,19},{19,3},{4,20},{20... | collective-permute-start | bytes 1572872 | tf_op jit(solution)/shard_map/ppermute | solution.py:281
  100.6 1.3 collective-permute-start.15
  101.9 1.3 collective-permute-start.16
  103.2 1.3 collective-permute-start.17
  104.5 1.9 %collective-permute-start.18 = (bf16[256,256]{1,0:T(8,128)(2,1)S(1)}, bf16[256,256]{1,0:T(8,128)(2,1)S(1)}, u32[]{:S(2)}, u32[]{:S(2)}) collective-permute-start(bf16[256,256]{1,0:T(8,128)(2,1)S(1)} %copy-done.13), channel_id=1, source_target_pairs={{32,0},{64,32},{96,64},{128,96},{160,128},{192,160},{224,192},{33,... | collective-permute-start | bytes 393224 | tf_op jit(solution)/shard_map/ppermute | solution.py:329
  106.5 2.0 %weight.1.refs_5_ = bf16[640,256]{1,0:T(8,128)(2,1)S(1)} custom-call(s32[4]{0:T(128)S(1)} %copy-done.1, bf16[8,640,128]{2,1,0:T(8,128)(2,1)S(1)} %all-to-all-done, bf16[8,640,128]{2,1,0:T(8,128)(2,1)S(1)} %collective-permute-done.19.xr, bf16[4,256,256]{2,1,0:T(8,128)(2,1)S(1)} %pad_maximum_fusion.mine, bf16[4,256,256]{2,1,0:T(8,128)(2,1)S(1)} %collective-permute-done.23.theirs), custom_call_target="tpu_custom_call" | custom-call | flops 671088640 | bytes 4194304 | tf_op jit(solution)/shard_map/weight/pallas_call | solution.py:233
  108.5 0.0 copy-start.3
  108.5 0.8 reshape.146
  109.3 14.0 %all-to-all-start.1 = ((bf16[32,20,256]{2,1,0:T(8,128)(2,1)}), bf16[32,20,256]{2,1,0:T(8,128)(2,1)S(1)}, u32[]{:S(2)}, u32[]{:S(2)}) async-start(bf16[32,20,256]{2,1,0:T(8,128)(2,1)} %reshape.146), calls=%async_computation.1 | async-start | bytes 786432 | tf_op jit(solution)/shard_map/all_to_all | solution.py:356
  123.3 2.1 %collective-permute-done.18.refs_4_ = bf16[256,256]{1,0:T(8,128)(2,1)S(1)} collective-permute-done((bf16[256,256]{1,0:T(8,128)(2,1)S(1)}, bf16[256,256]{1,0:T(8,128)(2,1)S(1)}, u32[]{:S(2)}, u32[]{:S(2)}) %collective-permute-start.18) | collective-permute-done | bytes 131104 | tf_op jit(solution)/shard_map/ppermute | solution.py:329
  125.4 0.1 key_sum.1
  125.5 0.8 collective-permute-start.24
  126.3 1.2 maximum_select_fusion
  127.5 3.3 %collective-permute-done.24 = bf16[128,256]{1,0:T(8,128)(2,1)S(1)} collective-permute-done((bf16[128,256]{1,0:T(8,128)(2,1)S(1)}, bf16[128,256]{1,0:T(8,128)(2,1)S(1)}, u32[]{:S(2)}, u32[]{:S(2)}) %collective-permute-start.24) | collective-permute-done | bytes 65568 | tf_op jit(solution)/shard_map/ppermute | solution.py:281
  130.8 0.7 maximum_select_fusion.1
  131.5 11.4 %all-to-all-done.1 = bf16[32,20,256]{2,1,0:T(8,128)(2,1)S(1)} async-done(((bf16[32,20,256]{2,1,0:T(8,128)(2,1)}), bf16[32,20,256]{2,1,0:T(8,128)(2,1)S(1)}, u32[]{:S(2)}, u32[]{:S(2)}) %all-to-all-start.1) | async-done | bytes 327712 | tf_op jit(solution)/shard_map/all_to_all | solution.py:356
  142.9 0.1 convert_reduce_fusion
  142.9 0.6 maximum_multiply_fusion
  (54 shorter events, 0.2 us)
Async XLA Ops:
  0.6 8.4 %copy-start.2 = (bf16[1,128,5120]{2,1,0:T(8,128)(2,1)S(1)}, bf16[1,128,5120]{2,1,0:T(8,128)(2,1)}, u32[]{:S(2)}) copy-start(bf16[1,128,5120]{2,1,0:T(8,128)(2,1)} %param.10) | copy-start | bytes 3932164
  2.4 13.7 %collective-permute-start.2 = (bf16[128,512]{1,0:T(8,128)(2,1)}, bf16[128,512]{1,0:T(8,128)(2,1)}, u32[]{:S(2)}, u32[]{:S(2)}) collective-permute-start(bf16[128,512]{1,0:T(8,128)(2,1)} %pad_maximum_fusion.3), channel_id=1, source_target_pairs={{0,16},{16,0},{1,17},{17,1},{2,18},{18,2},{3,19},{19,3},{4,20},{20... | collective-permute-start | bytes 393224 | tf_op jit(solution)/shard_map/ppermute | solution.py:281
  5.8 33.8 %collective-permute-start.1 = (bf16[128,2048]{1,0:T(8,128)(2,1)}, bf16[128,2048]{1,0:T(8,128)(2,1)}, u32[]{:S(2)}, u32[]{:S(2)}) collective-permute-start(bf16[128,2048]{1,0:T(8,128)(2,1)} %constant_dynamic-slice_fusion), channel_id=1, source_target_pairs={{0,16},{16,0},{1,17},{17,1},{2,18},{18,2},{3,19},{19,3},{4,20},{20... | collective-permute-start | bytes 1572872 | tf_op jit(solution)/shard_map/ppermute | solution.py:281
  7.4 38.5 %collective-permute-start = (bf16[128,2048]{1,0:T(8,128)(2,1)S(1)}, bf16[128,2048]{1,0:T(8,128)(2,1)}, u32[]{:S(2)}, u32[]{:S(2)}) collective-permute-start(bf16[128,2048]{1,0:T(8,128)(2,1)S(1)} %constant_dynamic-slice_fusion.1), channel_id=1, source_target_pairs={{0,16},{16,0},{1,17},{17,1},{2,18},{18,2},{3,19},{19,3},{4,20},{20... | collective-permute-start | bytes 1572872 | tf_op jit(solution)/shard_map/ppermute | solution.py:281
  11.6 9.2 %copy-start.9 = (s32[1,2048]{1,0:T(1,128)S(1)}, s32[1,2048]{1,0:T(1,128)}, u32[]{:S(2)}) copy-start(s32[1,2048]{1,0:T(1,128)} %param.11) | copy-start | bytes 24580
  11.6 34.2 %all-to-all-start = ((bf16[8,640,128]{2,1,0:T(8,128)(2,1)}), bf16[8,640,128]{2,1,0:T(8,128)(2,1)S(1)}, u32[]{:S(2)}, u32[]{:S(2)}) async-start(bf16[8,640,128]{2,1,0:T(8,128)(2,1)} %copy.16), calls=%async_computation | async-start | bytes 2621440 | tf_op jit(solution)/shard_map/all_to_all | solution.py:315
  17.0 28.9 %copy-start.5 = (bf16[256,256]{1,0:T(8,128)(2,1)}, bf16[256,256]{1,0:T(8,128)(2,1)S(1)}, u32[]{:S(2)}) copy-start(bf16[256,256]{1,0:T(8,128)(2,1)S(1)} %pad_maximum_fusion.4.k0) | copy-start | bytes 393220
  17.0 10.7 %collective-permute-start.3 = (bf16[256,256]{1,0:T(8,128)(2,1)S(1)}, bf16[256,256]{1,0:T(8,128)(2,1)S(1)}, u32[]{:S(2)}, u32[]{:S(2)}) collective-permute-start(bf16[256,256]{1,0:T(8,128)(2,1)S(1)} %pad_maximum_fusion.4.k0), channel_id=1, source_target_pairs={{0,32},{32,64},{64,96},{96,128},{128,160},{160,192},{192,224},{1,3... | collective-permute-start | bytes 393224 | tf_op jit(solution)/shard_map/ppermute | solution.py:290
  20.9 10.8 %collective-permute-start.5 = (bf16[256,256]{1,0:T(8,128)(2,1)S(1)}, bf16[256,256]{1,0:T(8,128)(2,1)}, u32[]{:S(2)}, u32[]{:S(2)}) collective-permute-start(bf16[256,256]{1,0:T(8,128)(2,1)S(1)} %pad_maximum_fusion.4.k0), channel_id=1, source_target_pairs={{0,192},{32,224},{64,0},{96,32},{1,193},{33,225},{65,1},{97,33},{2... | collective-permute-start | bytes 393224 | tf_op jit(solution)/shard_map/ppermute | solution.py:292
  25.7 34.3 %copy-start.6 = (bf16[256,256]{1,0:T(8,128)(2,1)}, bf16[256,256]{1,0:T(8,128)(2,1)S(1)}, u32[]{:S(2)}) copy-start(bf16[256,256]{1,0:T(8,128)(2,1)S(1)} %pad_maximum_fusion.5.v0) | copy-start | bytes 393220
  25.8 11.9 %collective-permute-start.7 = (bf16[256,256]{1,0:T(8,128)(2,1)S(1)}, bf16[256,256]{1,0:T(8,128)(2,1)S(1)}, u32[]{:S(2)}, u32[]{:S(2)}) collective-permute-start(bf16[256,256]{1,0:T(8,128)(2,1)S(1)} %pad_maximum_fusion.5.v0), channel_id=1, source_target_pairs={{0,32},{32,64},{64,96},{96,128},{128,160},{160,192},{192,224},{1,3... | collective-permute-start | bytes 393224 | tf_op jit(solution)/shard_map/ppermute | solution.py:304
  27.7 18.2 %copy-start.7 = (bf16[256,256]{1,0:T(8,128)(2,1)}, bf16[256,256]{1,0:T(8,128)(2,1)S(1)}, u32[]{:S(2)}) copy-start(bf16[256,256]{1,0:T(8,128)(2,1)S(1)} %collective-permute-done.3.k1) | copy-start | bytes 393220
  27.7 18.1 %collective-permute-start.4 = (bf16[512,256]{1,0:T(8,128)(2,1)S(1)}, bf16[512,256]{1,0:T(8,128)(2,1)S(1)}, u32[]{:S(2)}, u32[]{:S(2)}) collective-permute-start(bf16[512,256]{1,0:T(8,128)(2,1)S(1)} %pad_maximum_fusion.1), channel_id=1, source_target_pairs={{0,64},{32,96},{64,128},{96,160},{128,192},{160,224},{1,65},{33,97... | collective-permute-start | bytes 786440 | tf_op jit(solution)/shard_map/ppermute | solution.py:296
  31.7 14.2 %copy-start.10 = (s32[5,2,128]{2,1,0:T(2,128)}, s32[5,2,128]{2,1,0:T(2,128)S(1)}, u32[]{:S(2)}) copy-start(s32[5,2,128]{2,1,0:T(2,128)S(1)} %reverse_select_fusion) | copy-start | bytes 15364
  31.7 14.1 %collective-permute-start.6 = (bf16[256,256]{1,0:T(8,128)(2,1)}, bf16[256,256]{1,0:T(8,128)(2,1)S(1)}, u32[]{:S(2)}, u32[]{:S(2)}) collective-permute-start(bf16[256,256]{1,0:T(8,128)(2,1)} %collective-permute-done.5), channel_id=1, source_target_pairs={{192,128},{224,160},{0,192},{32,224},{193,129},{225,161},{1,193},{... | collective-permute-start | bytes 393224 | tf_op jit(solution)/shard_map/ppermute | solution.py:298
  37.6 22.5 %copy-start.8 = (bf16[256,256]{1,0:T(8,128)(2,1)}, bf16[256,256]{1,0:T(8,128)(2,1)S(1)}, u32[]{:S(2)}) copy-start(bf16[256,256]{1,0:T(8,128)(2,1)S(1)} %collective-permute-done.7.v1) | copy-start | bytes 393220
  37.6 26.4 %collective-permute-start.9 = (bf16[256,256]{1,0:T(8,128)(2,1)S(1)}, bf16[256,256]{1,0:T(8,128)(2,1)}, u32[]{:S(2)}, u32[]{:S(2)}) collective-permute-start(bf16[256,256]{1,0:T(8,128)(2,1)S(1)} %pad_maximum_fusion.5.v0), channel_id=1, source_target_pairs={{0,128},{32,160},{64,192},{96,224},{1,129},{33,161},{65,193},{97,2... | collective-permute-start | bytes 393224 | tf_op jit(solution)/shard_map/ppermute | solution.py:305
  39.6 29.9 %collective-permute-start.8 = (bf16[512,256]{1,0:T(8,128)(2,1)S(1)}, bf16[512,256]{1,0:T(8,128)(2,1)}, u32[]{:S(2)}, u32[]{:S(2)}) collective-permute-start(bf16[512,256]{1,0:T(8,128)(2,1)S(1)} %pad_maximum_fusion.2), channel_id=1, source_target_pairs={{0,64},{32,96},{64,128},{96,160},{128,192},{160,224},{1,65},{33,97... | collective-permute-start | bytes 786440 | tf_op jit(solution)/shard_map/ppermute | solution.py:307
  45.8 0.7 copy-start.15
  45.8 0.7 copy-start.12
  60.1 27.0 %collective-permute-start.10 = (bf16[256,256]{1,0:T(8,128)(2,1)}, bf16[256,256]{1,0:T(8,128)(2,1)S(1)}, u32[]{:S(2)}, u32[]{:S(2)}) collective-permute-start(bf16[256,256]{1,0:T(8,128)(2,1)} %get-tuple-element.39), channel_id=1, source_target_pairs={{128,0},{160,32},{192,64},{224,96},{129,1},{161,33},{193,65},{225,... | collective-permute-start | bytes 393224 | tf_op jit(solution)/shard_map/ppermute | solution.py:329
  61.4 25.7 %collective-permute-start.11 = (bf16[256,256]{1,0:T(8,128)(2,1)}, bf16[256,256]{1,0:T(8,128)(2,1)S(1)}, u32[]{:S(2)}, u32[]{:S(2)}) collective-permute-start(bf16[256,256]{1,0:T(8,128)(2,1)} %get-tuple-element.40), channel_id=1, source_target_pairs={{96,0},{128,32},{160,64},{192,96},{224,128},{97,1},{129,33},{161,6... | collective-permute-start | bytes 393224 | tf_op jit(solution)/shard_map/ppermute | solution.py:329
  62.7 24.4 %collective-permute-start.12 = (bf16[256,256]{1,0:T(8,128)(2,1)}, bf16[256,256]{1,0:T(8,128)(2,1)S(1)}, u32[]{:S(2)}, u32[]{:S(2)}) collective-permute-start(bf16[256,256]{1,0:T(8,128)(2,1)} %get-tuple-element.41), channel_id=1, source_target_pairs={{64,0},{96,32},{128,64},{160,96},{192,128},{224,160},{65,1},{97,33... | collective-permute-start | bytes 393224 | tf_op jit(solution)/shard_map/ppermute | solution.py:329
  64.0 23.1 %collective-permute-start.13 = (bf16[256,256]{1,0:T(8,128)(2,1)}, bf16[256,256]{1,0:T(8,128)(2,1)S(1)}, u32[]{:S(2)}, u32[]{:S(2)}) collective-permute-start(bf16[256,256]{1,0:T(8,128)(2,1)} %get-tuple-element.42), channel_id=1, source_target_pairs={{32,0},{64,32},{96,64},{128,96},{160,128},{192,160},{224,192},{33,... | collective-permute-start | bytes 393224 | tf_op jit(solution)/shard_map/ppermute | solution.py:329
  69.6 34.9 %collective-permute-start.19 = (bf16[8,640,128]{2,1,0:T(8,128)(2,1)S(1)}, bf16[8,640,128]{2,1,0:T(8,128)(2,1)S(1)}, u32[]{:S(2)}, u32[]{:S(2)}) collective-permute-start(bf16[8,640,128]{2,1,0:T(8,128)(2,1)S(1)} %all-to-all-done), channel_id=1, source_target_pairs={{0,16},{16,0},{1,17},{17,1},{2,18},{18,2},{3,19},{19,3},{4,20},{20... | collective-permute-start | bytes 3932168 | tf_op jit(solution)/shard_map/ppermute | solution.py:281
  70.3 16.8 %copy-start.4 = (f32[256,256]{1,0:T(8,128)S(1)}, f32[256,256]{1,0:T(8,128)}, u32[]{:S(2)}) copy-start(f32[256,256]{1,0:T(8,128)} %get-tuple-element.50) | copy-start | bytes 786436
  87.0 11.9 %copy-start.11 = (bf16[128,2048]{1,0:T(8,128)(2,1)S(1)}, bf16[128,2048]{1,0:T(8,128)(2,1)}, u32[]{:S(2)}) copy-start(bf16[128,2048]{1,0:T(8,128)(2,1)} %get-tuple-element.43) | copy-start | bytes 1572868
  87.0 16.2 %copy-start.14 = (bf16[256,256]{1,0:T(8,128)(2,1)S(1)}, bf16[256,256]{1,0:T(8,128)(2,1)}, u32[]{:S(2)}) copy-start(bf16[256,256]{1,0:T(8,128)(2,1)} %get-tuple-element.47) | copy-start | bytes 393220
  87.0 17.5 %copy-start.13 = (bf16[256,256]{1,0:T(8,128)(2,1)S(1)}, bf16[256,256]{1,0:T(8,128)(2,1)}, u32[]{:S(2)}) copy-start(bf16[256,256]{1,0:T(8,128)(2,1)} %get-tuple-element.48) | copy-start | bytes 393220
  87.0 19.4 %copy-start.1 = (s32[4]{0:T(128)S(1)}, s32[4]{0:T(128)}, u32[]{:S(2)}) copy-start(s32[4]{0:T(128)} %pad_add_fusion.s_ref) | copy-start | bytes 52
  87.2 7.9 %collective-permute-start.22 = (bf16[256,256]{1,0:T(8,128)(2,1)S(1)}, bf16[256,256]{1,0:T(8,128)(2,1)S(1)}, u32[]{:S(2)}, u32[]{:S(2)}) collective-permute-start(bf16[256,256]{1,0:T(8,128)(2,1)S(1)} %add_convert_fusion), channel_id=1, source_target_pairs={{0,6},{2,0},{4,2},{6,4},{1,7},{3,1},{5,3},{7,5},{8,14},{10,8},{12,... | collective-permute-start | bytes 393224 | tf_op jit(solution)/shard_map/ppermute | solution.py:348
  90.0 7.4 %collective-permute-start.21 = (bf16[256,256]{1,0:T(8,128)(2,1)S(1)}, bf16[256,256]{1,0:T(8,128)(2,1)S(1)}, u32[]{:S(2)}, u32[]{:S(2)}) collective-permute-start(bf16[256,256]{1,0:T(8,128)(2,1)S(1)} %add_convert_fusion), channel_id=1, source_target_pairs={{0,4},{2,6},{4,0},{6,2},{1,5},{3,7},{5,1},{7,3},{8,12},{10,14},{12... | collective-permute-start | bytes 393224 | tf_op jit(solution)/shard_map/ppermute | solution.py:348
  90.9 7.9 %collective-permute-start.20 = (bf16[256,256]{1,0:T(8,128)(2,1)S(1)}, bf16[256,256]{1,0:T(8,128)(2,1)S(1)}, u32[]{:S(2)}, u32[]{:S(2)}) collective-permute-start(bf16[256,256]{1,0:T(8,128)(2,1)S(1)} %add_convert_fusion), channel_id=1, source_target_pairs={{0,2},{2,4},{4,6},{6,0},{1,3},{3,5},{5,7},{7,1},{8,10},{10,12},{12... | collective-permute-start | bytes 393224 | tf_op jit(solution)/shard_map/ppermute | solution.py:348
  98.8 4.3 %collective-permute-start.23 = (bf16[4,256,256]{2,1,0:T(8,128)(2,1)S(1)}, bf16[4,256,256]{2,1,0:T(8,128)(2,1)S(1)}, u32[]{:S(2)}, u32[]{:S(2)}) collective-permute-start(bf16[4,256,256]{2,1,0:T(8,128)(2,1)S(1)} %pad_maximum_fusion.mine), channel_id=1, source_target_pairs={{0,1},{1,0},{2,3},{3,2},{4,5},{5,4},{6,7},{7,6},{8,9},{9,8},{10,11... | collective-permute-start | bytes 1572872 | tf_op jit(solution)/shard_map/ppermute | solution.py:350
  98.9 27.3 %collective-permute-start.14 = (bf16[128,2048]{1,0:T(8,128)(2,1)S(1)}, bf16[128,2048]{1,0:T(8,128)(2,1)S(1)}, u32[]{:S(2)}, u32[]{:S(2)}) collective-permute-start(bf16[128,2048]{1,0:T(8,128)(2,1)S(1)} %copy-done.11), channel_id=1, source_target_pairs={{0,16},{16,0},{1,17},{17,1},{2,18},{18,2},{3,19},{19,3},{4,20},{20... | collective-permute-start | bytes 1572872 | tf_op jit(solution)/shard_map/ppermute | solution.py:281
  100.6 22.7 %collective-permute-start.15 = (bf16[256,256]{1,0:T(8,128)(2,1)}, bf16[256,256]{1,0:T(8,128)(2,1)S(1)}, u32[]{:S(2)}, u32[]{:S(2)}) collective-permute-start(bf16[256,256]{1,0:T(8,128)(2,1)} %get-tuple-element.45), channel_id=1, source_target_pairs={{128,0},{160,32},{192,64},{224,96},{129,1},{161,33},{193,65},{225,... | collective-permute-start | bytes 393224 | tf_op jit(solution)/shard_map/ppermute | solution.py:329
  101.9 21.4 %collective-permute-start.16 = (bf16[256,256]{1,0:T(8,128)(2,1)}, bf16[256,256]{1,0:T(8,128)(2,1)S(1)}, u32[]{:S(2)}, u32[]{:S(2)}) collective-permute-start(bf16[256,256]{1,0:T(8,128)(2,1)} %get-tuple-element.46), channel_id=1, source_target_pairs={{96,0},{128,32},{160,64},{192,96},{224,128},{97,1},{129,33},{161,6... | collective-permute-start | bytes 393224 | tf_op jit(solution)/shard_map/ppermute | solution.py:329
  103.2 20.1 %collective-permute-start.17 = (bf16[256,256]{1,0:T(8,128)(2,1)S(1)}, bf16[256,256]{1,0:T(8,128)(2,1)S(1)}, u32[]{:S(2)}, u32[]{:S(2)}) collective-permute-start(bf16[256,256]{1,0:T(8,128)(2,1)S(1)} %copy-done.14), channel_id=1, source_target_pairs={{64,0},{96,32},{128,64},{160,96},{192,128},{224,160},{65,1},{97,33... | collective-permute-start | bytes 393224 | tf_op jit(solution)/shard_map/ppermute | solution.py:329
  104.5 20.9 %collective-permute-start.18 = (bf16[256,256]{1,0:T(8,128)(2,1)S(1)}, bf16[256,256]{1,0:T(8,128)(2,1)S(1)}, u32[]{:S(2)}, u32[]{:S(2)}) collective-permute-start(bf16[256,256]{1,0:T(8,128)(2,1)S(1)} %copy-done.13), channel_id=1, source_target_pairs={{32,0},{64,32},{96,64},{128,96},{160,128},{192,160},{224,192},{33,... | collective-permute-start | bytes 393224 | tf_op jit(solution)/shard_map/ppermute | solution.py:329
  108.5 16.9 %copy-start = (f32[256,256]{1,0:T(8,128)S(1)}, f32[256,256]{1,0:T(8,128)}, u32[]{:S(2)}) copy-start(f32[256,256]{1,0:T(8,128)} %get-tuple-element.44.refs_0_) | copy-start | bytes 786436
  108.5 17.8 %copy-start.3 = (bf16[128,2048]{1,0:T(8,128)(2,1)S(1)}, bf16[128,2048]{1,0:T(8,128)(2,1)}, u32[]{:S(2)}) copy-start(bf16[128,2048]{1,0:T(8,128)(2,1)} %get-tuple-element.36) | copy-start | bytes 1572868
  109.3 33.5 %all-to-all-start.1 = ((bf16[32,20,256]{2,1,0:T(8,128)(2,1)}), bf16[32,20,256]{2,1,0:T(8,128)(2,1)S(1)}, u32[]{:S(2)}, u32[]{:S(2)}) async-start(bf16[32,20,256]{2,1,0:T(8,128)(2,1)} %reshape.146), calls=%async_computation.1 | async-start | bytes 786432 | tf_op jit(solution)/shard_map/all_to_all | solution.py:356
  125.5 5.3 %collective-permute-start.24 = (bf16[128,256]{1,0:T(8,128)(2,1)S(1)}, bf16[128,256]{1,0:T(8,128)(2,1)S(1)}, u32[]{:S(2)}, u32[]{:S(2)}) collective-permute-start(bf16[128,256]{1,0:T(8,128)(2,1)S(1)} %get-tuple-element.56), channel_id=1, source_target_pairs={{0,16},{16,0},{1,17},{17,1},{2,18},{18,2},{3,19},{19,3},{4,20},{20... | collective-permute-start | bytes 196616 | tf_op jit(solution)/shard_map/ppermute | solution.py:281
